TPU v7x, 32 devices: a whole 2x2x4 slice. The times are simulated.
32 devices in a mesh: ctx: 8 (over z, x), tp: 4 (over y, core).
Axes of the slice: x: 2, y: 2, z: 4, core: 2. Of those that a mesh axis runs over, the one named last changes fastest.
Arguments:
- inputs: bfloat16 [4, 8, 2, 64, 1024], P(None, 'ctx', None, 'tp'), may hold values from -6 to 6
- pairing: int32 [4, 8], replicated, may hold values from 0 to 7, each once within a row
- first_gain: bfloat16 [1024], P('ctx'), may hold values from 0.5 to 1.5
- first_shift: bfloat16 [1024], P('ctx'), may hold values from -1 to 1
- query_key_value_weight: bfloat16 [1024, 3, 1024], P('ctx', None, 'tp'), may hold values from -0.1875 to 0.1875
- mix_bias: bfloat16 [2, 4, 256], P(None, 'tp', 'ctx'), may hold values from -1.5 to 1.5
- output_projection_weight: bfloat16 [1024, 1024], P('tp', 'ctx'), may hold values from -0.875 to 0.875
- out_bias: bfloat16 [1024], P('ctx'), may hold values from -1 to 1
- second_gain: bfloat16 [1024], P('ctx'), may hold values from 0.5 to 1.5
- second_shift: bfloat16 [1024], P('ctx'), may hold values from -1 to 1
- up_projection_weight: bfloat16 [1024, 4096], P('ctx', 'tp'), may hold values from -0.1875 to 0.1875
- up_projection_bias: bfloat16 [4, 1024], P('tp', 'ctx'), may hold values from -1.5 to 1.5
- down_projection_weight: bfloat16 [4096, 1024], P('tp', 'ctx'), may hold values from -0.09375 to 0.09375
- down_bias: bfloat16 [1024], P('ctx'), may hold values from -1 to 1
- cotangent: bfloat16 [4, 8, 2, 64, 1024], P(None, 'ctx', None, 'tp'), may hold values from -6 to 6
Outputs:
- result: bfloat16 [4, 8, 2, 64, 1024], P(None, 'ctx', None, 'tp')
- grad_inputs: float32 [4, 8, 2, 64, 1024], P(None, 'ctx', None, 'tp')
- grad_first_gain: float32 [1024], P('ctx')
- grad_first_shift: float32 [1024], P('ctx')
- grad_mix_weight: float32 [1024, 3, 1024], P('ctx', None, 'tp')
- grad_mix_bias: float32 [2, 4, 256], P(None, 'tp', 'ctx')
- grad_out_weight: float32 [1024, 1024], P('tp', 'ctx')
- grad_out_bias: float32 [1024], P('ctx')
- grad_second_gain: float32 [1024], P('ctx')
- grad_second_shift: float32 [1024], P('ctx')
- grad_up_weight: float32 [1024, 4096], P('ctx', 'tp')
- grad_up_bias: float32 [4, 1024], P('tp', 'ctx')
- grad_down_weight: float32 [4096, 1024], P('tp', 'ctx')
- grad_down_bias: float32 [1024], P('ctx')
Inputs may be any that keep to these rules, and one draw needn't show every extreme that they name: Each row of pairing is a permutation: every pair of blocks of a sequence is held by exactly one slot.
All inputs are finite; a program needn't handle non-finite values.
Results may differ from a plain program's by a relative error of at most 0.018.
Values may be sent and summed in bfloat16 or wider, within the bound.
No kernel may reach another device: no remote copies, remote signals or barrier semaphores. Data moves between devices by JAX's collectives and lax.ppermute only.
A program may use at most 320 MiB of HBM per device.

v0:
```python
import jax
import jax.numpy as jnp
from jax import lax
from jax.experimental import pallas as pl
from jax.experimental.pallas import tpu as pltpu
from jax.sharding import PartitionSpec as P

HD = 64


epsilon = 1e-05


def normalize(token_rows, scaling, offset):
    row_mean = jnp.mean(token_rows, axis=-1, keepdims=True)
    centered = token_rows - row_mean
    variance = jnp.mean(centered * centered, axis=-1, keepdims=True)
    return centered * lax.rsqrt(variance + epsilon) * scaling + offset


def gelu_tanh(values_in):
    return jax.nn.gelu(values_in, approximate=True)


def block_places(pairing_rows, block_rows):
    slot_count = pairing_rows.shape[-1]
    starts = jnp.stack([pairing_rows, 2 * slot_count - 1 - pairing_rows], axis=-1) * block_rows
    within = jnp.arange(block_rows, dtype=jnp.int32)
    return (starts[:, :, :, None] + within).reshape(pairing_rows.shape[0], -1)


def by_head(tensor, head_count):
    seq_span, row_span, model_width = tensor.shape
    return jnp.moveaxis(
        tensor.reshape(seq_span, row_span, head_count, model_width // head_count), 2, 0
    )


def from_head(tensor):
    head_count, seq_span, row_span, head_size = tensor.shape
    return jnp.moveaxis(tensor, 0, 2).reshape(seq_span, row_span, head_count * head_size)


def head_scores(queries, key_vectors, allowed, score_scale):
    scores = (
        jnp.einsum("gqd,gkd->gqk", queries, key_vectors, preferred_element_type=jnp.float32)
        * score_scale
    )
    return jnp.where(allowed, scores, -jnp.inf)


def recompute(queries, key_vectors, value_vectors, grad_out, log_total, allowed, score_scale):
    scores = head_scores(queries, key_vectors, allowed, score_scale)
    probabilities = jnp.exp(scores - log_total[:, :, None])
    grad_probs = jnp.einsum(
        "gqd,gkd->gqk", grad_out, value_vectors, preferred_element_type=jnp.float32
    )
    return (probabilities, grad_probs)


def spread_rows(normed):
    return lax.all_gather(normed, "tp", axis=2, tiled=True)


def collect_rows(partial_terms):
    return lax.psum_scatter(
        partial_terms.astype(jnp.bfloat16), "tp", scatter_dimension=2, tiled=True
    ).astype(jnp.float32)


def spread_grads(gradient_part):
    return lax.all_gather(gradient_part, "tp", axis=2, tiled=True)


def collect_grads(partial_terms):
    return lax.psum_scatter(
        partial_terms.astype(jnp.bfloat16), "tp", scatter_dimension=2, tiled=True
    ).astype(jnp.float32)


def fetch_keys(key_part, value_part):
    return (
        lax.all_gather(key_part, "ctx", axis=1, tiled=True),
        lax.all_gather(value_part, "ctx", axis=1, tiled=True),
    )


def general_body(
    inputs,
    pairing,
    first_gain,
    first_shift,
    query_key_value_weight,
    mix_bias,
    output_projection_weight,
    out_bias,
    second_gain,
    second_shift,
    up_projection_weight,
    up_projection_bias,
    down_projection_weight,
    down_bias,
    cotangent,
):
    seq_count = inputs.shape[0]
    part_rows = inputs.shape[3]
    model_width = inputs.shape[4]
    tp_count = lax.axis_size("tp")
    block_rows = part_rows * tp_count
    local_rows = 2 * block_rows
    ctx_index = lax.axis_index("ctx")
    score_scale = HD ** (-0.5)
    batch_seqs = seq_count
    for candidate in range(seq_count, 0, -1):
        if seq_count % candidate == 0 and candidate * local_rows >= 512:
            batch_seqs = candidate
    groups = seq_count // batch_seqs
    vector_stack = jnp.stack(
        [first_gain, first_shift, out_bias, second_gain, second_shift, down_bias]
    )
    fetched = (
        lax.all_gather(vector_stack, "ctx", axis=1, tiled=True),
        lax.all_gather(query_key_value_weight, "ctx", axis=0, tiled=True),
        lax.all_gather(mix_bias, "ctx", axis=2, tiled=True),
        lax.all_gather(output_projection_weight, "ctx", axis=1, tiled=True),
        lax.all_gather(up_projection_weight, "ctx", axis=0, tiled=True),
        lax.all_gather(up_projection_bias, "ctx", axis=1, tiled=True),
        lax.all_gather(down_projection_weight, "ctx", axis=1, tiled=True),
    )
    vectors_full = fetched[0].astype(jnp.float32)
    dim_local = fetched[2].shape[2]
    head_count = dim_local // HD
    token_rows = inputs.reshape(seq_count, 2, part_rows, model_width).astype(jnp.float32)
    first_norm_output = normalize(token_rows, vectors_full[0], vectors_full[1]).astype(jnp.bfloat16)
    first_all = spread_rows(first_norm_output)
    projected_output = jnp.einsum(
        "sabd,dkc->sabkc", first_all, fetched[1], preferred_element_type=jnp.float32
    )
    bias_full = fetched[2].astype(jnp.float32)
    bias_rows = jnp.stack([bias_full[0, 0], jnp.zeros((dim_local,), jnp.float32), bias_full[1, 0]])
    projected_output = (projected_output + bias_rows).astype(jnp.bfloat16)

    def grouped(tensor):
        return tensor.reshape(groups, batch_seqs, local_rows, tensor.shape[-1])

    def ungrouped(tensor):
        return tensor.reshape(seq_count, 2, block_rows, dim_local)

    query_groups = grouped(projected_output[:, :, :, 0])
    key_groups = grouped(projected_output[:, :, :, 1])
    value_groups = grouped(projected_output[:, :, :, 2])
    pairing_groups = pairing.reshape(groups, batch_seqs, pairing.shape[1])

    def forward_group(unused_carry, inputs_group):
        query_part, key_part, value_part, pairing_rows = inputs_group
        key_all, value_all = fetch_keys(key_part, value_part)
        places = block_places(pairing_rows, block_rows)
        own_places = lax.dynamic_slice_in_dim(places, ctx_index * local_rows, local_rows, 1)
        allowed = own_places[:, :, None] >= places[:, None, :]

        def head_forward(operands):
            queries, key_vectors, value_vectors = operands
            scores = head_scores(queries, key_vectors, allowed, score_scale)
            row_max = jnp.max(scores, axis=-1, keepdims=True)
            exponent = jnp.exp(scores - row_max)
            row_total = jnp.sum(exponent, axis=-1, keepdims=True)
            weights_low = (exponent / row_total).astype(jnp.bfloat16)
            attention_result = jnp.einsum(
                "gqk,gkd->gqd", weights_low, value_vectors, preferred_element_type=jnp.float32
            )
            return (attention_result.astype(jnp.bfloat16), (row_max + jnp.log(row_total))[:, :, 0])

        outputs, log_totals = lax.map(
            head_forward,
            (
                by_head(query_part, head_count),
                by_head(key_all, head_count),
                by_head(value_all, head_count),
            ),
        )
        return (unused_carry, (from_head(outputs), log_totals))

    unused_state, (output_groups, log_groups) = lax.scan(
        forward_group, None, (query_groups, key_groups, value_groups, pairing_groups)
    )
    attention_result = ungrouped(output_groups)
    residual_branch = collect_rows(
        jnp.einsum(
            "sabc,cd->sabd", attention_result, fetched[3], preferred_element_type=jnp.float32
        )
    )
    hidden = token_rows + residual_branch + vectors_full[2]
    second_norm_output = normalize(hidden, vectors_full[3], vectors_full[4]).astype(jnp.bfloat16)
    second_all = spread_rows(second_norm_output)
    before_activation = jnp.einsum(
        "sabd,df->sabf", second_all, fetched[4], preferred_element_type=jnp.float32
    ) + fetched[5][0].astype(jnp.float32)
    activation_rows = gelu_tanh(before_activation).astype(jnp.bfloat16)
    residual_branch_two = collect_rows(
        jnp.einsum("sabf,fd->sabd", activation_rows, fetched[6], preferred_element_type=jnp.float32)
    )
    result = (hidden + residual_branch_two + vectors_full[5]).astype(jnp.bfloat16)
    vectors_back = fetched[0].astype(jnp.float32)
    grad_result_low = cotangent.reshape(seq_count, 2, part_rows, model_width)
    grad_result = grad_result_low.astype(jnp.float32)
    grad_down_bias = jnp.sum(grad_result, axis=(0, 1, 2))
    grad_branch_two = spread_grads(grad_result_low)
    grad_down = jnp.einsum(
        "sabf,sabd->fd", activation_rows, grad_branch_two, preferred_element_type=jnp.float32
    )
    grad_activated = jnp.einsum(
        "sabd,fd->sabf", grad_branch_two, fetched[6], preferred_element_type=jnp.float32
    )
    gelu_pull = jax.vjp(gelu_tanh, before_activation)[1]
    grad_pre = gelu_pull(grad_activated)[0].astype(jnp.bfloat16)
    grad_up_bias = jnp.sum(grad_pre, axis=(0, 1, 2), dtype=jnp.float32)
    grad_up = jnp.einsum("sabd,sabf->df", second_all, grad_pre, preferred_element_type=jnp.float32)
    grad_second = collect_grads(
        jnp.einsum("sabf,df->sabd", grad_pre, fetched[4], preferred_element_type=jnp.float32)
    )
    second_pull = jax.vjp(normalize, hidden, vectors_back[3], vectors_back[4])[1]
    grad_hidden_norm, grad_second_gain, grad_second_shift = second_pull(grad_second)
    grad_hidden = grad_result + grad_hidden_norm
    grad_out_bias = jnp.sum(grad_hidden, axis=(0, 1, 2))
    grad_branch = spread_grads(grad_hidden.astype(jnp.bfloat16))
    grad_out_weight = jnp.einsum(
        "sabc,sabd->cd", attention_result, grad_branch, preferred_element_type=jnp.float32
    )
    grad_attended = jnp.einsum(
        "sabd,cd->sabc", grad_branch, fetched[3], preferred_element_type=jnp.float32
    ).astype(jnp.bfloat16)
    grad_groups = grouped(grad_attended)

    def backward_group(unused_carry, inputs_group):
        query_part, key_part, value_part, grad_part, log_part, pairing_rows = inputs_group
        key_all, value_all = fetch_keys(key_part, value_part)
        places = block_places(pairing_rows, block_rows)
        own_places = lax.dynamic_slice_in_dim(places, ctx_index * local_rows, local_rows, 1)
        allowed = own_places[:, :, None] >= places[:, None, :]

        def joint_pass(operands):
            queries, key_vectors, value_vectors, grad_out, log_total = operands
            probabilities, grad_probs = recompute(
                queries, key_vectors, value_vectors, grad_out, log_total, allowed, score_scale
            )
            row_delta = jnp.sum(probabilities * grad_probs, axis=-1, keepdims=True)
            grad_scores = (probabilities * (grad_probs - row_delta)).astype(jnp.bfloat16)
            grad_query = (
                jnp.einsum(
                    "gqk,gkd->gqd", grad_scores, key_vectors, preferred_element_type=jnp.float32
                )
                * score_scale
            )
            grad_key = (
                jnp.einsum("gqk,gqd->gkd", grad_scores, queries, preferred_element_type=jnp.float32)
                * score_scale
            )
            grad_value = jnp.einsum(
                "gqk,gqd->gkd",
                probabilities.astype(jnp.bfloat16),
                grad_out,
                preferred_element_type=jnp.float32,
            )
            return (grad_query, grad_key, grad_value)

        grad_queries, grad_keys, grad_values = lax.map(
            joint_pass,
            (
                by_head(query_part, head_count),
                by_head(key_all, head_count),
                by_head(value_all, head_count),
                by_head(grad_part, head_count),
                log_part,
            ),
        )
        grad_key_rows, grad_value_rows = (
            lax.psum_scatter(from_head(grad_keys), "ctx", scatter_dimension=1, tiled=True),
            lax.psum_scatter(from_head(grad_values), "ctx", scatter_dimension=1, tiled=True),
        )
        return (
            unused_carry,
            (
                from_head(grad_queries).astype(jnp.bfloat16),
                grad_key_rows.astype(jnp.bfloat16),
                grad_value_rows.astype(jnp.bfloat16),
            ),
        )

    unused_back, (query_grads, key_grads, value_grads) = lax.scan(
        backward_group,
        None,
        (query_groups, key_groups, value_groups, grad_groups, log_groups, pairing_groups),
    )
    grad_query_rows = ungrouped(query_grads)
    grad_value_rows = ungrouped(value_grads)
    grad_projected = jnp.stack([grad_query_rows, ungrouped(key_grads), grad_value_rows], axis=3)
    grad_mix_bias = jnp.stack(
        [
            jnp.sum(grad_query_rows, axis=(0, 1, 2), dtype=jnp.float32),
            jnp.sum(grad_value_rows, axis=(0, 1, 2), dtype=jnp.float32),
        ]
    )[:, None, :]
    grad_mix = jnp.einsum(
        "sabd,sabkc->dkc", first_all, grad_projected, preferred_element_type=jnp.float32
    )
    grad_first = collect_grads(
        jnp.einsum(
            "sabkc,dkc->sabd", grad_projected, fetched[1], preferred_element_type=jnp.float32
        )
    )
    first_pull = jax.vjp(normalize, token_rows, vectors_back[0], vectors_back[1])[1]
    grad_token_norm, grad_first_gain, grad_first_shift = first_pull(grad_first)
    grad_inputs = (grad_hidden + grad_token_norm).reshape(inputs.shape)
    vector_grads = jnp.stack(
        [
            grad_first_gain,
            grad_first_shift,
            grad_out_bias,
            grad_second_gain,
            grad_second_shift,
            grad_down_bias,
        ]
    )
    shards = (
        lax.psum_scatter(vector_grads, "ctx", scatter_dimension=1, tiled=True),
        lax.psum_scatter(grad_mix, "ctx", scatter_dimension=0, tiled=True),
        lax.psum_scatter(grad_mix_bias, "ctx", scatter_dimension=2, tiled=True),
        lax.psum_scatter(grad_out_weight, "ctx", scatter_dimension=1, tiled=True),
        lax.psum_scatter(grad_up, "ctx", scatter_dimension=0, tiled=True),
        lax.psum_scatter(grad_up_bias[None, :], "ctx", scatter_dimension=1, tiled=True),
        lax.psum_scatter(grad_down, "ctx", scatter_dimension=1, tiled=True),
    )
    vector_shard = lax.psum(shards[0], "tp")
    return (
        result.reshape(inputs.shape),
        grad_inputs,
        vector_shard[0],
        vector_shard[1],
        shards[1],
        shards[2],
        shards[3],
        vector_shard[2],
        vector_shard[3],
        vector_shard[4],
        shards[4],
        shards[5],
        shards[6],
        vector_shard[5],
    )


LANES = 128
CHUNK = 256
NT = (((1,), (1,)), ((), ()))
NN = (((1,), (0,)), ((), ()))
TN = (((0,), (0,)), ((), ()))


def mm(left, right, dims):
    return lax.dot_general(left, right, dims, preferred_element_type=jnp.float32)


def causal(span, chunk):
    key_place = lax.broadcasted_iota(jnp.int32, (span, chunk), 0)
    query_place = lax.broadcasted_iota(jnp.int32, (span, chunk), 1) + (span - chunk)
    return key_place <= query_place


def to_places(slots_ref, source, target, block_rows):
    for block in range(target.shape[0] // block_rows):
        start = pl.multiple_of(slots_ref[block] * block_rows, block_rows)
        target[pl.ds(block * block_rows, block_rows), :] = source[pl.ds(start, block_rows), :]


def to_slots(slots_ref, values, target, first_block, block_rows):
    for block in range(values.shape[0] // block_rows):
        start = pl.multiple_of(slots_ref[first_block + block] * block_rows, block_rows)
        target[pl.ds(start, block_rows), :] = values[block * block_rows : (block + 1) * block_rows]


def forward_kernel(block_rows, slots_ref, qkv_ref, out_ref, log_ref, rows):
    length, wide = rows.shape
    width = wide // 3
    chunk = min(CHUNK, length)
    to_places(slots_ref, qkv_ref, rows, block_rows)
    log_ref[...] = jnp.zeros(log_ref.shape, jnp.float32)
    for part in range(length // chunk):
        low, high = part * chunk, (part + 1) * chunk
        allowed = causal(high, chunk)
        columns = []
        for head in range(width // HD):
            lane = head * HD
            queries = rows[low:high, lane : lane + HD]
            keys = rows[0:high, width + lane : width + lane + HD]
            values = rows[0:high, 2 * width + lane : 2 * width + lane + HD]
            scores = jnp.where(allowed, mm(keys, queries, NT) * HD ** (-0.5), -1e30)
            top = jnp.max(scores, axis=0, keepdims=True)
            exponent = jnp.exp(scores - top)
            total = jnp.sum(exponent, axis=0, keepdims=True)
            weights = (exponent * (1.0 / total)).astype(jnp.bfloat16)
            columns.append(mm(values, weights, TN))
            log_ref[head : head + 1, low:high] = top + jnp.log(total)
        attended = jnp.concatenate(columns, axis=0).T.astype(jnp.bfloat16)
        to_slots(slots_ref, attended, out_ref, low // block_rows, block_rows)


def backward_kernel(
    block_rows, slots_ref, qkv_ref, grad_ref, log_ref, out_ref, rows, grads, key_sum, value_sum
):
    length, wide = rows.shape
    width = wide // 3
    chunk = min(CHUNK, length)
    scale = HD ** (-0.5)
    to_places(slots_ref, qkv_ref, rows, block_rows)
    to_places(slots_ref, grad_ref, grads, block_rows)
    key_sum[...] = jnp.zeros(key_sum.shape, jnp.float32)
    value_sum[...] = jnp.zeros(value_sum.shape, jnp.float32)
    for part in range(length // chunk):
        low, high = part * chunk, (part + 1) * chunk
        allowed = causal(high, chunk)
        query_columns, key_parts, value_parts = [], [], []
        for head in range(width // HD):
            lane = head * HD
            queries = rows[low:high, lane : lane + HD]
            keys = rows[0:high, width + lane : width + lane + HD]
            values = rows[0:high, 2 * width + lane : 2 * width + lane + HD]
            grad_out = grads[low:high, lane : lane + HD]
            scores = jnp.where(allowed, mm(keys, queries, NT) * scale, -1e30)
            probs = jnp.exp(scores - log_ref[head : head + 1, low:high])
            grad_probs = mm(values, grad_out, NT)
            delta = jnp.sum(probs * grad_probs, axis=0, keepdims=True)
            grad_scores = (probs * (grad_probs - delta)).astype(jnp.bfloat16)
            value_parts.append(mm(probs.astype(jnp.bfloat16), grad_out, NN))
            key_parts.append(mm(grad_scores, queries, NN))
            query_columns.append(mm(keys, grad_scores, TN))
        key_sum[0:high, :] += jnp.concatenate(key_parts, axis=1)
        value_sum[0:high, :] += jnp.concatenate(value_parts, axis=1)
        grad_query = (jnp.concatenate(query_columns, axis=0).T * scale).astype(jnp.bfloat16)
        to_slots(
            slots_ref, grad_query, out_ref.at[:, 0:width], low // block_rows, block_rows
        )
    to_slots(
        slots_ref,
        (key_sum[...] * scale).astype(jnp.bfloat16),
        out_ref.at[:, width : 2 * width],
        0,
        block_rows,
    )
    to_slots(
        slots_ref,
        value_sum[...].astype(jnp.bfloat16),
        out_ref.at[:, 2 * width : 3 * width],
        0,
        block_rows,
    )


def whole_shape(shape):
    return pl.BlockSpec(shape, lambda step: (0,) * len(shape))


def whole_block(array):
    return whole_shape(array.shape)


SMEM_SPEC = pl.BlockSpec(memory_space=pltpu.SMEM)
KERNEL_PARAMS = pltpu.CompilerParams(vmem_limit_bytes=60 * 1024 * 1024)


def attend_forward(slots, qkv, block_rows):
    length, wide = qkv.shape
    width = wide // 3
    area = length * length * width
    return pl.pallas_call(
        lambda *refs: forward_kernel(block_rows, *refs),
        out_shape=(
            jax.ShapeDtypeStruct((length, width), jnp.bfloat16),
            jax.ShapeDtypeStruct((8, length), jnp.float32),
        ),
        grid=(1,),
        in_specs=[SMEM_SPEC, whole_block(qkv)],
        out_specs=(whole_shape((length, width)), whole_shape((8, length))),
        scratch_shapes=[pltpu.VMEM((length, wide), jnp.bfloat16)],
        compiler_params=KERNEL_PARAMS,
        cost_estimate=pl.CostEstimate(
            flops=3 * area, bytes_accessed=8 * length * width, transcendentals=area // HD
        ),
        name="attend_forward",
    )(slots, qkv)


def attend_backward(slots, qkv, grad_out, log_total, block_rows):
    length, wide = qkv.shape
    width = wide // 3
    area = length * length * width
    return pl.pallas_call(
        lambda *refs: backward_kernel(block_rows, *refs),
        out_shape=jax.ShapeDtypeStruct((length, wide), jnp.bfloat16),
        grid=(1,),
        in_specs=[SMEM_SPEC, whole_block(qkv), whole_block(grad_out), whole_block(log_total)],
        out_specs=whole_shape((length, wide)),
        scratch_shapes=[
            pltpu.VMEM((length, wide), jnp.bfloat16),
            pltpu.VMEM((length, width), jnp.bfloat16),
            pltpu.VMEM((length, width), jnp.float32),
            pltpu.VMEM((length, width), jnp.float32),
        ],
        compiler_params=KERNEL_PARAMS,
        cost_estimate=pl.CostEstimate(
            flops=7 * area, bytes_accessed=14 * length * width, transcendentals=area // HD
        ),
        name="attend_backward",
    )(slots, qkv, grad_out, log_total)


def swap(values, axis, bit):
    count = lax.axis_size(axis)
    return lax.ppermute(values, axis, [(i, i ^ bit) for i in range(count)])


def together(*groups):
    return lax.optimization_barrier(groups)


def spread_step(held, axis, bit):
    keys = tuple(key for offsets, _ in held for key in offsets)
    arrays = [array for _, array in held]
    sent = arrays[0] if len(arrays) == 1 else jnp.concatenate(arrays, axis=0)
    return (keys, sent), (tuple(key ^ bit for key in keys), swap(sent, axis, bit))


def pack_kernel(pieces, mix_ref, out_weight_ref, *refs):
    vectors, (head_ref, tail_ref) = refs[:-2], refs[-2:]
    half = tail_ref.shape[1]
    parts, _, part_width = mix_ref.shape
    mix_width = parts * part_width
    shard = 2 * half
    for target, first in ((head_ref, 0), (tail_ref, half)):
        for part in range(parts):
            target[0, 0:half, part * part_width : (part + 1) * part_width] = mix_ref[
                part, first : first + half, :
            ]
        for piece in range(pieces):
            target[0, 0:half, mix_width + piece * shard : mix_width + (piece + 1) * shard] = (
                out_weight_ref[piece * shard + first : piece * shard + first + half, :]
            )
    extra = head_ref.shape[1] - half
    head_ref[0, half:, :] = jnp.zeros((extra, head_ref.shape[2]), jnp.bfloat16)
    for number, vector in enumerate(vectors):
        head_ref[0, half : half + 1, number * shard : number * shard + vector.shape[1]] = vector[...]


def late_kernel(up_ref, down_ref, late_ref):
    hidden_local = up_ref.shape[1]
    late_ref[:, 0:hidden_local] = up_ref[...]
    late_ref[:, hidden_local:] = down_ref[...].T


def pack_late(up_shard, down_shard):
    shard, hidden_local = up_shard.shape
    return pl.pallas_call(
        late_kernel,
        out_shape=jax.ShapeDtypeStruct((shard, 2 * hidden_local), jnp.bfloat16),
        grid=(1,),
        in_specs=[whole_block(up_shard), whole_block(down_shard)],
        out_specs=whole_shape((shard, 2 * hidden_local)),
        compiler_params=KERNEL_PARAMS,
        name="pack_late",
    )(up_shard, down_shard)


def pack(mix_shard, out_shard, vectors):
    parts, shard, part_width = mix_shard.shape
    pieces = out_shard.shape[0] // shard
    total = parts * part_width + out_shard.shape[0]
    return pl.pallas_call(
        lambda *refs: pack_kernel(pieces, *refs),
        out_shape=(
            jax.ShapeDtypeStruct((1, shard // 2 + 16, total), jnp.bfloat16),
            jax.ShapeDtypeStruct((1, shard // 2, total), jnp.bfloat16),
        ),
        grid=(1,),
        in_specs=[whole_block(array) for array in (mix_shard, out_shard, *vectors)],
        out_specs=(
            whole_shape((1, shard // 2 + 16, total)),
            whole_shape((1, shard // 2, total)),
        ),
        compiler_params=KERNEL_PARAMS,
        name="pack",
    )(mix_shard, out_shard, *vectors)


def first_kernel(head_keys, tail_keys, sizes, own_ref, *refs):
    groups, width, vector_count, bias_width = sizes
    tp_count = 4
    parts, refs = refs[:tp_count], refs[tp_count:]
    heads, refs = refs[: len(head_keys)], refs[len(head_keys) :]
    tails, refs = refs[: len(tail_keys)], refs[len(tail_keys) :]
    rows_ref, first_ref, weight_ref, out_weight_ref, table_ref, send_ref, gathered = refs
    own_tp, own_ctx = own_ref[0], own_ref[1]
    mix_width = weight_ref.shape[1]
    half = tails[0].shape[1]
    shard = 2 * half

    def put_out(piece, place, owner, first):
        columns = pl.ds(pl.multiple_of(owner * shard, shard), shard)
        for number in range(out_weight_ref.shape[0] // shard):
            low = mix_width + number * shard
            out_weight_ref[number * shard + first : number * shard + first + half, columns] = piece[
                place, 0:half, low : low + shard
            ]

    for keys, piece in zip(head_keys, heads):
        for place, key in enumerate(keys):
            owner = own_ctx ^ key
            rows = pl.ds(pl.multiple_of(owner * shard, shard), half)
            weight_ref[rows, :] = piece[place, 0:half, 0:mix_width]
            put_out(piece, place, owner, 0)
            extra = piece[place, half:, :].astype(jnp.float32)
            gathered[pl.ds(owner, 1), :] = extra[0:1, :]
    for keys, piece in zip(tail_keys, tails):
        for place, key in enumerate(keys):
            owner = own_ctx ^ key
            rows = pl.ds(pl.multiple_of(owner * shard + half, half), half)
            weight_ref[rows, :] = piece[place, :, 0:mix_width]
            put_out(piece, place, owner, half)
    count = gathered.shape[0]
    vectors = gathered[...]
    table_ref[...] = jnp.zeros(table_ref.shape, jnp.float32)
    for number in range(vector_count):
        lanes = slice(number * shard, (number + 1) * shard)
        for owner in range(count):
            table_ref[number : number + 1, owner * shard : (owner + 1) * shard] = vectors[
                owner : owner + 1, lanes
            ]
    bias_parts = []
    for number in range(2):
        low = vector_count * shard + number * bias_width
        bias_parts.append(
            jnp.concatenate(
                [vectors[owner : owner + 1, low : low + bias_width] for owner in range(count)],
                axis=1,
            )
        )
    bias = jnp.concatenate([bias_parts[0], jnp.zeros_like(bias_parts[0]), bias_parts[1]], axis=1)
    piece_count, part_rows, _ = parts[0].shape
    block_rows = tp_count * part_rows
    for key in range(tp_count):
        for piece in range(piece_count):
            row = pl.multiple_of(piece * block_rows + (own_tp ^ key) * part_rows, part_rows)
            rows_ref[pl.ds(row, part_rows), :] = parts[key][piece]
    seq_rows = send_ref.shape[1]
    dim_local = mix_width // 3
    gain, shift = table_ref[0:1, :], table_ref[1:2, :]
    for seq in range(rows_ref.shape[0] // seq_rows):
        rows = slice(seq * seq_rows, (seq + 1) * seq_rows)
        centered, scale = norm_parts(rows_ref[rows, :].astype(jnp.float32))
        normed = (centered * scale * gain + shift).astype(jnp.bfloat16)
        first_ref[rows, :] = normed
        projected = (mm(normed, weight_ref[...], NN) + bias).astype(jnp.bfloat16)
        for group in range(groups):
            for number in range(3):
                low = number * dim_local + group * width
                send_ref[seq * groups + group, :, number * width : (number + 1) * width] = (
                    projected[:, low : low + width]
                )


def first_part(own, parts, heads, tails, seq_count, groups, vector_count, bias_width):
    piece_count, part_rows, model_width = parts[0].shape
    row_count = piece_count * part_rows * 4
    count = seq_count * groups
    mix_width = 3 * model_width // 4
    head_keys, head_arrays = zip(*heads)
    tail_keys, tail_arrays = zip(*tails)
    seq_rows = row_count // seq_count
    width = mix_width // (3 * groups)
    low = jnp.bfloat16
    shapes = (
        ((row_count, model_width), low),
        ((row_count, model_width), low),
        ((model_width, mix_width), low),
        ((head_arrays[0].shape[2] - mix_width, model_width), low),
        ((8, model_width), jnp.float32),
        ((count, seq_rows, 3 * width), low),
    )
    return pl.pallas_call(
        lambda *refs: first_kernel(
            head_keys, tail_keys, (groups, width, vector_count, bias_width), *refs
        ),
        out_shape=tuple(jax.ShapeDtypeStruct(*shape) for shape in shapes),
        grid=(1,),
        in_specs=[SMEM_SPEC]
        + [whole_block(array) for array in (*parts, *head_arrays, *tail_arrays)],
        out_specs=tuple(whole_shape(shape) for shape, _ in shapes),
        scratch_shapes=[pltpu.VMEM((count, head_arrays[0].shape[2]), jnp.float32)],
        compiler_params=KERNEL_PARAMS,
        cost_estimate=pl.CostEstimate(
            flops=2 * row_count * model_width * mix_width,
            bytes_accessed=8 * 1024 * 1024,
            transcendentals=0,
        ),
        name="first_part",
    )(own, *parts, *head_arrays, *tail_arrays)


def feed_grads_kernel(second_ref, grad_pre_ref, cot_ref, activated_ref, out_ref):
    half = grad_pre_ref.shape[1]
    out_ref[:, 0:half] = mm(second_ref[...], grad_pre_ref[...], TN).astype(jnp.bfloat16)
    out_ref[:, half:] = mm(cot_ref[...], activated_ref[...], TN).astype(jnp.bfloat16)


def feed_grads(second_all, grad_pre, cot_all, activated):
    row_count, model_width = second_all.shape
    hidden_local = grad_pre.shape[1]
    step = min(256, model_width)
    column = pl.BlockSpec((row_count, step), lambda i: (0, i))
    fixed = pl.BlockSpec((row_count, hidden_local), lambda i: (0, 0))
    return pl.pallas_call(
        feed_grads_kernel,
        grid=(model_width // step,),
        out_shape=jax.ShapeDtypeStruct((model_width, 2 * hidden_local), jnp.bfloat16),
        in_specs=[column, fixed, column, fixed],
        out_specs=pl.BlockSpec((step, 2 * hidden_local), lambda i: (i, 0)),
        compiler_params=KERNEL_PARAMS,
        cost_estimate=pl.CostEstimate(
            flops=4 * row_count * model_width * hidden_local,
            bytes_accessed=8 * 1024 * 1024,
            transcendentals=0,
        ),
        name="feed_grads",
    )(second_all, grad_pre, cot_all, activated)


def feed_finish_kernel(sum_ref, up_ref, down_ref):
    half = up_ref.shape[1]
    up_ref[...] = sum_ref[:, 0:half].astype(jnp.float32)
    down_ref[...] = sum_ref[:, half:].astype(jnp.float32).T


def feed_finish(total):
    shard, twice = total.shape
    shapes = ((shard, twice // 2), (twice // 2, shard))
    return pl.pallas_call(
        feed_finish_kernel,
        grid=(1,),
        out_shape=tuple(jax.ShapeDtypeStruct(shape, jnp.float32) for shape in shapes),
        in_specs=[whole_block(total)],
        out_specs=tuple(whole_shape(shape) for shape in shapes),
        compiler_params=KERNEL_PARAMS,
        name="feed_finish",
    )(total)


def mix_finish_kernel(mine_ref, came_ref, mix_ref, out_ref):
    total = mine_ref[...].astype(jnp.float32) + came_ref[...].astype(jnp.float32)
    parts, _, part_width = mix_ref.shape
    for part in range(parts):
        mix_ref[part] = total[:, part * part_width : (part + 1) * part_width]
    out_ref[...] = total[:, parts * part_width :].T


def mix_finish(mine, came, dim_local):
    shapes = ((3, came.shape[0], dim_local), (dim_local, came.shape[0]))
    return pl.pallas_call(
        mix_finish_kernel,
        grid=(1,),
        out_shape=tuple(jax.ShapeDtypeStruct(shape, jnp.float32) for shape in shapes),
        in_specs=[whole_block(mine), whole_block(came)],
        out_specs=tuple(whole_shape(shape) for shape in shapes),
        compiler_params=KERNEL_PARAMS,
        name="mix_finish",
    )(mine, came)


MLP_ROWS = 128


def branch_kernel(own_ref, attended_ref, weight_ref, mine_ref, other_ref):
    core = own_ref[0] & 1
    count, seq_rows, width = attended_ref.shape
    seqs = mine_ref.shape[0] // seq_rows
    groups = count // (2 * seqs)
    for half, out_ref in enumerate((mine_ref, other_ref)):
        for seq in range(seqs):
            first = ((core ^ half) * seqs + seq) * groups
            total = mm(attended_ref[first], weight_ref[0:width, :], NN)
            for group in range(1, groups):
                total += mm(
                    attended_ref[first + group],
                    weight_ref[group * width : (group + 1) * width, :],
                    NN,
                )
            out_ref[seq * seq_rows : (seq + 1) * seq_rows, :] = total.astype(jnp.bfloat16)


def branch_part(own, attended, out_full):
    count, seq_rows, width = attended.shape
    rows = count * seq_rows * width // out_full.shape[0]
    shape = (rows // 2, out_full.shape[1])
    return pl.pallas_call(
        branch_kernel,
        grid=(1,),
        out_shape=(jax.ShapeDtypeStruct(shape, jnp.bfloat16),) * 2,
        in_specs=[SMEM_SPEC, whole_block(attended), whole_block(out_full)],
        out_specs=(whole_shape(shape),) * 2,
        compiler_params=KERNEL_PARAMS,
        name="branch_part",
    )(own, attended, out_full)


def hidden_grad_kernel(
    own_ref,
    sum_ref,
    other_ref,
    cot_ref,
    hidden_ref,
    table_ref,
    weight_ref,
    send_ref,
    branch_ref,
    own_grad_ref,
    sums_ref,
    rows_ref,
):
    own_tp = own_ref[0]
    core = own_tp & 1
    count, seq_rows, width = send_ref.shape
    _, part_rows, model_width = own_grad_ref.shape
    seqs = sum_ref.shape[0] // seq_rows
    groups = count // (2 * seqs)
    block_rows = seq_rows // 2
    gain = table_ref[3:4, :]
    sums = [jnp.zeros((1, model_width), jnp.float32) for _ in range(3)]
    for half, grad_ref in enumerate((sum_ref, other_ref)):
        for chunk in range(seqs):
            seq = (core ^ half) * seqs + chunk
            rows = pl.ds(pl.multiple_of(seq * seq_rows, seq_rows), seq_rows)
            grad = grad_ref[chunk * seq_rows : (chunk + 1) * seq_rows, :].astype(jnp.float32)
            centered, scale = norm_parts(hidden_ref[rows, :])
            normal = centered * scale
            total = cot_ref[rows, :].astype(jnp.float32) + norm_backward(normal, scale, grad, gain)
            low = total.astype(jnp.bfloat16)
            branch_ref[rows, :] = low
            rows_ref[...] = total
            for block in range(2):
                first = pl.multiple_of(block * block_rows + own_tp * part_rows, part_rows)
                own_grad_ref[seq * 2 + block] = rows_ref[pl.ds(first, part_rows), :]
            attended = mm(low, weight_ref[...], NT).astype(jnp.bfloat16)
            for group in range(groups):
                send_ref[seq * groups + group] = attended[:, group * width : (group + 1) * width]
            sums[0] += jnp.sum(total, axis=0, keepdims=True)
            sums[1] += jnp.sum(grad * normal, axis=0, keepdims=True)
            sums[2] += jnp.sum(grad, axis=0, keepdims=True)
    sums_ref[...] = jnp.zeros(sums_ref.shape, jnp.float32)
    for number, total in enumerate(sums):
        sums_ref[number : number + 1, :] = total


def hidden_grad_part(own, grad_sum, grad_other, cot_all, hidden, table, out_full, sizes):
    count, seq_rows, width, part_rows = sizes
    row_count, model_width = hidden.shape
    low = jnp.bfloat16
    shapes = (
        ((count, seq_rows, width), low),
        ((row_count, model_width), low),
        ((2 * row_count // seq_rows, part_rows, model_width), jnp.float32),
        ((8, model_width), jnp.float32),
    )
    arrays = (grad_sum, grad_other, cot_all, hidden, table, out_full)
    return pl.pallas_call(
        hidden_grad_kernel,
        grid=(1,),
        out_shape=tuple(jax.ShapeDtypeStruct(*shape) for shape in shapes),
        in_specs=[SMEM_SPEC] + [whole_block(array) for array in arrays],
        out_specs=tuple(whole_shape(shape) for shape, _ in shapes),
        scratch_shapes=[pltpu.VMEM((seq_rows, model_width), jnp.float32)],
        compiler_params=KERNEL_PARAMS,
        name="hidden_grad_part",
    )(own, *arrays)


def place_mixed(source_ref, target, width):
    count, seq_rows, total = source_ref.shape
    parts = total // width
    groups = target.shape[1] // total
    for index in range(count):
        seq, group = index // groups, index % groups
        for part in range(parts):
            low = (part * groups + group) * width
            target[seq * seq_rows : (seq + 1) * seq_rows, low : low + width] = source_ref[
                index, :, part * width : (part + 1) * width
            ]


def mix_grads_kernel(keys, own_ref, grad_ref, branch_ref, attended_ref, *refs):
    pieces, (mine_ref, other_ref, normed, attended) = refs[:-4], refs[-4:]
    own_core, own_ctx = own_ref[0] & 1, own_ref[1]
    place_mixed(attended_ref, attended, attended_ref.shape[2])
    half, shard, _ = mine_ref.shape
    width = grad_ref.shape[1]
    for (piece_keys, core_key), piece in zip(keys, pieces):
        part_rows = piece.shape[1]
        for place, key in enumerate(piece_keys):
            start = (own_ctx ^ key) * 2 * part_rows + (own_core ^ core_key) * part_rows
            normed[pl.ds(pl.multiple_of(start, part_rows), part_rows), :] = piece[place]
    for flipped, out_ref in enumerate((mine_ref, other_ref)):
        for index in range(half):
            owner = 2 * index + ((own_ctx & 1) ^ flipped)
            columns = pl.ds(pl.multiple_of(owner * shard, shard), shard)
            out_ref[index, :, 0:width] = mm(normed[:, columns], grad_ref[...], TN).astype(
                jnp.bfloat16
            )
            out_ref[index, :, width:] = mm(branch_ref[:, columns], attended[...], TN).astype(
                jnp.bfloat16
            )


def mix_grads(own, grad_qkv, grad_branch, attended, held):
    keys = [(offsets, core_key) for offsets, core_key, _ in held]
    pieces = [piece for _, _, piece in held]
    length, width = grad_qkv.shape
    row_count, model_width = grad_branch.shape
    count, seq_rows, _ = attended.shape
    out_width = attended.size // row_count
    shape = (count // 2, model_width // count, width + out_width)
    low = jnp.bfloat16
    arrays = (grad_qkv, grad_branch, attended, *pieces)
    return pl.pallas_call(
        lambda *refs: mix_grads_kernel(keys, *refs),
        grid=(1,),
        out_shape=(jax.ShapeDtypeStruct(shape, low),) * 2,
        in_specs=[SMEM_SPEC] + [whole_block(array) for array in arrays],
        out_specs=(whole_shape(shape),) * 2,
        scratch_shapes=[
            pltpu.VMEM((length, model_width), low),
            pltpu.VMEM((row_count, out_width), low),
        ],
        compiler_params=KERNEL_PARAMS,
        cost_estimate=pl.CostEstimate(
            flops=2 * model_width * (length * width + row_count * out_width),
            bytes_accessed=8 * 1024 * 1024,
            transcendentals=0,
        ),
        name="mix_grads",
    )(own, *arrays)


def mix_join_kernel(own_ref, mine_ref, came_ref, keep_ref, send_ref):
    own_ctx = own_ref[1]
    is_first = (own_ctx & 1) == 0
    own_bit = (own_ctx >> 1) & 1
    total, wide_total = mine_ref.shape[2], keep_ref.shape[2]
    width = (wide_total - total) // 3
    for flipped, out_ref in enumerate((keep_ref, send_ref)):
        for index in range(out_ref.shape[0]):
            source = 2 * index + (own_bit ^ flipped)
            mine, came = mine_ref[source], came_ref[source]
            first = jnp.where(is_first, mine, came)
            second = jnp.where(is_first, came, mine)
            for part in range(3):
                lanes = slice(part * width, (part + 1) * width)
                low = 2 * part * width
                out_ref[index, :, low : low + width] = first[:, lanes]
                out_ref[index, :, low + width : low + 2 * width] = second[:, lanes]
            out_ref[index, :, 6 * width :] = (
                mine[:, 3 * width :].astype(jnp.float32) + came[:, 3 * width :].astype(jnp.float32)
            ).astype(jnp.bfloat16)


def mix_join(own, mine, came, width):
    half, shard, total = mine.shape
    shape = (half // 2, shard, total + 3 * width)
    return pl.pallas_call(
        mix_join_kernel,
        grid=(1,),
        out_shape=(jax.ShapeDtypeStruct(shape, jnp.bfloat16),) * 2,
        in_specs=[SMEM_SPEC, whole_block(mine), whole_block(came)],
        out_specs=(whole_shape(shape),) * 2,
        compiler_params=KERNEL_PARAMS,
        name="mix_join",
    )(own, mine, came)


def first_grad_kernel(own_ref, mixed_ref, weight_ref, x_ref, mine_ref, other_ref, sums_ref, *refs):
    mixed, rows_ref = refs
    own_tp = own_ref[0]
    core = own_tp & 1
    count, seq_rows, total = mixed_ref.shape
    groups = mixed.shape[1] // total
    place_mixed(mixed_ref, mixed, total // 3)
    part_rows = mine_ref.shape[2]
    model_width = x_ref.shape[1]
    block_rows = seq_rows // 2
    sums = [jnp.zeros((1, model_width), jnp.float32) for _ in range(2)]
    for seq in range(count // groups):
        rows = slice(seq * seq_rows, (seq + 1) * seq_rows)
        partial = mm(mixed[rows, :], weight_ref[...], NT)
        rows_ref[...] = partial.astype(jnp.bfloat16)
        for block in range(2):
            for row in range(2):
                for flipped, out_ref in enumerate((mine_ref, other_ref)):
                    owner = 2 * row + (core ^ flipped)
                    first = pl.multiple_of(block * block_rows + owner * part_rows, part_rows)
                    out_ref[2 * seq + block, row] = rows_ref[pl.ds(first, part_rows), :]
        centered, scale = norm_parts(x_ref[rows, :].astype(jnp.float32))
        sums[0] += jnp.sum(partial * (centered * scale), axis=0, keepdims=True)
        sums[1] += jnp.sum(partial, axis=0, keepdims=True)
    sums_ref[...] = jnp.zeros(sums_ref.shape, jnp.float32)
    for number, value in enumerate(sums):
        sums_ref[number : number + 1, :] = value
    mixed_ref_sum = jnp.sum(mixed[...].astype(jnp.float32), axis=0, keepdims=True)
    sums_ref[2:3, 0 : mixed.shape[1]] = mixed_ref_sum


def first_grads(own, grad_mixed, mix_full, x_all, part_rows):
    count, seq_rows, total = grad_mixed.shape
    row_count, model_width = x_all.shape
    shape = (2 * row_count // seq_rows, 2, part_rows, model_width)
    low = jnp.bfloat16
    arrays = (grad_mixed, mix_full, x_all)
    return pl.pallas_call(
        first_grad_kernel,
        grid=(1,),
        out_shape=(
            jax.ShapeDtypeStruct(shape, low),
            jax.ShapeDtypeStruct(shape, low),
            jax.ShapeDtypeStruct((8, model_width), jnp.float32),
        ),
        in_specs=[SMEM_SPEC] + [whole_block(array) for array in arrays],
        out_specs=(whole_shape(shape), whole_shape(shape), whole_shape((8, model_width))),
        scratch_shapes=[
            pltpu.VMEM((row_count, mix_full.shape[1]), low),
            pltpu.VMEM((seq_rows, model_width), low),
        ],
        compiler_params=KERNEL_PARAMS,
        name="first_grads",
    )(own, *arrays)


def gelu_both(value):
    root = (2.0 / jnp.pi) ** 0.5
    square = value * value
    inner = jnp.tanh(root * value * (1.0 + 0.044715 * square))
    slope = 0.5 * (1.0 + inner) + 0.5 * value * (1.0 - inner * inner) * root * (
        1.0 + 3.0 * 0.044715 * square
    )
    return 0.5 * value * (1.0 + inner), slope


def feed_kernel(part_count, own_ref, sum_ref, other_ref, x_ref, table_ref, late_ref, *refs):
    cot_parts, refs = refs[:part_count], refs[part_count:]
    (
        hidden_ref,
        second_ref,
        activated_ref,
        grad_pre_ref,
        mine_ref,
        partner_ref,
        cot_ref,
        sums_ref,
    ) = refs
    own_tp = own_ref[0]
    core = own_tp & 1
    hidden_local = activated_ref.shape[1]
    blocks, part_rows, _ = cot_parts[0].shape
    for key, part in enumerate(cot_parts):
        for block in range(blocks):
            row = block * part_count * part_rows + (own_tp ^ key) * part_rows
            cot_ref[pl.ds(pl.multiple_of(row, part_rows), part_rows), :] = part[block]
    half_rows = sum_ref.shape[0]
    up_sum = jnp.zeros((1, hidden_local), jnp.float32)
    cot_sum = jnp.zeros((1, cot_ref.shape[1]), jnp.float32)
    for half, (branch_ref, out_ref) in enumerate(((sum_ref, mine_ref), (other_ref, partner_ref))):
        for chunk in range(half_rows // MLP_ROWS):
            inside = slice(chunk * MLP_ROWS, (chunk + 1) * MLP_ROWS)
            start = (core ^ half) * half_rows + chunk * MLP_ROWS
            rows = pl.ds(pl.multiple_of(start, MLP_ROWS), MLP_ROWS)
            hidden = (
                x_ref[rows, :].astype(jnp.float32)
                + branch_ref[inside, :].astype(jnp.float32)
                + table_ref[2:3, :]
            )
            hidden_ref[rows, :] = hidden
            centered, scale = norm_parts(hidden)
            second = (centered * scale * table_ref[3:4, :] + table_ref[4:5, :]).astype(jnp.bfloat16)
            second_ref[rows, :] = second
            activated, slope = gelu_both(mm(second, late_ref[:, 0:hidden_local], NN) + table_ref[6:7, :])
            activated_ref[rows, :] = activated.astype(jnp.bfloat16)
            cot = cot_ref[rows, :]
            grad_pre = (mm(cot, late_ref[:, hidden_local:], NN) * slope).astype(jnp.bfloat16)
            grad_pre_ref[rows, :] = grad_pre
            out_ref[inside, :] = mm(grad_pre, late_ref[:, 0:hidden_local], NT).astype(jnp.bfloat16)
            up_sum += jnp.sum(grad_pre.astype(jnp.float32), axis=0, keepdims=True)
            cot_sum += jnp.sum(cot.astype(jnp.float32), axis=0, keepdims=True)
    sums_ref[...] = jnp.zeros(sums_ref.shape, jnp.float32)
    sums_ref[0:1, 0:hidden_local] = up_sum
    sums_ref[1:2, 0 : cot_ref.shape[1]] = cot_sum


def feed_part(own, branch_sum, branch_other, x_all, table, late_all, cot_parts):
    row_count, model_width = x_all.shape
    hidden_local = late_all.shape[1] // 2
    low = jnp.bfloat16
    shapes = (
        ((row_count, model_width), jnp.float32),
        ((row_count, model_width), low),
        ((row_count, hidden_local), low),
        ((row_count, hidden_local), low),
        ((row_count // 2, model_width), low),
        ((row_count // 2, model_width), low),
        ((row_count, model_width), low),
        ((8, max(model_width, hidden_local)), jnp.float32),
    )
    arrays = (branch_sum, branch_other, x_all, table, late_all, *cot_parts)
    return pl.pallas_call(
        lambda *refs: feed_kernel(len(cot_parts), *refs),
        grid=(1,),
        out_shape=tuple(jax.ShapeDtypeStruct(*shape) for shape in shapes),
        in_specs=[SMEM_SPEC] + [whole_block(array) for array in arrays],
        out_specs=tuple(whole_shape(shape) for shape, _ in shapes),
        compiler_params=KERNEL_PARAMS,
        cost_estimate=pl.CostEstimate(
            flops=6 * row_count * model_width * hidden_local,
            bytes_accessed=16 * 1024 * 1024,
            transcendentals=row_count * hidden_local,
        ),
        name="feed_part",
    )(own, *arrays)


def spread_tp(part):
    return [part] + [swap(part, "tp", key) for key in (1, 2, 3)]


def add_halves(mine, other, beside=None):
    arrived = swap(other, "tp", 1)
    chip_sum = (mine.astype(jnp.float32) + arrived.astype(jnp.float32)).astype(jnp.bfloat16)
    arrived = swap(chip_sum, "tp", 2)
    if beside is not None:
        arrived, beside = together(arrived, beside)
    whole = (chip_sum.astype(jnp.float32) + arrived.astype(jnp.float32)).astype(jnp.bfloat16)
    return whole, swap(whole, "tp", 1), beside


def owner_first(partial, part_rows):
    core = lax.axis_index("tp") & 1
    parts = partial.astype(jnp.bfloat16).reshape(-1, 2, 2, part_rows, partial.shape[-1])
    mine = lax.dynamic_index_in_dim(parts, core, 2, keepdims=False)
    return mine, swap(lax.dynamic_index_in_dim(parts, 1 - core, 2, keepdims=False), "tp", 1)


def owner_second(mine, arrived):
    row = lax.axis_index("tp") >> 1
    chip_sum = mine.astype(jnp.float32) + arrived.astype(jnp.float32)
    mine = lax.dynamic_index_in_dim(chip_sum, row, 1, keepdims=False)
    other = lax.dynamic_index_in_dim(chip_sum, 1 - row, 1, keepdims=False)
    return mine, swap(other.astype(jnp.bfloat16), "tp", 2)


def add_rows_to_owner(partial, part_rows):
    mine, arrived = owner_second(*owner_first(partial, part_rows))
    return mine + arrived.astype(jnp.float32)


def exchange(pieces):
    return lax.all_to_all(pieces, "ctx", 0, 0, tiled=True)


def norm_parts(rows):
    row_mean = jnp.mean(rows, axis=-1, keepdims=True)
    centered = rows - row_mean
    variance = jnp.mean(centered * centered, axis=-1, keepdims=True)
    return centered, lax.rsqrt(variance + epsilon)


def norm_backward(normal, scale, gradient, gain):
    scaled = gradient * gain
    return scale * (
        scaled
        - jnp.mean(scaled, axis=-1, keepdims=True)
        - normal * jnp.mean(scaled * normal, axis=-1, keepdims=True)
    )


def fast_body(
    inputs,
    pairing,
    first_gain,
    first_shift,
    query_key_value_weight,
    mix_bias,
    output_projection_weight,
    out_bias,
    second_gain,
    second_shift,
    up_projection_weight,
    up_projection_bias,
    down_projection_weight,
    down_bias,
    cotangent,
):
    low = jnp.bfloat16
    wide = jnp.float32
    seq_count, _, _, part_rows, model_width = inputs.shape
    tp_count = lax.axis_size("tp")
    ctx_count = lax.axis_size("ctx")
    block_rows = part_rows * tp_count
    seq_rows = 2 * block_rows
    row_count = seq_count * seq_rows
    shard = model_width // ctx_count
    dim_local = query_key_value_weight.shape[2]
    hidden_local = up_projection_weight.shape[1]
    groups = ctx_count // seq_count
    width = dim_local // groups
    own_tp = lax.axis_index("tp")

    vectors = [
        first_gain[None],
        first_shift[None],
        out_bias[None],
        second_gain[None],
        second_shift[None],
        down_bias[None],
        up_projection_bias,
        jnp.concatenate([mix_bias[0], mix_bias[1]], axis=1),
    ]
    head, tail = pack(
        jnp.transpose(query_key_value_weight, (1, 0, 2)), output_projection_weight, vectors
    )
    bits = [1 << place for place in range(ctx_count.bit_length() - 1)]
    head_bits, tail_bits = bits[::-1], bits[:1] + bits[:0:-1]
    heads, tails = [((0,), head)], [((0,), tail)]
    row_parts = spread_tp(inputs.reshape(-1, part_rows, model_width))
    cot_part = cotangent.reshape(-1, part_rows, model_width)
    late_shard = pack_late(up_projection_weight, down_projection_weight)
    for step, (head_bit, tail_bit) in enumerate(zip(head_bits, tail_bits)):
        heads = list(spread_step(heads, "ctx", head_bit))
        tails = list(spread_step(tails, "ctx", tail_bit))
        arrivals = (heads[1][1], tails[1][1])
        if step == 0:
            arrivals, row_parts, cot_part = together(arrivals, row_parts, cot_part)
            cot_parts = spread_tp(cot_part)
        elif step == 1:
            arrivals, cot_parts = together(arrivals, cot_parts)
        else:
            arrivals, late_shard = together(arrivals, late_shard)
        heads[1], tails[1] = (heads[1][0], arrivals[0]), (tails[1][0], arrivals[1])
    late_all = lax.all_gather(late_shard, "ctx", axis=0, tiled=True)
    own = jnp.stack([own_tp, lax.axis_index("ctx")]).astype(jnp.int32)
    row_all, first_all, mix_full, out_full, table, projected = first_part(
        own, row_parts, heads, tails, seq_count, groups, 7, mix_bias.shape[2]
    )
    gain_one, bias_down = table[0], table[5]

    sequence = lax.axis_index("ctx") // groups
    pairs = lax.dynamic_index_in_dim(pairing, sequence, 0, keepdims=False)
    blocks = jnp.stack([pairs, 2 * ctx_count - 1 - pairs], axis=-1).reshape(-1)
    places = jnp.arange(2 * ctx_count, dtype=jnp.int32)
    slots = jnp.sum(
        jnp.where(blocks[None, :] == places[:, None], places[None, :], 0), axis=1
    ).astype(jnp.int32)
    qkv = exchange(projected).reshape(ctx_count * seq_rows, 3 * width)
    attended_heads, log_total = attend_forward(slots, qkv, block_rows)
    attended = exchange(attended_heads.reshape(ctx_count, seq_rows, width))
    attended, normed_seqs = together(attended, first_all.reshape(seq_count, 2, block_rows, -1))
    normed_seqs = lax.dynamic_index_in_dim(normed_seqs, own_tp & 1, 1, keepdims=False)
    held = []
    for key in range(0, ctx_count, groups):
        their_seq = (lax.axis_index("ctx") ^ key) // groups
        piece = lax.dynamic_index_in_dim(normed_seqs, their_seq, 0)
        held.append(((key,), swap(piece, "ctx", key) if key else piece))
    branch_sum, branch_other, _ = add_halves(*branch_part(own, attended, out_full))
    hidden, second_all, activated, grad_pre, mine, other, cot_all, early_sums = feed_part(
        own, branch_sum, branch_other, row_all, table, late_all, cot_parts
    )

    grad_pre, *pieces = together(grad_pre, *(piece for _, piece in held))
    held = [(keys, piece) for (keys, _), piece in zip(held, pieces)]
    feed_terms = feed_grads(second_all, grad_pre, cot_all, activated)
    feed_total = lax.psum_scatter(feed_terms, "ctx", scatter_dimension=0, tiled=True)
    held = list(spread_step(held, "ctx", 1))
    grad_sum, grad_other, last_piece = add_halves(mine, other, held[1][1])
    held[1] = (held[1][0], last_piece)
    offsets = held[0][0] + held[1][0]
    sent = jnp.concatenate([held[0][1], held[1][1]], axis=0)
    held = [(offsets, 0, sent), (offsets, 1, swap(sent, "tp", 1))]
    grad_attended, grad_branch, own_grad, hidden_sums = hidden_grad_part(
        own,
        grad_sum,
        grad_other,
        cot_all,
        hidden,
        table,
        out_full,
        (ctx_count, seq_rows, width, part_rows),
    )
    grad_attended, last_piece = together(grad_attended, held[1][2])
    held[1] = (offsets, 1, last_piece)
    grad_heads = exchange(grad_attended).reshape(ctx_count * seq_rows, width)
    grad_qkv = attend_backward(slots, qkv, grad_heads, log_total, block_rows)
    down_sum = add_rows_to_owner(mm(activated, late_all[:, hidden_local:], NT), part_rows)
    own_hidden = lax.dynamic_index_in_dim(
        hidden.reshape(-1, tp_count, part_rows, model_width), own_tp, 1, keepdims=False
    )
    result = (own_hidden + down_sum + bias_down).astype(low)

    mix_mine, mix_other = mix_grads(own, grad_qkv, grad_branch, attended, held)
    grad_mixed, mix_mine, mix_came = together(
        exchange(grad_qkv.reshape(ctx_count, seq_rows, 3 * width)),
        mix_mine,
        swap(mix_other, "ctx", 1),
    )
    mix_mine, mix_other = mix_join(own, mix_mine, mix_came, width)
    mix_came = swap(mix_other, "ctx", 2)
    grad_mixed, mix_mine = together(grad_mixed, mix_mine)
    mine, other, first_sums = first_grads(own, grad_mixed, mix_full, row_all, part_rows)
    gain_shift = first_sums[:2]
    mix_came, came, sums_came = together(
        mix_came, swap(other, "tp", 1), swap(gain_shift, "tp", 1)
    )
    mine, came = owner_second(mine, came)
    gain_shift = gain_shift + sums_came
    gain_shift = gain_shift + swap(gain_shift, "tp", 2)
    for bit in bits[2:]:
        terms = mix_mine.astype(wide) + mix_came.astype(wide)
        terms = terms.reshape((-1, 2) + terms.shape[1:])
        at = jnp.where(lax.axis_index("ctx") & bit != 0, 1, 0)
        mix_mine = lax.dynamic_index_in_dim(terms, at, 1, keepdims=False)
        mix_other = lax.dynamic_index_in_dim(terms, 1 - at, 1, keepdims=False).astype(low)
        mix_came = swap(mix_other, "ctx", bit)
    up_shard, down_shard = feed_finish(feed_total)
    grad_first = mine + came.astype(wide)
    own_rows = inputs.reshape(-1, part_rows, model_width).astype(wide)
    own_centered, own_scale = norm_parts(own_rows)
    grad_inputs = own_grad + norm_backward(
        own_centered * own_scale, own_scale, grad_first, gain_one
    )
    mix_came, up_shard, down_shard, grad_inputs = together(
        mix_came, up_shard, down_shard, grad_inputs
    )
    mix_shard_sum, out_shard_sum = mix_finish(mix_mine[0], mix_came[0], dim_local)

    def by_shard(vector):
        return vector.reshape(ctx_count, -1)

    small = jnp.concatenate(
        [
            by_shard(gain_shift[0]),
            by_shard(gain_shift[1]),
            by_shard(hidden_sums[0]),
            by_shard(hidden_sums[1]),
            by_shard(hidden_sums[2]),
            by_shard(early_sums[1, :model_width]),
            by_shard(early_sums[0, :hidden_local]),
            by_shard(first_sums[2, :dim_local]),
            by_shard(first_sums[2, 2 * dim_local : 3 * dim_local]),
        ],
        axis=1,
    )
    small = jnp.sum(exchange(small), axis=0)
    piece = 0
    sums = []
    for length in [shard] * 6 + [hidden_local // ctx_count] + [dim_local // ctx_count] * 2:
        sums.append(small[piece : piece + length])
        piece += length
    return (
        result.reshape(inputs.shape),
        grad_inputs.reshape(inputs.shape),
        sums[0],
        sums[1],
        jnp.transpose(mix_shard_sum, (1, 0, 2)),
        jnp.stack(sums[7:9])[:, None, :],
        out_shard_sum,
        sums[2],
        sums[3],
        sums[4],
        up_shard,
        sums[6][None, :],
        down_shard,
        sums[5],
    )


def fits_exchange(inputs, query_key_value_weight):
    ctx_count, tp_count = lax.axis_size("ctx"), lax.axis_size("tp")
    seq_count = inputs.shape[0]
    if tp_count != 4 or ctx_count % seq_count or ctx_count & (ctx_count - 1):
        return False
    dim_local = query_key_value_weight.shape[2]
    groups = ctx_count // seq_count
    length = ctx_count * 2 * tp_count * inputs.shape[3]
    shard = inputs.shape[4] // ctx_count
    if groups != 2 or seq_count < 2:
        return False
    return dim_local % (groups * LANES) == 0 and length <= 2048 and shard % LANES == 0


def body(inputs, pairing, first_gain, first_shift, query_key_value_weight, *others):
    chosen = fast_body if fits_exchange(inputs, query_key_value_weight) else general_body
    return chosen(inputs, pairing, first_gain, first_shift, query_key_value_weight, *others)


def solution(mesh):
    return jax.shard_map(
        body,
        mesh=mesh,
        in_specs=(
            P(None, "ctx", None, "tp", None),
            P(),
            P("ctx"),
            P("ctx"),
            P("ctx", None, "tp"),
            P(None, "tp", "ctx"),
            P("tp", "ctx"),
            P("ctx"),
            P("ctx"),
            P("ctx"),
            P("ctx", "tp"),
            P("tp", "ctx"),
            P("tp", "ctx"),
            P("ctx"),
            P(None, "ctx", None, "tp", None),
        ),
        out_specs=(
            P(None, "ctx", None, "tp", None),
            P(None, "ctx", None, "tp", None),
            P("ctx"),
            P("ctx"),
            P("ctx", None, "tp"),
            P(None, "tp", "ctx"),
            P("tp", "ctx"),
            P("ctx"),
            P("ctx"),
            P("ctx"),
            P("ctx", "tp"),
            P("tp", "ctx"),
            P("tp", "ctx"),
            P("ctx"),
        ),
        check_vma=False,
    )
```

profile of v0, /device:TPU:0, one launch (start us, length us, event | category | flops | bytes accessed | tf_op | source)
XLA Modules:
  0.0 330.1 jit_solution(253113752355731512)
XLA Ops:
  7.2 2.5 collective-permute-start.4
  13.5 2.8 collective-permute-start
  17.8 4.1 %collective-permute-done.1 = bf16[1,64,1024]{2,1,0:T(8,128)(2,1)S(1)} collective-permute-done((bf16[1,64,1024]{2,1,0:T(8,128)(2,1)}, bf16[1,64,1024]{2,1,0:T(8,128)(2,1)S(1)}, u32[]{:S(2)}, u32[]{:S(2)}) %collective-permute-start.1) | collective-permute-done | bytes 131104 | tf_op jit(solution)/shard_map/ppermute | solution.py:518
  21.9 2.8 collective-permute-done
  29.6 3.1 collective-permute-start.5
  34.6 8.0 %collective-permute-done.6 = bf16[2,64,1024]{2,1,0:T(8,128)(2,1)S(1)} collective-permute-done((bf16[2,64,1024]{2,1,0:T(8,128)(2,1)S(1)}, bf16[2,64,1024]{2,1,0:T(8,128)(2,1)S(1)}, u32[]{:S(2)}, u32[]{:S(2)}) %collective-permute-start.6) | collective-permute-done | bytes 262176 | tf_op jit(solution)/shard_map/ppermute | solution.py:518
  48.9 11.0 %collective-permute-done.11.refs_8_ = bf16[4,64,1024]{2,1,0:T(8,128)(2,1)S(1)} collective-permute-done((bf16[4,64,1024]{2,1,0:T(8,128)(2,1)S(1)}, bf16[4,64,1024]{2,1,0:T(8,128)(2,1)S(1)}, u32[]{:S(2)}, u32[]{:S(2)}) %collective-permute-start.11) | collective-permute-done | bytes 524320 | tf_op jit(solution)/shard_map/ppermute | solution.py:518
  62.2 5.1 %first_part.1 = (bf16[512,1024]{1,0:T(8,128)(2,1)}, bf16[512,1024]{1,0:T(8,128)(2,1)}, bf16[1024,768]{1,0:T(8,128)(2,1)}, bf16[256,1024]{1,0:T(8,128)(2,1)}, f32...) custom-call(s32[2]{0:T(128)} %pad_add_fusion.1.refs_0_.own_ref, bf16[8,16,1024]{2,1,0:T(8,128)(2,1)} %bitcast.95, ...), custom_call_target="tpu_custom_call" | custom-call | flops 805306368 | bytes 8388608 | tf_op jit(solution)/shard_map/first_part/pallas_call | solution.py:687
  67.3 4.9 %all-to-all-start = ((bf16[8,128,384]{2,1,0:T(8,128)(2,1)}), bf16[8,128,384]{2,1,0:T(8,128)(2,1)S(1)}, u32[]{:S(2)}, u32[]{:S(2)}) async-start(bf16[8,128,384]{2,1,0:T(8,128)(2,1)} %get-tuple-element.101), calls=%async_computation | async-start | bytes 1572864 | tf_op jit(solution)/shard_map/all_to_all | solution.py:1167
  73.7 33.8 %all-to-all-done = bf16[8,128,384]{2,1,0:T(8,128)(2,1)S(1)} async-done(((bf16[8,128,384]{2,1,0:T(8,128)(2,1)}), bf16[8,128,384]{2,1,0:T(8,128)(2,1)S(1)}, u32[]{:S(2)}, u32[]{:S(2)}) %all-to-all-start) | async-done | bytes 786464 | tf_op jit(solution)/shard_map/all_to_all | solution.py:1167
  108.4 6.6 %attend_forward.1 = (bf16[1024,128]{1,0:T(8,128)(2,1)}, f32[8,1024]{1,0:T(8,128)}) custom-call(s32[16]{0:T(128)} %select_reduce_fusion.refs_0_, bf16[1024,384]{1,0:T(8,128)(2,1)} %bitcast.101), custom_call_target="tpu_custom_call" | custom-call | flops 402653184 | bytes 1048576 | tf_op jit(solution)/shard_map/attend_forward/pallas_call | solution.py:474
  115.0 21.1 %all_to_all.29.attended_ref.refs_3_ = bf16[8,128,128]{2,1,0:T(8,128)(2,1)} all-to-all(bf16[8,128,128]{2,1,0:T(8,128)(2,1)} %bitcast.106), channel_id=1, replica_groups=mesh['ctx'=8,'tp'=4] {'ctx'}, dimensions={0} | all-to-all | bytes 524288 | tf_op jit(solution)/shard_map/all_to_all | solution.py:1167
  136.1 2.7 branch_part.1
  143.7 12.5 %collective-permute-done.13 = bf16[256,1024]{1,0:T(8,128)(2,1)S(1)} collective-permute-done((bf16[256,1024]{1,0:T(8,128)(2,1)S(1)}, bf16[256,1024]{1,0:T(8,128)(2,1)S(1)}, u32[]{:S(2)}, u32[]{:S(2)}) %collective-permute-start.13) | collective-permute-done | bytes 524320 | tf_op jit(solution)/shard_map/ppermute | solution.py:518
  157.8 3.3 %collective-permute-start.19 = (bf16[1,64,1024]{2,1,0:T(8,128)(2,1)S(1)}, bf16[1,64,1024]{2,1,0:T(8,128)(2,1)S(1)}, u32[]{:S(2)}, u32[]{:S(2)}) collective-permute-start(bf16[1,64,1024]{2,1,0:T(8,128)(2,1)S(1)} %get-tuple-element.226), channel_id=1, source_target_pairs={{0,8},{4,12},{8,0},{12,4},{16,24},{20,28},{24,16},{28,20},{1,9},{5... | collective-permute-start | bytes 393224 | tf_op jit(solution)/shard_map/ppermute | solution.py:518
  161.9 10.7 %feed_part.1 = (f32[512,1024]{1,0:T(8,128)}, bf16[512,1024]{1,0:T(8,128)(2,1)}, bf16[512,1024]{1,0:T(8,128)(2,1)}, bf16[512,1024]{1,0:T(8,128)(2,1)}, bf16[256,1...) custom-call(s32[2]{0:T(128)} %pad_add_fusion.1.refs_0_.own_ref, ...), custom_call_target="tpu_custom_call" | custom-call | flops 3221225472 | bytes 16777216 | tf_op jit(solution)/shard_map/feed_part/pallas_call | solution.py:1116
  172.6 6.4 %feed_grads.1 = bf16[1024,2048]{1,0:T(8,128)(2,1)} custom-call(bf16[512,1024]{1,0:T(8,128)(2,1)} %get-tuple-element.146.second_ref, bf16[512,1024]{1,0:T(8,128)(2,1)} %get-tuple-element.147.grad_pre_ref, bf16[512,1024]{1,0:T(8,128)(2,1)} %get-tuple-element.126.cot_ref, bf16[512,1024]{1,0:T(8,128)(2,1)} %get-tuple-element.116.activated_ref), custom_call_target="tpu_custom_call" | custom-call | flops 2147483648 | bytes 8388608 | tf_op jit(solution)/shard_map/feed_grads/pallas_call | solution.py:719
  183.7 16.4 %collective-permute-done.22 = bf16[4,64,1024]{2,1,0:T(8,128)(2,1)S(1)} collective-permute-done((bf16[4,64,1024]{2,1,0:T(8,128)(2,1)S(1)}, bf16[4,64,1024]{2,1,0:T(8,128)(2,1)S(1)}, u32[]{:S(2)}, u32[]{:S(2)}) %collective-permute-start.22) | collective-permute-done | bytes 524320 | tf_op jit(solution)/shard_map/ppermute | solution.py:518
  201.1 2.6 collective-permute-done.23.other_ref
  203.8 5.7 %hidden_grad_part.1 = (bf16[8,128,128]{2,1,0:T(8,128)(2,1)}, bf16[512,1024]{1,0:T(8,128)(2,1)}, f32[8,16,1024]{2,1,0:T(8,128)}, f32[8,1024]{1,0:T(8,128)}) custom-call(s32[2]{0:T(128)} %pad_add_fusion.1.refs_0_.own_ref, bf16[256,1024]{1,0:T(8,128)(2,1)} %copy-done.2, bf16[256,1024]{1,0:T(8,128)(2,1)} %collective-permute-done.23.other_ref, ...), custom_call_target="tpu_custom_call" | custom-call | tf_op jit(solution)/shard_map/hidden_grad_part/pallas_call | solution.py:871
  209.5 3.6 %all-to-all-start.2 = ((bf16[8,128,128]{2,1,0:T(8,128)(2,1)}), bf16[8,128,128]{2,1,0:T(8,128)(2,1)S(1)}, u32[]{:S(2)}, u32[]{:S(2)}) async-start(bf16[8,128,128]{2,1,0:T(8,128)(2,1)} %get-tuple-element.129), calls=%async_computation.2 | async-start | bytes 524288 | tf_op jit(solution)/shard_map/all_to_all | solution.py:1167
  213.1 3.2 fusion.2
  216.8 13.2 %all-to-all-done.2 = bf16[8,128,128]{2,1,0:T(8,128)(2,1)S(1)} async-done(((bf16[8,128,128]{2,1,0:T(8,128)(2,1)}), bf16[8,128,128]{2,1,0:T(8,128)(2,1)S(1)}, u32[]{:S(2)}, u32[]{:S(2)}) %all-to-all-start.2) | async-done | bytes 262176 | tf_op jit(solution)/shard_map/all_to_all | solution.py:1167
  230.7 7.0 %attend_backward.1.refs_1_ = bf16[1024,384]{1,0:T(8,128)(2,1)} custom-call(s32[16]{0:T(128)} %select_reduce_fusion.refs_0_, bf16[1024,384]{1,0:T(8,128)(2,1)} %bitcast.102, bf16[1024,128]{1,0:T(8,128)(2,1)} %bitcast.105, f32[8,1024]{1,0:T(8,128)} %get-tuple-element.130.refs_3_), custom_call_target="tpu_custom_call" | custom-call | flops 939524096 | bytes 1835008 | tf_op jit(solution)/shard_map/attend_backward/pallas_call | solution.py:496
  237.6 3.5 %all-to-all-start.3 = ((bf16[8,128,384]{2,1,0:T(8,128)(2,1)}), bf16[8,128,384]{2,1,0:T(8,128)(2,1)S(1)}, u32[]{:S(2)}, u32[]{:S(2)}) async-start(bf16[8,128,384]{2,1,0:T(8,128)(2,1)} %bitcast.98), calls=%async_computation.3 | async-start | bytes 1572864 | tf_op jit(solution)/shard_map/all_to_all | solution.py:1167
  241.4 4.9 %mix_grads.1 = (bf16[4,128,640]{2,1,0:T(8,128)(2,1)}, bf16[4,128,640]{2,1,0:T(8,128)(2,1)}) custom-call(s32[2]{0:T(128)} %pad_add_fusion.1.refs_0_.own_ref, bf16[1024,384]{1,0:T(8,128)(2,1)} %attend_backward.1.refs_1_, bf16[512,1024]{1,0:T(8,128)(2,1)} %get-tuple-element.131.refs_2_, bf16[8,128,128]{2,1,0:T(8,128)(2,1)} %all_to_all.29.attended_ref.refs_3_, ...), custom_call_target="tpu_custom_call" | custom-call | flops 1073741824 | bytes 8388608 | tf_op jit(solution)/shard_map/mix_grads/pallas_call | solution.py:929
  252.6 19.5 %collective-permute-done.25.came_ref = bf16[4,128,640]{2,1,0:T(8,128)(2,1)} collective-permute-done((bf16[4,128,640]{2,1,0:T(8,128)(2,1)}, bf16[4,128,640]{2,1,0:T(8,128)(2,1)}, u32[]{:S(2)}, u32[]{:S(2)}) %collective-permute-start.25) | collective-permute-done | bytes 655392 | tf_op jit(solution)/shard_map/ppermute | solution.py:518
  272.2 2.8 mix_join.1
  274.9 5.6 %first_grads.1 = (bf16[8,2,16,1024]{3,2,1,0:T(8,128)(2,1)}, bf16[8,2,16,1024]{3,2,1,0:T(8,128)(2,1)}, f32[8,1024]{1,0:T(8,128)}) custom-call(s32[2]{0:T(128)} %pad_add_fusion.1.refs_0_.own_ref, bf16[8,128,384]{2,1,0:T(8,128)(2,1)} %copy-done.1, bf16[1024,768]{1,0:T(8,128)(2,1)} %get-tuple-element.142.weight_ref, ...), custom_call_target="tpu_custom_call" | custom-call | tf_op jit(solution)/shard_map/first_grads/pallas_call | solution.py:1022
  285.8 9.4 %collective-permute-done.26 = bf16[2,128,1024]{2,1,0:T(8,128)(2,1)} collective-permute-done((bf16[2,128,1024]{2,1,0:T(8,128)(2,1)}, bf16[2,128,1024]{2,1,0:T(8,128)(2,1)}, u32[]{:S(2)}, u32[]{:S(2)}) %collective-permute-start.26) | collective-permute-done | bytes 524320 | tf_op jit(solution)/shard_map/ppermute | solution.py:518
  303.3 3.3 %all-to-all-start.4 = ((f32[8,1,960]{2,1,0:T(1,128)}), f32[8,1,960]{2,1,0:T(1,128)S(1)}, u32[]{:S(2)}, u32[]{:S(2)}) async-start(f32[8,1,960]{2,1,0:T(1,128)} %all_to_all.22), calls=%async_computation.5 | async-start | bytes 65536 | tf_op jit(solution)/shard_map/all_to_all | solution.py:1167
  307.2 8.7 %all-to-all-done.4 = f32[8,1,960]{2,1,0:T(1,128)S(1)} async-done(((f32[8,1,960]{2,1,0:T(1,128)}), f32[8,1,960]{2,1,0:T(1,128)S(1)}, u32[]{:S(2)}, u32[]{:S(2)}) %all-to-all-start.4) | async-done | bytes 30752 | tf_op jit(solution)/shard_map/all_to_all | solution.py:1167
  (175 shorter events, 64.7 us)
Async XLA Ops:
  7.2 153.9 %all-gather.2.cloned.1.call-start = ((), (), s32[]{:S(2)}) async-start(), calls=%async_computation.6 | async-start | bytes 4718592 | tf_op jit(solution)/shard_map/all_gather | solution.py:1249
  7.2 17.4 %collective-permute-start.4 = (bf16[8,16,1024]{2,1,0:T(8,128)(2,1)}, bf16[8,16,1024]{2,1,0:T(8,128)(2,1)S(1)}, u32[]{:S(2)}, u32[]{:S(2)}) collective-permute-start(bf16[8,16,1024]{2,1,0:T(8,128)(2,1)} %bitcast.92), channel_id=1, source_target_pairs={{0,3},{1,2},{2,1},{3,0},{4,7},{5,6},{6,5},{7,4},{8,11},{9,10},{10,... | collective-permute-start | bytes 786440 | tf_op jit(solution)/shard_map/ppermute | solution.py:518
  9.7 15.0 %collective-permute-start.3 = (bf16[8,16,1024]{2,1,0:T(8,128)(2,1)}, bf16[8,16,1024]{2,1,0:T(8,128)(2,1)S(1)}, u32[]{:S(2)}, u32[]{:S(2)}) collective-permute-start(bf16[8,16,1024]{2,1,0:T(8,128)(2,1)} %bitcast.93), channel_id=1, source_target_pairs={{0,2},{1,3},{2,0},{3,1},{4,6},{5,7},{6,4},{7,5},{8,10},{9,11},{10,... | collective-permute-start | bytes 786440 | tf_op jit(solution)/shard_map/ppermute | solution.py:518
  10.3 14.3 %collective-permute-start.2 = (bf16[8,16,1024]{2,1,0:T(8,128)(2,1)}, bf16[8,16,1024]{2,1,0:T(8,128)(2,1)S(1)}, u32[]{:S(2)}, u32[]{:S(2)}) collective-permute-start(bf16[8,16,1024]{2,1,0:T(8,128)(2,1)} %bitcast.94), channel_id=1, source_target_pairs={{0,1},{1,0},{2,3},{3,2},{4,5},{5,4},{6,7},{7,6},{8,9},{9,8},{10,11... | collective-permute-start | bytes 786440 | tf_op jit(solution)/shard_map/ppermute | solution.py:518
  13.5 11.2 %collective-permute-start = (bf16[1,80,1024]{2,1,0:T(8,128)(2,1)}, bf16[1,80,1024]{2,1,0:T(8,128)(2,1)S(1)}, u32[]{:S(2)}, u32[]{:S(2)}) collective-permute-start(bf16[1,80,1024]{2,1,0:T(8,128)(2,1)} %get-tuple-element.88), channel_id=1, source_target_pairs={{0,16},{4,20},{8,24},{12,28},{16,0},{20,4},{24,8},{28,12},{1,17},{... | collective-permute-start | bytes 491528 | tf_op jit(solution)/shard_map/ppermute | solution.py:518
  16.3 5.6 %collective-permute-start.1 = (bf16[1,64,1024]{2,1,0:T(8,128)(2,1)}, bf16[1,64,1024]{2,1,0:T(8,128)(2,1)S(1)}, u32[]{:S(2)}, u32[]{:S(2)}) collective-permute-start(bf16[1,64,1024]{2,1,0:T(8,128)(2,1)} %get-tuple-element.89), channel_id=1, source_target_pairs={{0,4},{4,0},{8,12},{12,8},{16,20},{20,16},{24,28},{28,24},{1,5},{5... | collective-permute-start | bytes 393224 | tf_op jit(solution)/shard_map/ppermute | solution.py:518
  24.7 17.9 %collective-permute-start.9 = (bf16[8,16,1024]{2,1,0:T(8,128)(2,1)}, bf16[8,16,1024]{2,1,0:T(8,128)(2,1)S(1)}, u32[]{:S(2)}, u32[]{:S(2)}) collective-permute-start(bf16[8,16,1024]{2,1,0:T(8,128)(2,1)} %bitcast.132), channel_id=1, source_target_pairs={{0,3},{1,2},{2,1},{3,0},{4,7},{5,6},{6,5},{7,4},{8,11},{9,10},{10,... | collective-permute-start | bytes 786440 | tf_op jit(solution)/shard_map/ppermute | solution.py:518
  25.0 17.5 %collective-permute-start.8 = (bf16[8,16,1024]{2,1,0:T(8,128)(2,1)}, bf16[8,16,1024]{2,1,0:T(8,128)(2,1)S(1)}, u32[]{:S(2)}, u32[]{:S(2)}) collective-permute-start(bf16[8,16,1024]{2,1,0:T(8,128)(2,1)} %bitcast.133), channel_id=1, source_target_pairs={{0,2},{1,3},{2,0},{3,1},{4,6},{5,7},{6,4},{7,5},{8,10},{9,11},{10,... | collective-permute-start | bytes 786440 | tf_op jit(solution)/shard_map/ppermute | solution.py:518
  26.2 16.4 %collective-permute-start.7 = (bf16[8,16,1024]{2,1,0:T(8,128)(2,1)}, bf16[8,16,1024]{2,1,0:T(8,128)(2,1)S(1)}, u32[]{:S(2)}, u32[]{:S(2)}) collective-permute-start(bf16[8,16,1024]{2,1,0:T(8,128)(2,1)} %bitcast.134), channel_id=1, source_target_pairs={{0,1},{1,0},{2,3},{3,2},{4,5},{5,4},{6,7},{7,6},{8,9},{9,8},{10,11... | collective-permute-start | bytes 786440 | tf_op jit(solution)/shard_map/ppermute | solution.py:518
  27.6 15.0 %collective-permute-start.6 = (bf16[2,64,1024]{2,1,0:T(8,128)(2,1)S(1)}, bf16[2,64,1024]{2,1,0:T(8,128)(2,1)S(1)}, u32[]{:S(2)}, u32[]{:S(2)}) collective-permute-start(bf16[2,64,1024]{2,1,0:T(8,128)(2,1)S(1)} %pad_maximum_fusion.2), channel_id=1, source_target_pairs={{0,16},{4,20},{8,24},{12,28},{16,0},{20,4},{24,8},{28,12},{1,17},{... | collective-permute-start | bytes 786440 | tf_op jit(solution)/shard_map/ppermute | solution.py:518
  29.6 15.4 %collective-permute-start.5 = (bf16[2,80,1024]{2,1,0:T(8,128)(2,1)S(1)}, bf16[2,80,1024]{2,1,0:T(8,128)(2,1)S(1)}, u32[]{:S(2)}, u32[]{:S(2)}) collective-permute-start(bf16[2,80,1024]{2,1,0:T(8,128)(2,1)S(1)} %pad_maximum_fusion.1), channel_id=1, source_target_pairs={{0,8},{4,12},{8,0},{12,4},{16,24},{20,28},{24,16},{28,20},{1,9},{5... | collective-permute-start | bytes 983048 | tf_op jit(solution)/shard_map/ppermute | solution.py:518
  45.1 16.2 %collective-permute-start.10 = (bf16[4,80,1024]{2,1,0:T(8,128)(2,1)S(1)}, bf16[4,80,1024]{2,1,0:T(8,128)(2,1)S(1)}, u32[]{:S(2)}, u32[]{:S(2)}) collective-permute-start(bf16[4,80,1024]{2,1,0:T(8,128)(2,1)S(1)} %constant_dynamic-update-slice_fusion.refs_5_), channel_id=1, source_target_pairs={{0,4},{4,0},{8,12},{12,8},{16,20},{20,16},{24,28},{28,24},{1,5},{5... | collective-permute-start | bytes 1966088 | tf_op jit(solution)/shard_map/ppermute | solution.py:518
  46.7 13.1 %collective-permute-start.11 = (bf16[4,64,1024]{2,1,0:T(8,128)(2,1)S(1)}, bf16[4,64,1024]{2,1,0:T(8,128)(2,1)S(1)}, u32[]{:S(2)}, u32[]{:S(2)}) collective-permute-start(bf16[4,64,1024]{2,1,0:T(8,128)(2,1)S(1)} %constant_dynamic-update-slice_fusion.3.refs_7_), channel_id=1, source_target_pairs={{0,8},{4,12},{8,0},{12,4},{16,24},{20,28},{24,16},{28,20},{1,9},{5... | collective-permute-start | bytes 1572872 | tf_op jit(solution)/shard_map/ppermute | solution.py:518
  67.3 40.2 %all-to-all-start = ((bf16[8,128,384]{2,1,0:T(8,128)(2,1)}), bf16[8,128,384]{2,1,0:T(8,128)(2,1)S(1)}, u32[]{:S(2)}, u32[]{:S(2)}) async-start(bf16[8,128,384]{2,1,0:T(8,128)(2,1)} %get-tuple-element.101), calls=%async_computation | async-start | bytes 1572864 | tf_op jit(solution)/shard_map/all_to_all | solution.py:1167
  72.2 246.3 %reduce-scatter.2.cloned.1.call-start = ((), (), s32[]{:S(2)}) async-start(), calls=%async_computation.7 | async-start | bytes 4718592 | tf_op jit(solution)/shard_map/reduce_scatter | solution.py:1281
  142.1 14.0 %collective-permute-start.13 = (bf16[256,1024]{1,0:T(8,128)(2,1)S(1)}, bf16[256,1024]{1,0:T(8,128)(2,1)S(1)}, u32[]{:S(2)}, u32[]{:S(2)}) collective-permute-start(bf16[256,1024]{1,0:T(8,128)(2,1)S(1)} %add_convert_fusion.3), channel_id=1, source_target_pairs={{0,2},{1,3},{2,0},{3,1},{4,6},{5,7},{6,4},{7,5},{8,10},{9,11},{10,... | collective-permute-start | bytes 1572872 | tf_op jit(solution)/shard_map/ppermute | solution.py:518
  156.6 15.9 %collective-permute-start.21 = (bf16[1,64,1024]{2,1,0:T(8,128)(2,1)S(1)}, bf16[1,64,1024]{2,1,0:T(8,128)(2,1)S(1)}, u32[]{:S(2)}, u32[]{:S(2)}) collective-permute-start(bf16[1,64,1024]{2,1,0:T(8,128)(2,1)S(1)} %get-tuple-element.224), channel_id=1, source_target_pairs={{0,24},{4,28},{8,16},{12,20},{16,8},{20,12},{24,0},{28,4},{1,25},{... | collective-permute-start | bytes 393224 | tf_op jit(solution)/shard_map/ppermute | solution.py:518
  157.8 14.8 %collective-permute-start.20 = (bf16[1,64,1024]{2,1,0:T(8,128)(2,1)S(1)}, bf16[1,64,1024]{2,1,0:T(8,128)(2,1)S(1)}, u32[]{:S(2)}, u32[]{:S(2)}) collective-permute-start(bf16[1,64,1024]{2,1,0:T(8,128)(2,1)S(1)} %get-tuple-element.225), channel_id=1, source_target_pairs={{0,16},{4,20},{8,24},{12,28},{16,0},{20,4},{24,8},{28,12},{1,17},{... | collective-permute-start | bytes 393224 | tf_op jit(solution)/shard_map/ppermute | solution.py:518
  157.8 14.8 %collective-permute-start.19 = (bf16[1,64,1024]{2,1,0:T(8,128)(2,1)S(1)}, bf16[1,64,1024]{2,1,0:T(8,128)(2,1)S(1)}, u32[]{:S(2)}, u32[]{:S(2)}) collective-permute-start(bf16[1,64,1024]{2,1,0:T(8,128)(2,1)S(1)} %get-tuple-element.226), channel_id=1, source_target_pairs={{0,8},{4,12},{8,0},{12,4},{16,24},{20,28},{24,16},{28,20},{1,9},{5... | collective-permute-start | bytes 393224 | tf_op jit(solution)/shard_map/ppermute | solution.py:518
  180.1 20.0 %collective-permute-start.22 = (bf16[4,64,1024]{2,1,0:T(8,128)(2,1)S(1)}, bf16[4,64,1024]{2,1,0:T(8,128)(2,1)S(1)}, u32[]{:S(2)}, u32[]{:S(2)}) collective-permute-start(bf16[4,64,1024]{2,1,0:T(8,128)(2,1)S(1)} %pad_maximum_fusion), channel_id=1, source_target_pairs={{0,4},{4,0},{8,12},{12,8},{16,20},{20,16},{24,28},{28,24},{1,5},{5... | collective-permute-start | bytes 1572872 | tf_op jit(solution)/shard_map/ppermute | solution.py:518
  182.1 18.0 %collective-permute-start.18 = (bf16[256,1024]{1,0:T(8,128)(2,1)S(1)}, bf16[256,1024]{1,0:T(8,128)(2,1)S(1)}, u32[]{:S(2)}, u32[]{:S(2)}) collective-permute-start(bf16[256,1024]{1,0:T(8,128)(2,1)S(1)} %add_convert_fusion.1), channel_id=1, source_target_pairs={{0,2},{1,3},{2,0},{3,1},{4,6},{5,7},{6,4},{7,5},{8,10},{9,11},{10,... | collective-permute-start | bytes 1572872 | tf_op jit(solution)/shard_map/ppermute | solution.py:518
  200.2 9.3 %collective-permute-start.24 = (bf16[8,64,1024]{2,1,0:T(8,128)(2,1)S(1)}, bf16[8,64,1024]{2,1,0:T(8,128)(2,1)S(1)}, u32[]{:S(2)}, u32[]{:S(2)}) collective-permute-start(bf16[8,64,1024]{2,1,0:T(8,128)(2,1)S(1)} %constant_dynamic-update-slice_fusion.6.refs_4_), channel_id=1, source_target_pairs={{0,1},{1,0},{2,3},{3,2},{4,5},{5,4},{6,7},{7,6},{8,9},{9,8},{10,11... | collective-permute-start | bytes 3145736 | tf_op jit(solution)/shard_map/ppermute | solution.py:518
  209.5 20.5 %all-to-all-start.2 = ((bf16[8,128,128]{2,1,0:T(8,128)(2,1)}), bf16[8,128,128]{2,1,0:T(8,128)(2,1)S(1)}, u32[]{:S(2)}, u32[]{:S(2)}) async-start(bf16[8,128,128]{2,1,0:T(8,128)(2,1)} %get-tuple-element.129), calls=%async_computation.2 | async-start | bytes 524288 | tf_op jit(solution)/shard_map/all_to_all | solution.py:1167
  216.4 31.8 %collective-permute-start.15 = (bf16[8,2,16,1024]{3,2,1,0:T(8,128)(2,1)S(1)}, bf16[8,2,16,1024]{3,2,1,0:T(8,128)(2,1)}, u32[]{:S(2)}, u32[]{:S(2)}) collective-permute-start(bf16[8,2,16,1024]{3,2,1,0:T(8,128)(2,1)S(1)} %dynamic-slice_bitcast_fusion.1), channel_id=1, source_target_pairs={{0,1},{1,0},{2,3},{3,2},{4,5},{5,4},{6,7},{7,6},{8,9},{9,8},{10,11... | collective-permute-start | bytes 1572872 | tf_op jit(solution)/shard_map/ppermute | solution.py:518
  237.6 34.6 %all-to-all-start.3 = ((bf16[8,128,384]{2,1,0:T(8,128)(2,1)}), bf16[8,128,384]{2,1,0:T(8,128)(2,1)S(1)}, u32[]{:S(2)}, u32[]{:S(2)}) async-start(bf16[8,128,384]{2,1,0:T(8,128)(2,1)} %bitcast.98), calls=%async_computation.3 | async-start | bytes 1572864 | tf_op jit(solution)/shard_map/all_to_all | solution.py:1167
  246.3 25.9 %collective-permute-start.25 = (bf16[4,128,640]{2,1,0:T(8,128)(2,1)}, bf16[4,128,640]{2,1,0:T(8,128)(2,1)}, u32[]{:S(2)}, u32[]{:S(2)}) collective-permute-start(bf16[4,128,640]{2,1,0:T(8,128)(2,1)} %get-tuple-element.134), channel_id=1, source_target_pairs={{0,4},{4,0},{8,12},{12,8},{16,20},{20,16},{24,28},{28,24},{1,5},{5... | collective-permute-start | bytes 1966088 | tf_op jit(solution)/shard_map/ppermute | solution.py:518
  249.5 31.6 %collective-permute-start.16 = (bf16[8,16,1024]{2,1,0:T(8,128)(2,1)S(1)}, bf16[8,16,1024]{2,1,0:T(8,128)(2,1)S(1)}, u32[]{:S(2)}, u32[]{:S(2)}) collective-permute-start(bf16[8,16,1024]{2,1,0:T(8,128)(2,1)S(1)} %fusion.11), channel_id=1, source_target_pairs={{0,2},{1,3},{2,0},{3,1},{4,6},{5,7},{6,4},{7,5},{8,10},{9,11},{10,... | collective-permute-start | bytes 786440 | tf_op jit(solution)/shard_map/ppermute | solution.py:518
  280.5 14.7 %collective-permute-start.26 = (bf16[2,128,1024]{2,1,0:T(8,128)(2,1)}, bf16[2,128,1024]{2,1,0:T(8,128)(2,1)}, u32[]{:S(2)}, u32[]{:S(2)}) collective-permute-start(bf16[2,128,1024]{2,1,0:T(8,128)(2,1)} %get-tuple-element.140), channel_id=1, source_target_pairs={{0,8},{4,12},{8,0},{12,4},{16,24},{20,28},{24,16},{28,20},{1,9},{5... | collective-permute-start | bytes 1572872 | tf_op jit(solution)/shard_map/ppermute | solution.py:518
  295.9 6.6 %collective-permute-start.31 = (f32[2,1024]{1,0:T(2,128)S(1)}, f32[2,1024]{1,0:T(2,128)S(1)}, u32[]{:S(2)}, u32[]{:S(2)}) collective-permute-start(f32[2,1024]{1,0:T(2,128)S(1)} %slice_add_fusion), channel_id=1, source_target_pairs={{0,2},{1,3},{2,0},{3,1},{4,6},{5,7},{6,4},{7,5},{8,10},{9,11},{10,... | collective-permute-start | bytes 24584 | tf_op jit(solution)/shard_map/ppermute | solution.py:518
  301.0 19.6 %collective-permute-start.29 = (bf16[1,128,1024]{2,1,0:T(8,128)(2,1)S(1)}, bf16[1,128,1024]{2,1,0:T(8,128)(2,1)S(1)}, u32[]{:S(2)}, u32[]{:S(2)}) collective-permute-start(bf16[1,128,1024]{2,1,0:T(8,128)(2,1)S(1)} %dynamic-slice_convert_fusion.1), channel_id=1, source_target_pairs={{0,16},{4,20},{8,24},{12,28},{16,0},{20,4},{24,8},{28,12},{1,17},{... | collective-permute-start | bytes 786440 | tf_op jit(solution)/shard_map/ppermute | solution.py:518
  303.3 12.6 %all-to-all-start.4 = ((f32[8,1,960]{2,1,0:T(1,128)}), f32[8,1,960]{2,1,0:T(1,128)S(1)}, u32[]{:S(2)}, u32[]{:S(2)}) async-start(f32[8,1,960]{2,1,0:T(1,128)} %all_to_all.22), calls=%async_computation.5 | async-start | bytes 65536 | tf_op jit(solution)/shard_map/all_to_all | solution.py:1167
  306.7 10.5 %collective-permute-start.30 = (bf16[8,16,1024]{2,1,0:T(8,128)(2,1)S(1)}, bf16[8,16,1024]{2,1,0:T(8,128)(2,1)S(1)}, u32[]{:S(2)}, u32[]{:S(2)}) collective-permute-start(bf16[8,16,1024]{2,1,0:T(8,128)(2,1)S(1)} %fusion.12), channel_id=1, source_target_pairs={{0,2},{1,3},{2,0},{3,1},{4,6},{5,7},{6,4},{7,5},{8,10},{9,11},{10,... | collective-permute-start | bytes 786440 | tf_op jit(solution)/shard_map/ppermute | solution.py:518
  (33 other events, 281.8 us)
Sparse Core Ops, SparseCore 0:
  61.5 93.2 all-gather.1
  179.1 105.6 reduce-scatter.1
where the time goes:
time: 332 us; the launch traced here: 330 us
  waiting for transfers between devices  149 us (45%)
  Pallas kernels  65.2 us (20%)
  starting transfers between devices  48.6 us (15%)
  blocking collectives  21.1 us (6%)
  other arithmetic  15 us (5%)
  between operations  14.7 us (4%)
  local copies, waits for them, and re-layouts  13.8 us (4%)
    ppermute x32, waiting for transfers between devices, swap(): return lax.ppermute(values, axis, [(i, i ^ bit) for i in range(count)])  92.8 us
    all_to_all x4, waiting for transfers between devices, exchange(): return lax.all_to_all(pieces, 'ctx', 0, 0, tiled=True)  55.7 us
    ppermute x32, starting transfers between devices, swap(): return lax.ppermute(values, axis, [(i, i ^ bit) for i in range(count)])  33.1 us
    all_to_all x1, blocking collectives, exchange(): return lax.all_to_all(pieces, 'ctx', 0, 0, tiled=True)  21.1 us
    all_to_all x4, starting transfers between devices, exchange(): return lax.all_to_all(pieces, 'ctx', 0, 0, tiled=True)  15.4 us
    pallas_call x1, Pallas kernels, feed_part(): pl.pallas_call(lambda *refs: feed_kernel(len(cot_parts), *refs), grid=(1,...  10.7 us
    pallas_call x1, Pallas kernels, attend_backward(): pl.pallas_call(lambda *refs: backward_kernel(block_rows, *refs), out_shap...  6.95 us
  transfers between devices with their start and end apart: 38, of which 17 were waited for; matrix products, arithmetic and copies ran while one was open for 8% of the time, Pallas kernels for 17%

commit v1 on v0

--- a/solution.py
+++ b/solution.py
@@ -752,25 +752,82 @@
     )(total)
 
 
-def mix_finish_kernel(mine_ref, came_ref, mix_ref, out_ref):
+def mix_finish_kernel(mine_ref, came_ref, out_mine_ref, out_came_ref, mix_ref, out_ref):
     total = mine_ref[...].astype(jnp.float32) + came_ref[...].astype(jnp.float32)
     parts, _, part_width = mix_ref.shape
     for part in range(parts):
         mix_ref[part] = total[:, part * part_width : (part + 1) * part_width]
-    out_ref[...] = total[:, parts * part_width :].T
-
-
-def mix_finish(mine, came, dim_local):
-    shapes = ((3, came.shape[0], dim_local), (dim_local, came.shape[0]))
+    out_ref[...] = (out_mine_ref[...].astype(jnp.float32) + out_came_ref[...].astype(jnp.float32)).T
+
+
+def mix_finish(mine, came, out_mine, out_came):
+    shard, dim_local = out_came.shape
+    shapes = ((3, shard, dim_local), (dim_local, shard))
+    arrays = (mine, came, out_mine, out_came)
     return pl.pallas_call(
         mix_finish_kernel,
         grid=(1,),
         out_shape=tuple(jax.ShapeDtypeStruct(shape, jnp.float32) for shape in shapes),
-        in_specs=[whole_block(mine), whole_block(came)],
+        in_specs=[whole_block(array) for array in arrays],
         out_specs=tuple(whole_shape(shape) for shape in shapes),
         compiler_params=KERNEL_PARAMS,
         name="mix_finish",
-    )(mine, came)
+    )(*arrays)
+
+
+def small_kernel(own_ref, first_ref, hidden_ref, early_ref, out_ref):
+    devices, _, shard = out_ref.shape
+    tp_count = 4
+    own_tp = own_ref[0]
+    share = 1.0 / tp_count
+    rows = [
+        first_ref[0:1, :],
+        first_ref[1:2, :],
+        hidden_ref[0:1, :] * share,
+        hidden_ref[1:2, :] * share,
+        hidden_ref[2:3, :] * share,
+        early_ref[1:2, :] * share,
+    ]
+    out_ref[...] = jnp.zeros(out_ref.shape, jnp.float32)
+    piece = shard // tp_count
+    count = devices // tp_count
+    for owner in range(count):
+        for place in range(tp_count):
+            index = owner * tp_count + place
+            for number, row in enumerate(rows):
+                out_ref[index, number : number + 1, :] = row[:, owner * shard : (owner + 1) * shard]
+            own = jnp.where(own_tp == place, 1.0, 0.0)
+            out_ref[index, len(rows) : len(rows) + 1, :] = (
+                early_ref[0:1, owner * shard : (owner + 1) * shard] * own
+            )
+            for number, part in enumerate((0, 2)):
+                low = part * count * piece + owner * piece
+                out_ref[
+                    index, len(rows) + 1 : len(rows) + 2, number * piece : (number + 1) * piece
+                ] = first_ref[2:3, low : low + piece] * own
+
+
+def small_pack(own, first_sums, hidden_sums, early_sums, count):
+    shape = (4 * count, 8, first_sums.shape[1] // count)
+    arrays = (first_sums, hidden_sums, early_sums)
+    return pl.pallas_call(
+        small_kernel,
+        grid=(1,),
+        out_shape=jax.ShapeDtypeStruct(shape, jnp.float32),
+        in_specs=[SMEM_SPEC] + [whole_block(array) for array in arrays],
+        out_specs=whole_shape(shape),
+        compiler_params=KERNEL_PARAMS,
+        name="small_pack",
+    )(own, *arrays)
+
+
+def halve(mine, came, bit):
+    terms = mine.astype(jnp.float32) + came.astype(jnp.float32)
+    terms = terms.reshape((-1, 2) + terms.shape[1:])
+    at = jnp.where(lax.axis_index("ctx") & bit != 0, 1, 0)
+    mine = lax.dynamic_index_in_dim(terms, at, 1, keepdims=False)
+    other = lax.dynamic_index_in_dim(terms, 1 - at, 1, keepdims=False)
+    return mine, swap(other.astype(jnp.bfloat16), "ctx", bit)
 
 
 MLP_ROWS = 128
@@ -893,12 +950,44 @@
             ]
 
 
-def mix_grads_kernel(keys, own_ref, grad_ref, branch_ref, attended_ref, *refs):
-    pieces, (mine_ref, other_ref, normed, attended) = refs[:-4], refs[-4:]
+def halved_grads_kernel(own_ref, left_ref, right_ref, mine_ref, other_ref, *placed):
+    if placed:
+        place_mixed(right_ref, placed[0], right_ref.shape[2])
+        right_ref = placed[0]
+    half, shard, _ = mine_ref.shape
+    for flipped, out_ref in ((1, other_ref), (0, mine_ref)):
+        for index in range(half):
+            owner = 2 * index + ((own_ref[1] & 1) ^ flipped)
+            columns = pl.ds(pl.multiple_of(owner * shard, shard), shard)
+            out_ref[index] = mm(left_ref[:, columns], right_ref[...], TN).astype(jnp.bfloat16)
+
+
+def halved_grads(own, left, right, count):
+    row_count, model_width = left.shape
+    width = right.size // row_count
+    shape = (count // 2, model_width // count, width)
+    placed = [pltpu.VMEM((row_count, width), jnp.bfloat16)] if len(right.shape) == 3 else []
+    return pl.pallas_call(
+        halved_grads_kernel,
+        grid=(1,),
+        out_shape=(jax.ShapeDtypeStruct(shape, jnp.bfloat16),) * 2,
+        in_specs=[SMEM_SPEC, whole_block(left), whole_block(right)],
+        out_specs=(whole_shape(shape),) * 2,
+        scratch_shapes=placed,
+        compiler_params=KERNEL_PARAMS,
+        cost_estimate=pl.CostEstimate(
+            flops=2 * model_width * row_count * width,
+            bytes_accessed=2 * (left.size + right.size + model_width * width),
+            transcendentals=0,
+        ),
+        name="halved_grads",
+    )(own, left, right)
+
+
+def mix_grads_kernel(keys, own_ref, grad_ref, *refs):
+    pieces, (mine_ref, other_ref, normed) = refs[:-3], refs[-3:]
     own_core, own_ctx = own_ref[0] & 1, own_ref[1]
-    place_mixed(attended_ref, attended, attended_ref.shape[2])
     half, shard, _ = mine_ref.shape
-    width = grad_ref.shape[1]
     for (piece_keys, core_key), piece in zip(keys, pieces):
         part_rows = piece.shape[1]
         for place, key in enumerate(piece_keys):
@@ -908,37 +997,27 @@
         for index in range(half):
             owner = 2 * index + ((own_ctx & 1) ^ flipped)
             columns = pl.ds(pl.multiple_of(owner * shard, shard), shard)
-            out_ref[index, :, 0:width] = mm(normed[:, columns], grad_ref[...], TN).astype(
-                jnp.bfloat16
-            )
-            out_ref[index, :, width:] = mm(branch_ref[:, columns], attended[...], TN).astype(
-                jnp.bfloat16
-            )
-
-
-def mix_grads(own, grad_qkv, grad_branch, attended, held):
+            out_ref[index] = mm(normed[:, columns], grad_ref[...], TN).astype(jnp.bfloat16)
+
+
+def mix_grads(own, grad_qkv, count, held):
     keys = [(offsets, core_key) for offsets, core_key, _ in held]
     pieces = [piece for _, _, piece in held]
     length, width = grad_qkv.shape
-    row_count, model_width = grad_branch.shape
-    count, seq_rows, _ = attended.shape
-    out_width = attended.size // row_count
-    shape = (count // 2, model_width // count, width + out_width)
+    model_width = pieces[0].shape[2]
+    shape = (count // 2, model_width // count, width)
     low = jnp.bfloat16
-    arrays = (grad_qkv, grad_branch, attended, *pieces)
+    arrays = (grad_qkv, *pieces)
     return pl.pallas_call(
         lambda *refs: mix_grads_kernel(keys, *refs),
         grid=(1,),
         out_shape=(jax.ShapeDtypeStruct(shape, low),) * 2,
         in_specs=[SMEM_SPEC] + [whole_block(array) for array in arrays],
         out_specs=(whole_shape(shape),) * 2,
-        scratch_shapes=[
-            pltpu.VMEM((length, model_width), low),
-            pltpu.VMEM((row_count, out_width), low),
-        ],
+        scratch_shapes=[pltpu.VMEM((length, model_width), low)],
         compiler_params=KERNEL_PARAMS,
         cost_estimate=pl.CostEstimate(
-            flops=2 * model_width * (length * width + row_count * out_width),
+            flops=2 * model_width * length * width,
             bytes_accessed=8 * 1024 * 1024,
             transcendentals=0,
         ),
@@ -950,8 +1029,7 @@
     own_ctx = own_ref[1]
     is_first = (own_ctx & 1) == 0
     own_bit = (own_ctx >> 1) & 1
-    total, wide_total = mine_ref.shape[2], keep_ref.shape[2]
-    width = (wide_total - total) // 3
+    width = mine_ref.shape[2] // 3
     for flipped, out_ref in enumerate((keep_ref, send_ref)):
         for index in range(out_ref.shape[0]):
             source = 2 * index + (own_bit ^ flipped)
@@ -963,14 +1041,11 @@
                 low = 2 * part * width
                 out_ref[index, :, low : low + width] = first[:, lanes]
                 out_ref[index, :, low + width : low + 2 * width] = second[:, lanes]
-            out_ref[index, :, 6 * width :] = (
-                mine[:, 3 * width :].astype(jnp.float32) + came[:, 3 * width :].astype(jnp.float32)
-            ).astype(jnp.bfloat16)
-
-
-def mix_join(own, mine, came, width):
+
+
+def mix_join(own, mine, came):
     half, shard, total = mine.shape
-    shape = (half // 2, shard, total + 3 * width)
+    shape = (half // 2, shard, 2 * total)
     return pl.pallas_call(
         mix_join_kernel,
         grid=(1,),
@@ -1297,80 +1372,62 @@
     )
     grad_attended, last_piece = together(grad_attended, held[1][2])
     held[1] = (offsets, 1, last_piece)
-    grad_heads = exchange(grad_attended).reshape(ctx_count * seq_rows, width)
+    out_mine, out_other = halved_grads(own, grad_branch, attended, ctx_count)
+    grad_heads, out_came = together(exchange(grad_attended), swap(out_other, "ctx", 1))
+    out_mine, out_came = halve(out_mine, out_came, 2)
+    grad_heads = grad_heads.reshape(ctx_count * seq_rows, width)
     grad_qkv = attend_backward(slots, qkv, grad_heads, log_total, block_rows)
+    grad_qkv, out_came = together(grad_qkv, out_came)
+    for bit in bits[2:]:
+        out_mine, out_came = halve(out_mine, out_came, bit)
     down_sum = add_rows_to_owner(mm(activated, late_all[:, hidden_local:], NT), part_rows)
     own_hidden = lax.dynamic_index_in_dim(
         hidden.reshape(-1, tp_count, part_rows, model_width), own_tp, 1, keepdims=False
     )
     result = (own_hidden + down_sum + bias_down).astype(low)
 
-    mix_mine, mix_other = mix_grads(own, grad_qkv, grad_branch, attended, held)
-    grad_mixed, mix_mine, mix_came = together(
+    mix_mine, mix_other = mix_grads(own, grad_qkv, ctx_count, held)
+    grad_mixed, mix_mine, mix_came, out_came, result = together(
         exchange(grad_qkv.reshape(ctx_count, seq_rows, 3 * width)),
         mix_mine,
         swap(mix_other, "ctx", 1),
-    )
-    mix_mine, mix_other = mix_join(own, mix_mine, mix_came, width)
+        out_came,
+        result,
+    )
+    mix_mine, mix_other = mix_join(own, mix_mine, mix_came)
     mix_came = swap(mix_other, "ctx", 2)
     grad_mixed, mix_mine = together(grad_mixed, mix_mine)
     mine, other, first_sums = first_grads(own, grad_mixed, mix_full, row_all, part_rows)
-    gain_shift = first_sums[:2]
-    mix_came, came, sums_came = together(
-        mix_came, swap(other, "tp", 1), swap(gain_shift, "tp", 1)
-    )
+    small = lax.all_to_all(
+        small_pack(own, first_sums, hidden_sums, early_sums, ctx_count),
+        ("ctx", "tp"),
+        0,
+        0,
+        tiled=True,
+    )
+    mix_came, came = together(mix_came, swap(other, "tp", 1))
     mine, came = owner_second(mine, came)
-    gain_shift = gain_shift + sums_came
-    gain_shift = gain_shift + swap(gain_shift, "tp", 2)
     for bit in bits[2:]:
-        terms = mix_mine.astype(wide) + mix_came.astype(wide)
-        terms = terms.reshape((-1, 2) + terms.shape[1:])
-        at = jnp.where(lax.axis_index("ctx") & bit != 0, 1, 0)
-        mix_mine = lax.dynamic_index_in_dim(terms, at, 1, keepdims=False)
-        mix_other = lax.dynamic_index_in_dim(terms, 1 - at, 1, keepdims=False).astype(low)
-        mix_came = swap(mix_other, "ctx", bit)
+        mix_mine, mix_came = halve(mix_mine, mix_came, bit)
     up_shard, down_shard = feed_finish(feed_total)
+    came, up_shard, down_shard = together(came, up_shard, down_shard)
     grad_first = mine + came.astype(wide)
     own_rows = inputs.reshape(-1, part_rows, model_width).astype(wide)
     own_centered, own_scale = norm_parts(own_rows)
     grad_inputs = own_grad + norm_backward(
         own_centered * own_scale, own_scale, grad_first, gain_one
     )
-    mix_came, up_shard, down_shard, grad_inputs = together(
-        mix_came, up_shard, down_shard, grad_inputs
-    )
-    mix_shard_sum, out_shard_sum = mix_finish(mix_mine[0], mix_came[0], dim_local)
-
-    def by_shard(vector):
-        return vector.reshape(ctx_count, -1)
-
-    small = jnp.concatenate(
-        [
-            by_shard(gain_shift[0]),
-            by_shard(gain_shift[1]),
-            by_shard(hidden_sums[0]),
-            by_shard(hidden_sums[1]),
-            by_shard(hidden_sums[2]),
-            by_shard(early_sums[1, :model_width]),
-            by_shard(early_sums[0, :hidden_local]),
-            by_shard(first_sums[2, :dim_local]),
-            by_shard(first_sums[2, 2 * dim_local : 3 * dim_local]),
-        ],
-        axis=1,
-    )
-    small = jnp.sum(exchange(small), axis=0)
-    piece = 0
-    sums = []
-    for length in [shard] * 6 + [hidden_local // ctx_count] + [dim_local // ctx_count] * 2:
-        sums.append(small[piece : piece + length])
-        piece += length
+    mix_came, grad_inputs, small = together(mix_came, grad_inputs, small)
+    mix_shard_sum, out_shard_sum = mix_finish(mix_mine[0], mix_came[0], out_mine[0], out_came[0])
+    sums = jnp.sum(small, axis=0)
+    piece = dim_local // ctx_count
     return (
         result.reshape(inputs.shape),
         grad_inputs.reshape(inputs.shape),
         sums[0],
         sums[1],
         jnp.transpose(mix_shard_sum, (1, 0, 2)),
-        jnp.stack(sums[7:9])[:, None, :],
+        jnp.stack([sums[7, :piece], sums[7, piece : 2 * piece]])[:, None, :],
         out_shard_sum,
         sums[2],
         sums[3],
@@ -1382,7 +1439,7 @@
     )
 
 
-def fits_exchange(inputs, query_key_value_weight):
+def fits_exchange(inputs, query_key_value_weight, up_projection_weight):
     ctx_count, tp_count = lax.axis_size("ctx"), lax.axis_size("tp")
     seq_count = inputs.shape[0]
     if tp_count != 4 or ctx_count % seq_count or ctx_count & (ctx_count - 1):
@@ -1391,13 +1448,16 @@
     groups = ctx_count // seq_count
     length = ctx_count * 2 * tp_count * inputs.shape[3]
     shard = inputs.shape[4] // ctx_count
-    if groups != 2 or seq_count < 2:
+    if groups != 2 or seq_count < 2 or dim_local * 4 != inputs.shape[4]:
+        return False
+    if up_projection_weight.shape[1] != inputs.shape[4]:
         return False
     return dim_local % (groups * LANES) == 0 and length <= 2048 and shard % LANES == 0
 
 
 def body(inputs, pairing, first_gain, first_shift, query_key_value_weight, *others):
-    chosen = fast_body if fits_exchange(inputs, query_key_value_weight) else general_body
+    fits = fits_exchange(inputs, query_key_value_weight, others[5])
+    chosen = fast_body if fits else general_body
     return chosen(inputs, pairing, first_gain, first_shift, query_key_value_weight, *others)
 
 

time: 332 us -> 326 us (0.982)
  waiting for transfers between devices: 149 us -> 136 us
  starting transfers between devices: 48.6 us -> 52.1 us
    all_to_all x4 -> x3, waiting for transfers between devices: 55.7 us -> 42.3 us  [exchange(): return lax.all_to_all(pieces, 'ctx', 0, 0, tiled=True)]
    all_to_all x0 -> x1, starting transfers between devices: none -> 5.59 us  [fast_body(): lax.all_to_all(small_pack(own, first_sums, hidden_sums, early_sums, ctx_c...]
    unnamed x62 -> x72, local copies, waits for them, and re-layouts: 6.21 us -> 11.3 us
    pallas_call x0 -> x2, Pallas kernels: none -> 4.14 us  [the longest x1 2.56 us: halved_grads(): pl.pallas_call(halved_grads_kernel, grid=(1,), out_shape=(jax.ShapeDtypeS...]
    slice x6 -> x1, local copies, waits for them, and re-layouts: 3.76 us -> 0.07 us  [fast_body(): sums[7, :piece]]
    all_to_all x4 -> x3, starting transfers between devices: 15.4 us -> 12.1 us  [exchange(): return lax.all_to_all(pieces, 'ctx', 0, 0, tiled=True)]
    ppermute x32 -> x33, starting transfers between devices: 33.1 us -> 34.4 us  [swap(): return lax.ppermute(values, axis, [(i, i ^ bit) for i in range(count)])]
    ppermute x32 -> x33, waiting for transfers between devices: 92.8 us -> 94 us  [swap(): return lax.ppermute(values, axis, [(i, i ^ bit) for i in range(count)])]
  transfers between devices with their start and end apart: 38 -> 39, of which waited for: 17 -> 17; matrix products, arithmetic and copies ran while one was open for 8% -> 7% of each run, Pallas kernels for 17% -> 18%
where the time goes in v1:
time: 326 us; the launch traced here: 325 us
  waiting for transfers between devices  136 us (42%)
  Pallas kernels  68.2 us (21%)
  starting transfers between devices  52.1 us (16%)
  blocking collectives  21.1 us (6%)
  local copies, waits for them, and re-layouts  16.3 us (5%)
  between operations  14.7 us (5%)
  other arithmetic  13 us (4%)
    ppermute x33, waiting for transfers between devices, swap(): return lax.ppermute(values, axis, [(i, i ^ bit) for i in range(count)])  94 us
    all_to_all x3, waiting for transfers between devices, exchange(): return lax.all_to_all(pieces, 'ctx', 0, 0, tiled=True)  42.3 us
    ppermute x33, starting transfers between devices, swap(): return lax.ppermute(values, axis, [(i, i ^ bit) for i in range(count)])  34.4 us
    all_to_all x1, blocking collectives, exchange(): return lax.all_to_all(pieces, 'ctx', 0, 0, tiled=True)  21.1 us
    all_to_all x3, starting transfers between devices, exchange(): return lax.all_to_all(pieces, 'ctx', 0, 0, tiled=True)  12.1 us
    unnamed x72, local copies, waits for them, and re-layouts  11.3 us
    pallas_call x1, Pallas kernels, feed_part(): pl.pallas_call(lambda *refs: feed_kernel(len(cot_parts), *refs), grid=(1,...  10.7 us
    pallas_call x1, Pallas kernels, attend_backward(): pl.pallas_call(lambda *refs: backward_kernel(block_rows, *refs), out_shap...  6.96 us
  transfers between devices with their start and end apart: 39, of which 17 were waited for; matrix products, arithmetic and copies ran while one was open for 7% of the time, Pallas kernels for 18%

profile of v1, /device:TPU:0, one launch (start us, length us, event | category | flops | bytes accessed | tf_op | source)
XLA Modules:
  0.0 324.7 jit_solution(16750134649920636377)
XLA Ops:
  13.5 2.8 collective-permute-start
  17.8 4.1 %collective-permute-done.1 = bf16[1,64,1024]{2,1,0:T(8,128)(2,1)S(1)} collective-permute-done((bf16[1,64,1024]{2,1,0:T(8,128)(2,1)}, bf16[1,64,1024]{2,1,0:T(8,128)(2,1)S(1)}, u32[]{:S(2)}, u32[]{:S(2)}) %collective-permute-start.1) | collective-permute-done | bytes 131104 | tf_op jit(solution)/shard_map/ppermute | solution.py:518
  21.9 2.8 collective-permute-done
  29.6 3.1 collective-permute-start.5
  34.6 8.0 %collective-permute-done.6 = bf16[2,64,1024]{2,1,0:T(8,128)(2,1)S(1)} collective-permute-done((bf16[2,64,1024]{2,1,0:T(8,128)(2,1)S(1)}, bf16[2,64,1024]{2,1,0:T(8,128)(2,1)S(1)}, u32[]{:S(2)}, u32[]{:S(2)}) %collective-permute-start.6) | collective-permute-done | bytes 262176 | tf_op jit(solution)/shard_map/ppermute | solution.py:518
  48.9 11.0 %collective-permute-done.11.refs_8_ = bf16[4,64,1024]{2,1,0:T(8,128)(2,1)S(1)} collective-permute-done((bf16[4,64,1024]{2,1,0:T(8,128)(2,1)S(1)}, bf16[4,64,1024]{2,1,0:T(8,128)(2,1)S(1)}, u32[]{:S(2)}, u32[]{:S(2)}) %collective-permute-start.11) | collective-permute-done | bytes 524320 | tf_op jit(solution)/shard_map/ppermute | solution.py:518
  62.2 5.1 %first_part.1 = (bf16[512,1024]{1,0:T(8,128)(2,1)}, bf16[512,1024]{1,0:T(8,128)(2,1)}, bf16[1024,768]{1,0:T(8,128)(2,1)}, bf16[256,1024]{1,0:T(8,128)(2,1)}, f32...) custom-call(s32[2]{0:T(128)} %pad_add_fusion.1.refs_0_.own_ref, bf16[8,16,1024]{2,1,0:T(8,128)(2,1)} %bitcast.106, ...), custom_call_target="tpu_custom_call" | custom-call | flops 805306368 | bytes 8388608 | tf_op jit(solution)/shard_map/first_part/pallas_call | solution.py:687
  67.4 4.9 %all-to-all-start = ((bf16[8,128,384]{2,1,0:T(8,128)(2,1)}), bf16[8,128,384]{2,1,0:T(8,128)(2,1)S(1)}, u32[]{:S(2)}, u32[]{:S(2)}) async-start(bf16[8,128,384]{2,1,0:T(8,128)(2,1)} %get-tuple-element.110), calls=%async_computation | async-start | bytes 1572864 | tf_op jit(solution)/shard_map/all_to_all | solution.py:1242
  73.8 33.7 %all-to-all-done = bf16[8,128,384]{2,1,0:T(8,128)(2,1)S(1)} async-done(((bf16[8,128,384]{2,1,0:T(8,128)(2,1)}), bf16[8,128,384]{2,1,0:T(8,128)(2,1)S(1)}, u32[]{:S(2)}, u32[]{:S(2)}) %all-to-all-start) | async-done | bytes 786464 | tf_op jit(solution)/shard_map/all_to_all | solution.py:1242
  108.4 6.6 %attend_forward.1 = (bf16[1024,128]{1,0:T(8,128)(2,1)}, f32[8,1024]{1,0:T(8,128)}) custom-call(s32[16]{0:T(128)} %select_reduce_fusion.refs_0_, bf16[1024,384]{1,0:T(8,128)(2,1)} %bitcast.113), custom_call_target="tpu_custom_call" | custom-call | flops 402653184 | bytes 1048576 | tf_op jit(solution)/shard_map/attend_forward/pallas_call | solution.py:474
  115.0 21.1 %all_to_all.25.attended_ref.right_ref = bf16[8,128,128]{2,1,0:T(8,128)(2,1)} all-to-all(bf16[8,128,128]{2,1,0:T(8,128)(2,1)} %bitcast.118), channel_id=1, replica_groups=mesh['ctx'=8,'tp'=4] {'ctx'}, dimensions={0} | all-to-all | bytes 524288 | tf_op jit(solution)/shard_map/all_to_all | solution.py:1242
  136.1 2.7 branch_part.1
  143.7 12.5 %collective-permute-done.13 = bf16[256,1024]{1,0:T(8,128)(2,1)S(1)} collective-permute-done((bf16[256,1024]{1,0:T(8,128)(2,1)S(1)}, bf16[256,1024]{1,0:T(8,128)(2,1)S(1)}, u32[]{:S(2)}, u32[]{:S(2)}) %collective-permute-start.13) | collective-permute-done | bytes 524320 | tf_op jit(solution)/shard_map/ppermute | solution.py:518
  157.7 3.3 %collective-permute-start.17 = (bf16[1,64,1024]{2,1,0:T(8,128)(2,1)S(1)}, bf16[1,64,1024]{2,1,0:T(8,128)(2,1)S(1)}, u32[]{:S(2)}, u32[]{:S(2)}) collective-permute-start(bf16[1,64,1024]{2,1,0:T(8,128)(2,1)S(1)} %get-tuple-element.228), channel_id=1, source_target_pairs={{0,8},{4,12},{8,0},{12,4},{16,24},{20,28},{24,16},{28,20},{1,9},{5... | collective-permute-start | bytes 393224 | tf_op jit(solution)/shard_map/ppermute | solution.py:518
  161.9 10.7 %feed_part.1 = (f32[512,1024]{1,0:T(8,128)}, bf16[512,1024]{1,0:T(8,128)(2,1)}, bf16[512,1024]{1,0:T(8,128)(2,1)}, bf16[512,1024]{1,0:T(8,128)(2,1)}, bf16[256,1...) custom-call(s32[2]{0:T(128)} %pad_add_fusion.1.refs_0_.own_ref, ...), custom_call_target="tpu_custom_call" | custom-call | flops 3221225472 | bytes 16777216 | tf_op jit(solution)/shard_map/feed_part/pallas_call | solution.py:1191
  172.6 6.5 %feed_grads.1 = bf16[1024,2048]{1,0:T(8,128)(2,1)} custom-call(bf16[512,1024]{1,0:T(8,128)(2,1)} %get-tuple-element.164.second_ref, bf16[512,1024]{1,0:T(8,128)(2,1)} %get-tuple-element.165.grad_pre_ref, bf16[512,1024]{1,0:T(8,128)(2,1)} %get-tuple-element.133.cot_ref, bf16[512,1024]{1,0:T(8,128)(2,1)} %get-tuple-element.149.activated_ref), custom_call_target="tpu_custom_call" | custom-call | flops 2147483648 | bytes 8388608 | tf_op jit(solution)/shard_map/feed_grads/pallas_call | solution.py:719
  186.5 13.8 %collective-permute-done.20 = bf16[4,64,1024]{2,1,0:T(8,128)(2,1)S(1)} collective-permute-done((bf16[4,64,1024]{2,1,0:T(8,128)(2,1)S(1)}, bf16[4,64,1024]{2,1,0:T(8,128)(2,1)S(1)}, u32[]{:S(2)}, u32[]{:S(2)}) %collective-permute-start.20) | collective-permute-done | bytes 524320 | tf_op jit(solution)/shard_map/ppermute | solution.py:518
  201.9 2.6 collective-permute-done.21.other_ref
  205.3 5.9 %hidden_grad_part.1 = (bf16[8,128,128]{2,1,0:T(8,128)(2,1)}, bf16[512,1024]{1,0:T(8,128)(2,1)}, f32[8,16,1024]{2,1,0:T(8,128)}, f32[8,1024]{1,0:T(8,128)}) custom-call(s32[2]{0:T(128)} %pad_add_fusion.1.refs_0_.own_ref, bf16[256,1024]{1,0:T(8,128)(2,1)} %copy-done.2, bf16[256,1024]{1,0:T(8,128)(2,1)} %copy-done.12, ...), custom_call_target="tpu_custom_call" | custom-call | tf_op jit(solution)/shard_map/hidden_grad_part/pallas_call | solution.py:928
  211.2 2.6 halved_grads.1
  215.2 3.6 %all-to-all-start.2 = ((bf16[8,128,128]{2,1,0:T(8,128)(2,1)}), bf16[8,128,128]{2,1,0:T(8,128)(2,1)S(1)}, u32[]{:S(2)}, u32[]{:S(2)}) async-start(bf16[8,128,128]{2,1,0:T(8,128)(2,1)} %get-tuple-element.137), calls=%async_computation.2 | async-start | bytes 524288 | tf_op jit(solution)/shard_map/all_to_all | solution.py:1242
  218.8 2.9 fusion.2
  222.9 8.5 %all-to-all-done.2 = bf16[8,128,128]{2,1,0:T(8,128)(2,1)S(1)} async-done(((bf16[8,128,128]{2,1,0:T(8,128)(2,1)}), bf16[8,128,128]{2,1,0:T(8,128)(2,1)S(1)}, u32[]{:S(2)}, u32[]{:S(2)}) %all-to-all-start.2) | async-done | bytes 262176 | tf_op jit(solution)/shard_map/all_to_all | solution.py:1242
  232.1 7.0 %attend_backward.1.refs_1_ = bf16[1024,384]{1,0:T(8,128)(2,1)} custom-call(s32[16]{0:T(128)} %select_reduce_fusion.refs_0_, bf16[1024,384]{1,0:T(8,128)(2,1)} %bitcast.114, bf16[1024,128]{1,0:T(8,128)(2,1)} %bitcast.117, f32[8,1024]{1,0:T(8,128)} %get-tuple-element.141.refs_3_), custom_call_target="tpu_custom_call" | custom-call | flops 939524096 | bytes 1835008 | tf_op jit(solution)/shard_map/attend_backward/pallas_call | solution.py:496
  239.7 3.5 %all-to-all-start.3 = ((bf16[8,128,384]{2,1,0:T(8,128)(2,1)}), bf16[8,128,384]{2,1,0:T(8,128)(2,1)S(1)}, u32[]{:S(2)}, u32[]{:S(2)}) async-start(bf16[8,128,384]{2,1,0:T(8,128)(2,1)} %bitcast.115), calls=%async_computation.3 | async-start | bytes 1572864 | tf_op jit(solution)/shard_map/all_to_all | solution.py:1242
  247.1 4.0 %mix_grads.1 = (bf16[4,128,384]{2,1,0:T(8,128)(2,1)}, bf16[4,128,384]{2,1,0:T(8,128)(2,1)}) custom-call(s32[2]{0:T(128)} %pad_add_fusion.1.refs_0_.own_ref, bf16[1024,384]{1,0:T(8,128)(2,1)} %attend_backward.1.refs_1_, bf16[8,64,1024]{2,1,0:T(8,128)(2,1)} %constant_dynamic-update-slice_fusion.6.refs_2_, bf16[8,64,1024]{2,1,0:T(8,128)(2,1)} %collective-permute-done.22.refs_3_), custom_call_target="tpu_custom_call" | custom-call | flops 805306368 | bytes 8388608 | tf_op jit(solution)/shard_map/mix_grads/pallas_call | solution.py:1011
  257.4 22.5 %collective-permute-done.26 = bf16[1,128,256]{2,1,0:T(8,128)(2,1)S(1)} collective-permute-done((bf16[1,128,256]{2,1,0:T(8,128)(2,1)S(1)}, bf16[1,128,256]{2,1,0:T(8,128)(2,1)S(1)}, u32[]{:S(2)}, u32[]{:S(2)}) %collective-permute-start.26) | collective-permute-done | bytes 65568 | tf_op jit(solution)/shard_map/ppermute | solution.py:518
  283.4 5.5 %first_grads.1 = (bf16[8,2,16,1024]{3,2,1,0:T(8,128)(2,1)}, bf16[8,2,16,1024]{3,2,1,0:T(8,128)(2,1)}, f32[8,1024]{1,0:T(8,128)}) custom-call(s32[2]{0:T(128)} %pad_add_fusion.1.refs_0_.own_ref, bf16[8,128,384]{2,1,0:T(8,128)(2,1)} %copy-done.1, bf16[1024,768]{1,0:T(8,128)(2,1)} %get-tuple-element.158.weight_ref, ...), custom_call_target="tpu_custom_call" | custom-call | tf_op jit(solution)/shard_map/first_grads/pallas_call | solution.py:1097
  291.5 5.6 %all-to-all-start.4 = ((f32[32,8,128]{2,1,0:T(8,128)}), f32[32,8,128]{2,1,0:T(8,128)S(1)}, u32[]{:S(2)}, u32[]{:S(2)}) async-start(f32[32,8,128]{2,1,0:T(8,128)} %small_pack.1), calls=%async_computation.5 | async-start | bytes 262144 | tf_op jit(solution)/shard_map/all_to_all | solution.py:1401
  297.1 3.7 %collective-permute-done.29 = bf16[2,128,768]{2,1,0:T(8,128)(2,1)S(1)} collective-permute-done((bf16[2,128,768]{2,1,0:T(8,128)(2,1)S(1)}, bf16[2,128,768]{2,1,0:T(8,128)(2,1)S(1)}, u32[]{:S(2)}, u32[]{:S(2)}) %collective-permute-start.29) | collective-permute-done | bytes 393248 | tf_op jit(solution)/shard_map/ppermute | solution.py:518
  306.8 3.3 %collective-permute-done.32 = bf16[8,16,1024]{2,1,0:T(8,128)(2,1)S(1)} collective-permute-done((bf16[8,16,1024]{2,1,0:T(8,128)(2,1)S(1)}, bf16[8,16,1024]{2,1,0:T(8,128)(2,1)S(1)}, u32[]{:S(2)}, u32[]{:S(2)}) %collective-permute-start.32) | collective-permute-done | bytes 262176 | tf_op jit(solution)/shard_map/ppermute | solution.py:518
  311.4 3.2 collective-permute-done.31
  (183 shorter events, 72.7 us)
Async XLA Ops:
  7.2 153.9 %all-gather.2.cloned.1.call-start = ((), (), s32[]{:S(2)}) async-start(), calls=%async_computation.6 | async-start | bytes 4718592 | tf_op jit(solution)/shard_map/all_gather | solution.py:1324
  7.2 17.4 %collective-permute-start.4 = (bf16[8,16,1024]{2,1,0:T(8,128)(2,1)}, bf16[8,16,1024]{2,1,0:T(8,128)(2,1)S(1)}, u32[]{:S(2)}, u32[]{:S(2)}) collective-permute-start(bf16[8,16,1024]{2,1,0:T(8,128)(2,1)} %bitcast.103), channel_id=1, source_target_pairs={{0,3},{1,2},{2,1},{3,0},{4,7},{5,6},{6,5},{7,4},{8,11},{9,10},{10,... | collective-permute-start | bytes 786440 | tf_op jit(solution)/shard_map/ppermute | solution.py:518
  9.7 15.0 %collective-permute-start.3 = (bf16[8,16,1024]{2,1,0:T(8,128)(2,1)}, bf16[8,16,1024]{2,1,0:T(8,128)(2,1)S(1)}, u32[]{:S(2)}, u32[]{:S(2)}) collective-permute-start(bf16[8,16,1024]{2,1,0:T(8,128)(2,1)} %bitcast.104), channel_id=1, source_target_pairs={{0,2},{1,3},{2,0},{3,1},{4,6},{5,7},{6,4},{7,5},{8,10},{9,11},{10,... | collective-permute-start | bytes 786440 | tf_op jit(solution)/shard_map/ppermute | solution.py:518
  10.3 14.3 %collective-permute-start.2 = (bf16[8,16,1024]{2,1,0:T(8,128)(2,1)}, bf16[8,16,1024]{2,1,0:T(8,128)(2,1)S(1)}, u32[]{:S(2)}, u32[]{:S(2)}) collective-permute-start(bf16[8,16,1024]{2,1,0:T(8,128)(2,1)} %bitcast.105), channel_id=1, source_target_pairs={{0,1},{1,0},{2,3},{3,2},{4,5},{5,4},{6,7},{7,6},{8,9},{9,8},{10,11... | collective-permute-start | bytes 786440 | tf_op jit(solution)/shard_map/ppermute | solution.py:518
  13.5 11.2 %collective-permute-start = (bf16[1,80,1024]{2,1,0:T(8,128)(2,1)}, bf16[1,80,1024]{2,1,0:T(8,128)(2,1)S(1)}, u32[]{:S(2)}, u32[]{:S(2)}) collective-permute-start(bf16[1,80,1024]{2,1,0:T(8,128)(2,1)} %get-tuple-element.97), channel_id=1, source_target_pairs={{0,16},{4,20},{8,24},{12,28},{16,0},{20,4},{24,8},{28,12},{1,17},{... | collective-permute-start | bytes 491528 | tf_op jit(solution)/shard_map/ppermute | solution.py:518
  24.7 17.9 %collective-permute-start.9 = (bf16[8,16,1024]{2,1,0:T(8,128)(2,1)}, bf16[8,16,1024]{2,1,0:T(8,128)(2,1)S(1)}, u32[]{:S(2)}, u32[]{:S(2)}) collective-permute-start(bf16[8,16,1024]{2,1,0:T(8,128)(2,1)} %bitcast.139), channel_id=1, source_target_pairs={{0,3},{1,2},{2,1},{3,0},{4,7},{5,6},{6,5},{7,4},{8,11},{9,10},{10,... | collective-permute-start | bytes 786440 | tf_op jit(solution)/shard_map/ppermute | solution.py:518
  25.0 17.5 %collective-permute-start.8 = (bf16[8,16,1024]{2,1,0:T(8,128)(2,1)}, bf16[8,16,1024]{2,1,0:T(8,128)(2,1)S(1)}, u32[]{:S(2)}, u32[]{:S(2)}) collective-permute-start(bf16[8,16,1024]{2,1,0:T(8,128)(2,1)} %bitcast.140), channel_id=1, source_target_pairs={{0,2},{1,3},{2,0},{3,1},{4,6},{5,7},{6,4},{7,5},{8,10},{9,11},{10,... | collective-permute-start | bytes 786440 | tf_op jit(solution)/shard_map/ppermute | solution.py:518
  26.2 16.4 %collective-permute-start.7 = (bf16[8,16,1024]{2,1,0:T(8,128)(2,1)}, bf16[8,16,1024]{2,1,0:T(8,128)(2,1)S(1)}, u32[]{:S(2)}, u32[]{:S(2)}) collective-permute-start(bf16[8,16,1024]{2,1,0:T(8,128)(2,1)} %bitcast.141), channel_id=1, source_target_pairs={{0,1},{1,0},{2,3},{3,2},{4,5},{5,4},{6,7},{7,6},{8,9},{9,8},{10,11... | collective-permute-start | bytes 786440 | tf_op jit(solution)/shard_map/ppermute | solution.py:518
  27.6 15.0 %collective-permute-start.6 = (bf16[2,64,1024]{2,1,0:T(8,128)(2,1)S(1)}, bf16[2,64,1024]{2,1,0:T(8,128)(2,1)S(1)}, u32[]{:S(2)}, u32[]{:S(2)}) collective-permute-start(bf16[2,64,1024]{2,1,0:T(8,128)(2,1)S(1)} %pad_maximum_fusion.2), channel_id=1, source_target_pairs={{0,16},{4,20},{8,24},{12,28},{16,0},{20,4},{24,8},{28,12},{1,17},{... | collective-permute-start | bytes 786440 | tf_op jit(solution)/shard_map/ppermute | solution.py:518
  29.6 15.4 %collective-permute-start.5 = (bf16[2,80,1024]{2,1,0:T(8,128)(2,1)S(1)}, bf16[2,80,1024]{2,1,0:T(8,128)(2,1)S(1)}, u32[]{:S(2)}, u32[]{:S(2)}) collective-permute-start(bf16[2,80,1024]{2,1,0:T(8,128)(2,1)S(1)} %pad_maximum_fusion.1), channel_id=1, source_target_pairs={{0,8},{4,12},{8,0},{12,4},{16,24},{20,28},{24,16},{28,20},{1,9},{5... | collective-permute-start | bytes 983048 | tf_op jit(solution)/shard_map/ppermute | solution.py:518
  45.1 16.2 %collective-permute-start.10 = (bf16[4,80,1024]{2,1,0:T(8,128)(2,1)S(1)}, bf16[4,80,1024]{2,1,0:T(8,128)(2,1)S(1)}, u32[]{:S(2)}, u32[]{:S(2)}) collective-permute-start(bf16[4,80,1024]{2,1,0:T(8,128)(2,1)S(1)} %constant_dynamic-update-slice_fusion.refs_5_), channel_id=1, source_target_pairs={{0,4},{4,0},{8,12},{12,8},{16,20},{20,16},{24,28},{28,24},{1,5},{5... | collective-permute-start | bytes 1966088 | tf_op jit(solution)/shard_map/ppermute | solution.py:518
  46.7 13.1 %collective-permute-start.11 = (bf16[4,64,1024]{2,1,0:T(8,128)(2,1)S(1)}, bf16[4,64,1024]{2,1,0:T(8,128)(2,1)S(1)}, u32[]{:S(2)}, u32[]{:S(2)}) collective-permute-start(bf16[4,64,1024]{2,1,0:T(8,128)(2,1)S(1)} %constant_dynamic-update-slice_fusion.3.refs_7_), channel_id=1, source_target_pairs={{0,8},{4,12},{8,0},{12,4},{16,24},{20,28},{24,16},{28,20},{1,9},{5... | collective-permute-start | bytes 1572872 | tf_op jit(solution)/shard_map/ppermute | solution.py:518
  67.4 40.2 %all-to-all-start = ((bf16[8,128,384]{2,1,0:T(8,128)(2,1)}), bf16[8,128,384]{2,1,0:T(8,128)(2,1)S(1)}, u32[]{:S(2)}, u32[]{:S(2)}) async-start(bf16[8,128,384]{2,1,0:T(8,128)(2,1)} %get-tuple-element.110), calls=%async_computation | async-start | bytes 1572864 | tf_op jit(solution)/shard_map/all_to_all | solution.py:1242
  72.2 232.4 %reduce-scatter.2.cloned.1.call-start = ((), (), s32[]{:S(2)}) async-start(), calls=%async_computation.7 | async-start | bytes 4718592 | tf_op jit(solution)/shard_map/reduce_scatter | solution.py:1356
  142.1 14.0 %collective-permute-start.13 = (bf16[256,1024]{1,0:T(8,128)(2,1)S(1)}, bf16[256,1024]{1,0:T(8,128)(2,1)S(1)}, u32[]{:S(2)}, u32[]{:S(2)}) collective-permute-start(bf16[256,1024]{1,0:T(8,128)(2,1)S(1)} %add_convert_fusion.3), channel_id=1, source_target_pairs={{0,2},{1,3},{2,0},{3,1},{4,6},{5,7},{6,4},{7,5},{8,10},{9,11},{10,... | collective-permute-start | bytes 1572872 | tf_op jit(solution)/shard_map/ppermute | solution.py:518
  156.6 16.0 %collective-permute-start.19 = (bf16[1,64,1024]{2,1,0:T(8,128)(2,1)S(1)}, bf16[1,64,1024]{2,1,0:T(8,128)(2,1)S(1)}, u32[]{:S(2)}, u32[]{:S(2)}) collective-permute-start(bf16[1,64,1024]{2,1,0:T(8,128)(2,1)S(1)} %get-tuple-element.226), channel_id=1, source_target_pairs={{0,24},{4,28},{8,16},{12,20},{16,8},{20,12},{24,0},{28,4},{1,25},{... | collective-permute-start | bytes 393224 | tf_op jit(solution)/shard_map/ppermute | solution.py:518
  157.7 14.9 %collective-permute-start.18 = (bf16[1,64,1024]{2,1,0:T(8,128)(2,1)S(1)}, bf16[1,64,1024]{2,1,0:T(8,128)(2,1)S(1)}, u32[]{:S(2)}, u32[]{:S(2)}) collective-permute-start(bf16[1,64,1024]{2,1,0:T(8,128)(2,1)S(1)} %get-tuple-element.227), channel_id=1, source_target_pairs={{0,16},{4,20},{8,24},{12,28},{16,0},{20,4},{24,8},{28,12},{1,17},{... | collective-permute-start | bytes 393224 | tf_op jit(solution)/shard_map/ppermute | solution.py:518
  157.7 14.9 %collective-permute-start.17 = (bf16[1,64,1024]{2,1,0:T(8,128)(2,1)S(1)}, bf16[1,64,1024]{2,1,0:T(8,128)(2,1)S(1)}, u32[]{:S(2)}, u32[]{:S(2)}) collective-permute-start(bf16[1,64,1024]{2,1,0:T(8,128)(2,1)S(1)} %get-tuple-element.228), channel_id=1, source_target_pairs={{0,8},{4,12},{8,0},{12,4},{16,24},{20,28},{24,16},{28,20},{1,9},{5... | collective-permute-start | bytes 393224 | tf_op jit(solution)/shard_map/ppermute | solution.py:518
  180.2 20.0 %collective-permute-start.20 = (bf16[4,64,1024]{2,1,0:T(8,128)(2,1)S(1)}, bf16[4,64,1024]{2,1,0:T(8,128)(2,1)S(1)}, u32[]{:S(2)}, u32[]{:S(2)}) collective-permute-start(bf16[4,64,1024]{2,1,0:T(8,128)(2,1)S(1)} %pad_maximum_fusion), channel_id=1, source_target_pairs={{0,4},{4,0},{8,12},{12,8},{16,20},{20,16},{24,28},{28,24},{1,5},{5... | collective-permute-start | bytes 1572872 | tf_op jit(solution)/shard_map/ppermute | solution.py:518
  182.3 18.0 %collective-permute-start.16 = (bf16[256,1024]{1,0:T(8,128)(2,1)S(1)}, bf16[256,1024]{1,0:T(8,128)(2,1)S(1)}, u32[]{:S(2)}, u32[]{:S(2)}) collective-permute-start(bf16[256,1024]{1,0:T(8,128)(2,1)S(1)} %add_convert_fusion.1), channel_id=1, source_target_pairs={{0,2},{1,3},{2,0},{3,1},{4,6},{5,7},{6,4},{7,5},{8,10},{9,11},{10,... | collective-permute-start | bytes 1572872 | tf_op jit(solution)/shard_map/ppermute | solution.py:518
  201.1 14.1 %collective-permute-start.22 = (bf16[8,64,1024]{2,1,0:T(8,128)(2,1)}, bf16[8,64,1024]{2,1,0:T(8,128)(2,1)}, u32[]{:S(2)}, u32[]{:S(2)}) collective-permute-start(bf16[8,64,1024]{2,1,0:T(8,128)(2,1)} %constant_dynamic-update-slice_fusion.6.refs_2_), channel_id=1, source_target_pairs={{0,1},{1,0},{2,3},{3,2},{4,5},{5,4},{6,7},{7,6},{8,9},{9,8},{10,11... | collective-permute-start | bytes 3145736 | tf_op jit(solution)/shard_map/ppermute | solution.py:518
  213.7 9.1 %collective-permute-start.23 = (bf16[4,128,256]{2,1,0:T(8,128)(2,1)}, bf16[4,128,256]{2,1,0:T(8,128)(2,1)S(1)}, u32[]{:S(2)}, u32[]{:S(2)}) collective-permute-start(bf16[4,128,256]{2,1,0:T(8,128)(2,1)} %get-tuple-element.139), channel_id=1, source_target_pairs={{0,4},{4,0},{8,12},{12,8},{16,20},{20,16},{24,28},{28,24},{1,5},{5... | collective-permute-start | bytes 786440 | tf_op jit(solution)/shard_map/ppermute | solution.py:518
  215.2 16.2 %all-to-all-start.2 = ((bf16[8,128,128]{2,1,0:T(8,128)(2,1)}), bf16[8,128,128]{2,1,0:T(8,128)(2,1)S(1)}, u32[]{:S(2)}, u32[]{:S(2)}) async-start(bf16[8,128,128]{2,1,0:T(8,128)(2,1)} %get-tuple-element.137), calls=%async_computation.2 | async-start | bytes 524288 | tf_op jit(solution)/shard_map/all_to_all | solution.py:1242
  222.8 21.5 %collective-permute-start.27 = (bf16[8,2,16,1024]{3,2,1,0:T(8,128)(2,1)S(1)}, bf16[8,2,16,1024]{3,2,1,0:T(8,128)(2,1)S(1)}, u32[]{:S(2)}, u32[]{:S(2)}) collective-permute-start(bf16[8,2,16,1024]{3,2,1,0:T(8,128)(2,1)S(1)} %dynamic-slice_bitcast_fusion), channel_id=1, source_target_pairs={{0,1},{1,0},{2,3},{3,2},{4,5},{5,4},{6,7},{7,6},{8,9},{9,8},{10,11... | collective-permute-start | bytes 1572872 | tf_op jit(solution)/shard_map/ppermute | solution.py:518
  239.7 40.8 %all-to-all-start.3 = ((bf16[8,128,384]{2,1,0:T(8,128)(2,1)}), bf16[8,128,384]{2,1,0:T(8,128)(2,1)S(1)}, u32[]{:S(2)}, u32[]{:S(2)}) async-start(bf16[8,128,384]{2,1,0:T(8,128)(2,1)} %bitcast.115), calls=%async_computation.3 | async-start | bytes 1572864 | tf_op jit(solution)/shard_map/all_to_all | solution.py:1242
  245.6 10.0 %collective-permute-start.28 = (bf16[8,16,1024]{2,1,0:T(8,128)(2,1)S(1)}, bf16[8,16,1024]{2,1,0:T(8,128)(2,1)S(1)}, u32[]{:S(2)}, u32[]{:S(2)}) collective-permute-start(bf16[8,16,1024]{2,1,0:T(8,128)(2,1)S(1)} %fusion.11), channel_id=1, source_target_pairs={{0,2},{1,3},{2,0},{3,1},{4,6},{5,7},{6,4},{7,5},{8,10},{9,11},{10,... | collective-permute-start | bytes 786440 | tf_op jit(solution)/shard_map/ppermute | solution.py:518
  251.1 29.4 %collective-permute-start.25 = (bf16[4,128,384]{2,1,0:T(8,128)(2,1)}, bf16[4,128,384]{2,1,0:T(8,128)(2,1)S(1)}, u32[]{:S(2)}, u32[]{:S(2)}) collective-permute-start(bf16[4,128,384]{2,1,0:T(8,128)(2,1)} %get-tuple-element.147), channel_id=1, source_target_pairs={{0,4},{4,0},{8,12},{12,8},{16,20},{20,16},{24,28},{28,24},{1,5},{5... | collective-permute-start | bytes 1179656 | tf_op jit(solution)/shard_map/ppermute | solution.py:518
  253.1 26.8 %collective-permute-start.26 = (bf16[1,128,256]{2,1,0:T(8,128)(2,1)S(1)}, bf16[1,128,256]{2,1,0:T(8,128)(2,1)S(1)}, u32[]{:S(2)}, u32[]{:S(2)}) collective-permute-start(bf16[1,128,256]{2,1,0:T(8,128)(2,1)S(1)} %dynamic-slice_convert_fusion.3), channel_id=1, source_target_pairs={{0,16},{4,20},{8,24},{12,28},{16,0},{20,4},{24,8},{28,12},{1,17},{... | collective-permute-start | bytes 196616 | tf_op jit(solution)/shard_map/ppermute | solution.py:518
  288.9 11.9 %collective-permute-start.30 = (bf16[8,2,16,1024]{3,2,1,0:T(8,128)(2,1)}, bf16[8,2,16,1024]{3,2,1,0:T(8,128)(2,1)S(1)}, u32[]{:S(2)}, u32[]{:S(2)}) collective-permute-start(bf16[8,2,16,1024]{3,2,1,0:T(8,128)(2,1)} %get-tuple-element.159), channel_id=1, source_target_pairs={{0,1},{1,0},{2,3},{3,2},{4,5},{5,4},{6,7},{7,6},{8,9},{9,8},{10,11... | collective-permute-start | bytes 1572872 | tf_op jit(solution)/shard_map/ppermute | solution.py:518
  289.0 11.9 %collective-permute-start.29 = (bf16[2,128,768]{2,1,0:T(8,128)(2,1)S(1)}, bf16[2,128,768]{2,1,0:T(8,128)(2,1)S(1)}, u32[]{:S(2)}, u32[]{:S(2)}) collective-permute-start(bf16[2,128,768]{2,1,0:T(8,128)(2,1)S(1)} %copy-done.28), channel_id=1, source_target_pairs={{0,8},{4,12},{8,0},{12,4},{16,24},{20,28},{24,16},{28,20},{1,9},{5... | collective-permute-start | bytes 1179656 | tf_op jit(solution)/shard_map/ppermute | solution.py:518
  291.5 19.9 %all-to-all-start.4 = ((f32[32,8,128]{2,1,0:T(8,128)}), f32[32,8,128]{2,1,0:T(8,128)S(1)}, u32[]{:S(2)}, u32[]{:S(2)}) async-start(f32[32,8,128]{2,1,0:T(8,128)} %small_pack.1), calls=%async_computation.5 | async-start | bytes 262144 | tf_op jit(solution)/shard_map/all_to_all | solution.py:1401
  303.8 10.9 %collective-permute-start.31 = (bf16[1,128,768]{2,1,0:T(8,128)(2,1)S(1)}, bf16[1,128,768]{2,1,0:T(8,128)(2,1)S(1)}, u32[]{:S(2)}, u32[]{:S(2)}) collective-permute-start(bf16[1,128,768]{2,1,0:T(8,128)(2,1)S(1)} %dynamic-slice_convert_fusion.2), channel_id=1, source_target_pairs={{0,16},{4,20},{8,24},{12,28},{16,0},{20,4},{24,8},{28,12},{1,17},{... | collective-permute-start | bytes 589832 | tf_op jit(solution)/shard_map/ppermute | solution.py:518
  (39 other events, 286.9 us)
Sparse Core Ops, SparseCore 0:
  61.5 93.2 all-gather.1
  179.3 105.2 reduce-scatter.1

commit v2 on v1

--- a/solution.py
+++ b/solution.py
@@ -657,7 +657,9 @@
         centered, scale = norm_parts(rows_ref[rows, :].astype(jnp.float32))
         normed = (centered * scale * gain + shift).astype(jnp.bfloat16)
         first_ref[rows, :] = normed
-        projected = (mm(normed, weight_ref[...], NN) + bias).astype(jnp.bfloat16)
+    projected_all = (mm(first_ref[...], weight_ref[...], NN) + bias).astype(jnp.bfloat16)
+    for seq in range(rows_ref.shape[0] // seq_rows):
+        projected = projected_all[seq * seq_rows : (seq + 1) * seq_rows, :]
         for group in range(groups):
             for number in range(3):
                 low = number * dim_local + group * width
@@ -830,25 +832,22 @@
     return mine, swap(other.astype(jnp.bfloat16), "ctx", bit)
 
 
-MLP_ROWS = 128
-
-
-def branch_kernel(own_ref, attended_ref, weight_ref, mine_ref, other_ref):
+MLP_ROWS = 256
+
+
+def branch_kernel(own_ref, attended_ref, weight_ref, mine_ref, other_ref, attended):
     core = own_ref[0] & 1
     count, seq_rows, width = attended_ref.shape
     seqs = mine_ref.shape[0] // seq_rows
     groups = count // (2 * seqs)
-    for half, out_ref in enumerate((mine_ref, other_ref)):
+    for half, out_ref in ((1, other_ref), (0, mine_ref)):
         for seq in range(seqs):
-            first = ((core ^ half) * seqs + seq) * groups
-            total = mm(attended_ref[first], weight_ref[0:width, :], NN)
-            for group in range(1, groups):
-                total += mm(
-                    attended_ref[first + group],
-                    weight_ref[group * width : (group + 1) * width, :],
-                    NN,
-                )
-            out_ref[seq * seq_rows : (seq + 1) * seq_rows, :] = total.astype(jnp.bfloat16)
+            for group in range(groups):
+                source = ((core ^ half) * seqs + seq) * groups + group
+                attended[
+                    seq * seq_rows : (seq + 1) * seq_rows, group * width : (group + 1) * width
+                ] = attended_ref[source]
+        out_ref[...] = mm(attended[...], weight_ref[...], NN).astype(jnp.bfloat16)
 
 
 def branch_part(own, attended, out_full):
@@ -861,6 +860,7 @@
         out_shape=(jax.ShapeDtypeStruct(shape, jnp.bfloat16),) * 2,
         in_specs=[SMEM_SPEC, whole_block(attended), whole_block(out_full)],
         out_specs=(whole_shape(shape),) * 2,
+        scratch_shapes=[pltpu.VMEM((rows // 2, out_full.shape[0]), jnp.bfloat16)],
         compiler_params=KERNEL_PARAMS,
         name="branch_part",
     )(own, attended, out_full)
@@ -903,12 +903,15 @@
             for block in range(2):
                 first = pl.multiple_of(block * block_rows + own_tp * part_rows, part_rows)
                 own_grad_ref[seq * 2 + block] = rows_ref[pl.ds(first, part_rows), :]
-            attended = mm(low, weight_ref[...], NT).astype(jnp.bfloat16)
-            for group in range(groups):
-                send_ref[seq * groups + group] = attended[:, group * width : (group + 1) * width]
             sums[0] += jnp.sum(total, axis=0, keepdims=True)
             sums[1] += jnp.sum(grad * normal, axis=0, keepdims=True)
             sums[2] += jnp.sum(grad, axis=0, keepdims=True)
+    attended = mm(branch_ref[...], weight_ref[...], NT).astype(jnp.bfloat16)
+    for index in range(count):
+        seq, group = index // groups, index % groups
+        send_ref[index] = attended[
+            seq * seq_rows : (seq + 1) * seq_rows, group * width : (group + 1) * width
+        ]
     sums_ref[...] = jnp.zeros(sums_ref.shape, jnp.float32)
     for number, total in enumerate(sums):
         sums_ref[number : number + 1, :] = total
@@ -1068,9 +1071,10 @@
     model_width = x_ref.shape[1]
     block_rows = seq_rows // 2
     sums = [jnp.zeros((1, model_width), jnp.float32) for _ in range(2)]
+    partial_all = mm(mixed[...], weight_ref[...], NT)
     for seq in range(count // groups):
         rows = slice(seq * seq_rows, (seq + 1) * seq_rows)
-        partial = mm(mixed[rows, :], weight_ref[...], NT)
+        partial = partial_all[rows, :]
         rows_ref[...] = partial.astype(jnp.bfloat16)
         for block in range(2):
             for row in range(2):
@@ -1373,20 +1377,19 @@
     grad_attended, last_piece = together(grad_attended, held[1][2])
     held[1] = (offsets, 1, last_piece)
     out_mine, out_other = halved_grads(own, grad_branch, attended, ctx_count)
-    grad_heads, out_came = together(exchange(grad_attended), swap(out_other, "ctx", 1))
-    out_mine, out_came = halve(out_mine, out_came, 2)
-    grad_heads = grad_heads.reshape(ctx_count * seq_rows, width)
+    out_came = swap(out_other, "ctx", 1)
+    grad_heads = exchange(grad_attended).reshape(ctx_count * seq_rows, width)
     grad_qkv = attend_backward(slots, qkv, grad_heads, log_total, block_rows)
     grad_qkv, out_came = together(grad_qkv, out_came)
-    for bit in bits[2:]:
-        out_mine, out_came = halve(out_mine, out_came, bit)
+    mix_mine, mix_other = mix_grads(own, grad_qkv, ctx_count, held)
+    mix_other, out_came = together(mix_other, out_came)
+    out_mine, out_came = halve(out_mine, out_came, 2)
     down_sum = add_rows_to_owner(mm(activated, late_all[:, hidden_local:], NT), part_rows)
     own_hidden = lax.dynamic_index_in_dim(
         hidden.reshape(-1, tp_count, part_rows, model_width), own_tp, 1, keepdims=False
     )
     result = (own_hidden + down_sum + bias_down).astype(low)
 
-    mix_mine, mix_other = mix_grads(own, grad_qkv, ctx_count, held)
     grad_mixed, mix_mine, mix_came, out_came, result = together(
         exchange(grad_qkv.reshape(ctx_count, seq_rows, 3 * width)),
         mix_mine,
@@ -1397,27 +1400,26 @@
     mix_mine, mix_other = mix_join(own, mix_mine, mix_came)
     mix_came = swap(mix_other, "ctx", 2)
     grad_mixed, mix_mine = together(grad_mixed, mix_mine)
+    for bit in bits[2:]:
+        out_mine, out_came = halve(out_mine, out_came, bit)
     mine, other, first_sums = first_grads(own, grad_mixed, mix_full, row_all, part_rows)
-    small = lax.all_to_all(
-        small_pack(own, first_sums, hidden_sums, early_sums, ctx_count),
-        ("ctx", "tp"),
-        0,
-        0,
-        tiled=True,
-    )
-    mix_came, came = together(mix_came, swap(other, "tp", 1))
-    mine, came = owner_second(mine, came)
+    small_terms = small_pack(own, first_sums, hidden_sums, early_sums, ctx_count)
+    other, small_terms = together(other, small_terms)
+    small = lax.all_to_all(small_terms, ("ctx", "tp"), 0, 0, tiled=True)
+    mine, came = owner_second(mine, swap(other, "tp", 1))
+    mix_came, came, out_came = together(mix_came, came, out_came)
     for bit in bits[2:]:
         mix_mine, mix_came = halve(mix_mine, mix_came, bit)
     up_shard, down_shard = feed_finish(feed_total)
-    came, up_shard, down_shard = together(came, up_shard, down_shard)
     grad_first = mine + came.astype(wide)
     own_rows = inputs.reshape(-1, part_rows, model_width).astype(wide)
     own_centered, own_scale = norm_parts(own_rows)
     grad_inputs = own_grad + norm_backward(
         own_centered * own_scale, own_scale, grad_first, gain_one
     )
-    mix_came, grad_inputs, small = together(mix_came, grad_inputs, small)
+    mix_came, grad_inputs, small, up_shard, down_shard = together(
+        mix_came, grad_inputs, small, up_shard, down_shard
+    )
     mix_shard_sum, out_shard_sum = mix_finish(mix_mine[0], mix_came[0], out_mine[0], out_came[0])
     sums = jnp.sum(small, axis=0)
     piece = dim_local // ctx_count

time: 326 us -> 312 us (0.957)
  waiting for transfers between devices: 136 us -> 124 us
  starting transfers between devices: 52.1 us -> 57.5 us
  local copies, waits for them, and re-layouts: 16.3 us -> 12.4 us
    ppermute x33, waiting for transfers between devices: 94 us -> 81 us  [swap(): return lax.ppermute(values, axis, [(i, i ^ bit) for i in range(count)])]
    ppermute x33, starting transfers between devices: 34.4 us -> 42 us  [swap(): return lax.ppermute(values, axis, [(i, i ^ bit) for i in range(count)])]
    unnamed x72 -> x68, local copies, waits for them, and re-layouts: 11.3 us -> 7.66 us
  transfers between devices with their start and end apart: 39 -> 39, of which waited for: 17 -> 18; matrix products, arithmetic and copies ran while one was open for 7% -> 7% of each run, Pallas kernels for 18% -> 18%
where the time goes in v2:
time: 312 us; the launch traced here: 311 us
  waiting for transfers between devices  124 us (40%)
  Pallas kernels  65.3 us (21%)
  starting transfers between devices  57.5 us (18%)
  blocking collectives  21.1 us (7%)
  between operations  14.7 us (5%)
  other arithmetic  13.1 us (4%)
  local copies, waits for them, and re-layouts  12.4 us (4%)
    ppermute x33, waiting for transfers between devices, swap(): return lax.ppermute(values, axis, [(i, i ^ bit) for i in range(count)])  81 us
    all_to_all x3, waiting for transfers between devices, exchange(): return lax.all_to_all(pieces, 'ctx', 0, 0, tiled=True)  42.9 us
    ppermute x33, starting transfers between devices, swap(): return lax.ppermute(values, axis, [(i, i ^ bit) for i in range(count)])  42 us
    all_to_all x1, blocking collectives, exchange(): return lax.all_to_all(pieces, 'ctx', 0, 0, tiled=True)  21.1 us
    all_to_all x3, starting transfers between devices, exchange(): return lax.all_to_all(pieces, 'ctx', 0, 0, tiled=True)  12.1 us
    pallas_call x1, Pallas kernels, feed_part(): pl.pallas_call(lambda *refs: feed_kernel(len(cot_parts), *refs), grid=(1,...  9.31 us
    unnamed x68, local copies, waits for them, and re-layouts  7.66 us
    pallas_call x1, Pallas kernels, attend_backward(): pl.pallas_call(lambda *refs: backward_kernel(block_rows, *refs), out_shap...  6.94 us
  transfers between devices with their start and end apart: 39, of which 18 were waited for; matrix products, arithmetic and copies ran while one was open for 7% of the time, Pallas kernels for 18%

profile of v2, /device:TPU:0, one launch (start us, length us, event | category | flops | bytes accessed | tf_op | source)
XLA Modules:
  0.0 311.0 jit_solution(13424388424743457200)
XLA Ops:
  13.5 2.8 collective-permute-start
  17.8 4.1 %collective-permute-done.1 = bf16[1,64,1024]{2,1,0:T(8,128)(2,1)S(1)} collective-permute-done((bf16[1,64,1024]{2,1,0:T(8,128)(2,1)}, bf16[1,64,1024]{2,1,0:T(8,128)(2,1)S(1)}, u32[]{:S(2)}, u32[]{:S(2)}) %collective-permute-start.1) | collective-permute-done | bytes 131104 | tf_op jit(solution)/shard_map/ppermute | solution.py:518
  21.9 2.8 collective-permute-done
  29.6 3.1 collective-permute-start.5
  34.6 8.0 %collective-permute-done.6 = bf16[2,64,1024]{2,1,0:T(8,128)(2,1)S(1)} collective-permute-done((bf16[2,64,1024]{2,1,0:T(8,128)(2,1)S(1)}, bf16[2,64,1024]{2,1,0:T(8,128)(2,1)S(1)}, u32[]{:S(2)}, u32[]{:S(2)}) %collective-permute-start.6) | collective-permute-done | bytes 262176 | tf_op jit(solution)/shard_map/ppermute | solution.py:518
  48.9 11.0 %collective-permute-done.11.refs_8_ = bf16[4,64,1024]{2,1,0:T(8,128)(2,1)S(1)} collective-permute-done((bf16[4,64,1024]{2,1,0:T(8,128)(2,1)S(1)}, bf16[4,64,1024]{2,1,0:T(8,128)(2,1)S(1)}, u32[]{:S(2)}, u32[]{:S(2)}) %collective-permute-start.11) | collective-permute-done | bytes 524320 | tf_op jit(solution)/shard_map/ppermute | solution.py:518
  62.2 5.2 %first_part.1 = (bf16[512,1024]{1,0:T(8,128)(2,1)}, bf16[512,1024]{1,0:T(8,128)(2,1)}, bf16[1024,768]{1,0:T(8,128)(2,1)}, bf16[256,1024]{1,0:T(8,128)(2,1)}, f32...) custom-call(s32[2]{0:T(128)} %pad_add_fusion.1.refs_0_.own_ref, bf16[8,16,1024]{2,1,0:T(8,128)(2,1)} %bitcast.106, ...), custom_call_target="tpu_custom_call" | custom-call | flops 805306368 | bytes 8388608 | tf_op jit(solution)/shard_map/first_part/pallas_call | solution.py:689
  67.4 4.9 %all-to-all-start = ((bf16[8,128,384]{2,1,0:T(8,128)(2,1)}), bf16[8,128,384]{2,1,0:T(8,128)(2,1)S(1)}, u32[]{:S(2)}, u32[]{:S(2)}) async-start(bf16[8,128,384]{2,1,0:T(8,128)(2,1)} %get-tuple-element.112), calls=%async_computation | async-start | bytes 1572864 | tf_op jit(solution)/shard_map/all_to_all | solution.py:1246
  73.8 33.7 %all-to-all-done = bf16[8,128,384]{2,1,0:T(8,128)(2,1)S(1)} async-done(((bf16[8,128,384]{2,1,0:T(8,128)(2,1)}), bf16[8,128,384]{2,1,0:T(8,128)(2,1)S(1)}, u32[]{:S(2)}, u32[]{:S(2)}) %all-to-all-start) | async-done | bytes 786464 | tf_op jit(solution)/shard_map/all_to_all | solution.py:1246
  108.4 6.6 %attend_forward.1 = (bf16[1024,128]{1,0:T(8,128)(2,1)}, f32[8,1024]{1,0:T(8,128)}) custom-call(s32[16]{0:T(128)} %select_reduce_fusion.refs_0_, bf16[1024,384]{1,0:T(8,128)(2,1)} %bitcast.113), custom_call_target="tpu_custom_call" | custom-call | flops 402653184 | bytes 1048576 | tf_op jit(solution)/shard_map/attend_forward/pallas_call | solution.py:474
  115.0 21.1 %all_to_all.25.attended_ref.right_ref = bf16[8,128,128]{2,1,0:T(8,128)(2,1)} all-to-all(bf16[8,128,128]{2,1,0:T(8,128)(2,1)} %bitcast.118), channel_id=1, replica_groups=mesh['ctx'=8,'tp'=4] {'ctx'}, dimensions={0} | all-to-all | bytes 524288 | tf_op jit(solution)/shard_map/all_to_all | solution.py:1246
  143.5 12.5 %collective-permute-done.13 = bf16[256,1024]{1,0:T(8,128)(2,1)S(1)} collective-permute-done((bf16[256,1024]{1,0:T(8,128)(2,1)S(1)}, bf16[256,1024]{1,0:T(8,128)(2,1)S(1)}, u32[]{:S(2)}, u32[]{:S(2)}) %collective-permute-start.13) | collective-permute-done | bytes 524320 | tf_op jit(solution)/shard_map/ppermute | solution.py:518
  157.6 3.3 %collective-permute-start.17 = (bf16[1,64,1024]{2,1,0:T(8,128)(2,1)S(1)}, bf16[1,64,1024]{2,1,0:T(8,128)(2,1)S(1)}, u32[]{:S(2)}, u32[]{:S(2)}) collective-permute-start(bf16[1,64,1024]{2,1,0:T(8,128)(2,1)S(1)} %get-tuple-element.232), channel_id=1, source_target_pairs={{0,8},{4,12},{8,0},{12,4},{16,24},{20,28},{24,16},{28,20},{1,9},{5... | collective-permute-start | bytes 393224 | tf_op jit(solution)/shard_map/ppermute | solution.py:518
  161.7 9.3 %feed_part.1 = (f32[512,1024]{1,0:T(8,128)}, bf16[512,1024]{1,0:T(8,128)(2,1)}, bf16[512,1024]{1,0:T(8,128)(2,1)}, bf16[512,1024]{1,0:T(8,128)(2,1)}, bf16[256,1...) custom-call(s32[2]{0:T(128)} %pad_add_fusion.1.refs_0_.own_ref, ...), custom_call_target="tpu_custom_call" | custom-call | flops 3221225472 | bytes 16777216 | tf_op jit(solution)/shard_map/feed_part/pallas_call | solution.py:1195
  171.0 6.4 %feed_grads.1 = bf16[1024,2048]{1,0:T(8,128)(2,1)} custom-call(bf16[512,1024]{1,0:T(8,128)(2,1)} %get-tuple-element.172.second_ref, bf16[512,1024]{1,0:T(8,128)(2,1)} %get-tuple-element.173.grad_pre_ref, bf16[512,1024]{1,0:T(8,128)(2,1)} %get-tuple-element.135.cot_ref, bf16[512,1024]{1,0:T(8,128)(2,1)} %get-tuple-element.151.activated_ref), custom_call_target="tpu_custom_call" | custom-call | flops 2147483648 | bytes 8388608 | tf_op jit(solution)/shard_map/feed_grads/pallas_call | solution.py:721
  182.2 16.4 %collective-permute-done.20 = bf16[4,64,1024]{2,1,0:T(8,128)(2,1)S(1)} collective-permute-done((bf16[4,64,1024]{2,1,0:T(8,128)(2,1)S(1)}, bf16[4,64,1024]{2,1,0:T(8,128)(2,1)S(1)}, u32[]{:S(2)}, u32[]{:S(2)}) %collective-permute-start.20) | collective-permute-done | bytes 524320 | tf_op jit(solution)/shard_map/ppermute | solution.py:518
  199.5 2.6 collective-permute-done.21.other_ref
  202.9 5.6 %hidden_grad_part.1 = (bf16[8,128,128]{2,1,0:T(8,128)(2,1)}, bf16[512,1024]{1,0:T(8,128)(2,1)}, f32[8,16,1024]{2,1,0:T(8,128)}, f32[8,1024]{1,0:T(8,128)}) custom-call(s32[2]{0:T(128)} %pad_add_fusion.1.refs_0_.own_ref, bf16[256,1024]{1,0:T(8,128)(2,1)} %copy-done.2, bf16[256,1024]{1,0:T(8,128)(2,1)} %copy-done.11, ...), custom_call_target="tpu_custom_call" | custom-call | tf_op jit(solution)/shard_map/hidden_grad_part/pallas_call | solution.py:931
  208.5 3.6 %all-to-all-start.2 = ((bf16[8,128,128]{2,1,0:T(8,128)(2,1)}), bf16[8,128,128]{2,1,0:T(8,128)(2,1)S(1)}, u32[]{:S(2)}, u32[]{:S(2)}) async-start(bf16[8,128,128]{2,1,0:T(8,128)(2,1)} %get-tuple-element.139), calls=%async_computation.2 | async-start | bytes 524288 | tf_op jit(solution)/shard_map/all_to_all | solution.py:1246
  212.1 2.9 fusion.2
  215.0 2.6 halved_grads.1
  219.4 9.2 %all-to-all-done.2 = bf16[8,128,128]{2,1,0:T(8,128)(2,1)S(1)} async-done(((bf16[8,128,128]{2,1,0:T(8,128)(2,1)}), bf16[8,128,128]{2,1,0:T(8,128)(2,1)S(1)}, u32[]{:S(2)}, u32[]{:S(2)}) %all-to-all-start.2) | async-done | bytes 262176 | tf_op jit(solution)/shard_map/all_to_all | solution.py:1246
  229.3 6.9 %attend_backward.1.refs_1_ = bf16[1024,384]{1,0:T(8,128)(2,1)} custom-call(s32[16]{0:T(128)} %select_reduce_fusion.refs_0_, bf16[1024,384]{1,0:T(8,128)(2,1)} %bitcast.114, bf16[1024,128]{1,0:T(8,128)(2,1)} %bitcast.117, f32[8,1024]{1,0:T(8,128)} %get-tuple-element.140.refs_3_), custom_call_target="tpu_custom_call" | custom-call | flops 939524096 | bytes 1835008 | tf_op jit(solution)/shard_map/attend_backward/pallas_call | solution.py:496
  236.2 3.6 %all-to-all-start.3 = ((bf16[8,128,384]{2,1,0:T(8,128)(2,1)}), bf16[8,128,384]{2,1,0:T(8,128)(2,1)S(1)}, u32[]{:S(2)}, u32[]{:S(2)}) async-start(bf16[8,128,384]{2,1,0:T(8,128)(2,1)} %bitcast.115), calls=%async_computation.3 | async-start | bytes 1572864 | tf_op jit(solution)/shard_map/all_to_all | solution.py:1246
  243.8 4.0 %mix_grads.1 = (bf16[4,128,384]{2,1,0:T(8,128)(2,1)}, bf16[4,128,384]{2,1,0:T(8,128)(2,1)}) custom-call(s32[2]{0:T(128)} %pad_add_fusion.1.refs_0_.own_ref, bf16[1024,384]{1,0:T(8,128)(2,1)} %attend_backward.1.refs_1_, bf16[8,64,1024]{2,1,0:T(8,128)(2,1)} %copy-done.24, bf16[8,64,1024]{2,1,0:T(8,128)(2,1)} %collective-permute-done.22.refs_3_), custom_call_target="tpu_custom_call" | custom-call | flops 805306368 | bytes 8388608 | tf_op jit(solution)/shard_map/mix_grads/pallas_call | solution.py:1014
  253.3 3.3 %collective-permute-done.25 = bf16[2,128,256]{2,1,0:T(8,128)(2,1)S(1)} collective-permute-done((bf16[2,128,256]{2,1,0:T(8,128)(2,1)S(1)}, bf16[2,128,256]{2,1,0:T(8,128)(2,1)S(1)}, u32[]{:S(2)}, u32[]{:S(2)}) %collective-permute-start.25) | collective-permute-done | bytes 131104 | tf_op jit(solution)/shard_map/ppermute | solution.py:518
  257.3 5.2 %collective-permute-done.24.came_ref = bf16[4,128,384]{2,1,0:T(8,128)(2,1)S(1)} collective-permute-done((bf16[4,128,384]{2,1,0:T(8,128)(2,1)}, bf16[4,128,384]{2,1,0:T(8,128)(2,1)S(1)}, u32[]{:S(2)}, u32[]{:S(2)}) %collective-permute-start.24) | collective-permute-done | bytes 393248 | tf_op jit(solution)/shard_map/ppermute | solution.py:518
  265.4 4.5 %first_grads.1 = (bf16[8,2,16,1024]{3,2,1,0:T(8,128)(2,1)}, bf16[8,2,16,1024]{3,2,1,0:T(8,128)(2,1)}, f32[8,1024]{1,0:T(8,128)}) custom-call(s32[2]{0:T(128)} %pad_add_fusion.1.refs_0_.own_ref, bf16[8,128,384]{2,1,0:T(8,128)(2,1)} %copy-done.1, bf16[1024,768]{1,0:T(8,128)(2,1)} %get-tuple-element.160.weight_ref, ...), custom_call_target="tpu_custom_call" | custom-call | tf_op jit(solution)/shard_map/first_grads/pallas_call | solution.py:1101
  271.7 5.0 %collective-permute-start.28 = (bf16[2,128,768]{2,1,0:T(8,128)(2,1)}, bf16[2,128,768]{2,1,0:T(8,128)(2,1)S(1)}, u32[]{:S(2)}, u32[]{:S(2)}) collective-permute-start(bf16[2,128,768]{2,1,0:T(8,128)(2,1)} %get-tuple-element.158), channel_id=1, source_target_pairs={{0,8},{4,12},{8,0},{12,4},{16,24},{20,28},{24,16},{28,20},{1,9},{5... | collective-permute-start | bytes 1179656 | tf_op jit(solution)/shard_map/ppermute | solution.py:518
  281.3 3.3 %all-to-all-start.4 = ((f32[32,8,128]{2,1,0:T(8,128)}), f32[32,8,128]{2,1,0:T(8,128)S(1)}, u32[]{:S(2)}, u32[]{:S(2)}) async-start(f32[32,8,128]{2,1,0:T(8,128)} %small_pack.1), calls=%async_computation.4 | async-start | bytes 262144 | tf_op jit(solution)/shard_map/all_to_all | solution.py:1408
  288.9 2.5 collective-permute-start.32
  295.6 5.3 %collective-permute-done.32 = bf16[1,128,768]{2,1,0:T(8,128)(2,1)S(1)} collective-permute-done((bf16[1,128,768]{2,1,0:T(8,128)(2,1)S(1)}, bf16[1,128,768]{2,1,0:T(8,128)(2,1)S(1)}, u32[]{:S(2)}, u32[]{:S(2)}) %collective-permute-start.32) | collective-permute-done | bytes 196640 | tf_op jit(solution)/shard_map/ppermute | solution.py:518
  (179 shorter events, 75.0 us)
Async XLA Ops:
  7.2 153.7 %all-gather.2.cloned.1.call-start = ((), (), s32[]{:S(2)}) async-start(), calls=%async_computation.6 | async-start | bytes 4718592 | tf_op jit(solution)/shard_map/all_gather | solution.py:1328
  7.2 17.4 %collective-permute-start.4 = (bf16[8,16,1024]{2,1,0:T(8,128)(2,1)}, bf16[8,16,1024]{2,1,0:T(8,128)(2,1)S(1)}, u32[]{:S(2)}, u32[]{:S(2)}) collective-permute-start(bf16[8,16,1024]{2,1,0:T(8,128)(2,1)} %bitcast.103), channel_id=1, source_target_pairs={{0,3},{1,2},{2,1},{3,0},{4,7},{5,6},{6,5},{7,4},{8,11},{9,10},{10,... | collective-permute-start | bytes 786440 | tf_op jit(solution)/shard_map/ppermute | solution.py:518
  9.7 15.0 %collective-permute-start.3 = (bf16[8,16,1024]{2,1,0:T(8,128)(2,1)}, bf16[8,16,1024]{2,1,0:T(8,128)(2,1)S(1)}, u32[]{:S(2)}, u32[]{:S(2)}) collective-permute-start(bf16[8,16,1024]{2,1,0:T(8,128)(2,1)} %bitcast.104), channel_id=1, source_target_pairs={{0,2},{1,3},{2,0},{3,1},{4,6},{5,7},{6,4},{7,5},{8,10},{9,11},{10,... | collective-permute-start | bytes 786440 | tf_op jit(solution)/shard_map/ppermute | solution.py:518
  10.3 14.3 %collective-permute-start.2 = (bf16[8,16,1024]{2,1,0:T(8,128)(2,1)}, bf16[8,16,1024]{2,1,0:T(8,128)(2,1)S(1)}, u32[]{:S(2)}, u32[]{:S(2)}) collective-permute-start(bf16[8,16,1024]{2,1,0:T(8,128)(2,1)} %bitcast.105), channel_id=1, source_target_pairs={{0,1},{1,0},{2,3},{3,2},{4,5},{5,4},{6,7},{7,6},{8,9},{9,8},{10,11... | collective-permute-start | bytes 786440 | tf_op jit(solution)/shard_map/ppermute | solution.py:518
  13.5 11.2 %collective-permute-start = (bf16[1,80,1024]{2,1,0:T(8,128)(2,1)}, bf16[1,80,1024]{2,1,0:T(8,128)(2,1)S(1)}, u32[]{:S(2)}, u32[]{:S(2)}) collective-permute-start(bf16[1,80,1024]{2,1,0:T(8,128)(2,1)} %get-tuple-element.99), channel_id=1, source_target_pairs={{0,16},{4,20},{8,24},{12,28},{16,0},{20,4},{24,8},{28,12},{1,17},{... | collective-permute-start | bytes 491528 | tf_op jit(solution)/shard_map/ppermute | solution.py:518
  24.7 17.9 %collective-permute-start.9 = (bf16[8,16,1024]{2,1,0:T(8,128)(2,1)}, bf16[8,16,1024]{2,1,0:T(8,128)(2,1)S(1)}, u32[]{:S(2)}, u32[]{:S(2)}) collective-permute-start(bf16[8,16,1024]{2,1,0:T(8,128)(2,1)} %bitcast.138), channel_id=1, source_target_pairs={{0,3},{1,2},{2,1},{3,0},{4,7},{5,6},{6,5},{7,4},{8,11},{9,10},{10,... | collective-permute-start | bytes 786440 | tf_op jit(solution)/shard_map/ppermute | solution.py:518
  25.0 17.5 %collective-permute-start.8 = (bf16[8,16,1024]{2,1,0:T(8,128)(2,1)}, bf16[8,16,1024]{2,1,0:T(8,128)(2,1)S(1)}, u32[]{:S(2)}, u32[]{:S(2)}) collective-permute-start(bf16[8,16,1024]{2,1,0:T(8,128)(2,1)} %bitcast.139), channel_id=1, source_target_pairs={{0,2},{1,3},{2,0},{3,1},{4,6},{5,7},{6,4},{7,5},{8,10},{9,11},{10,... | collective-permute-start | bytes 786440 | tf_op jit(solution)/shard_map/ppermute | solution.py:518
  26.2 16.4 %collective-permute-start.7 = (bf16[8,16,1024]{2,1,0:T(8,128)(2,1)}, bf16[8,16,1024]{2,1,0:T(8,128)(2,1)S(1)}, u32[]{:S(2)}, u32[]{:S(2)}) collective-permute-start(bf16[8,16,1024]{2,1,0:T(8,128)(2,1)} %bitcast.140), channel_id=1, source_target_pairs={{0,1},{1,0},{2,3},{3,2},{4,5},{5,4},{6,7},{7,6},{8,9},{9,8},{10,11... | collective-permute-start | bytes 786440 | tf_op jit(solution)/shard_map/ppermute | solution.py:518
  27.6 15.0 %collective-permute-start.6 = (bf16[2,64,1024]{2,1,0:T(8,128)(2,1)S(1)}, bf16[2,64,1024]{2,1,0:T(8,128)(2,1)S(1)}, u32[]{:S(2)}, u32[]{:S(2)}) collective-permute-start(bf16[2,64,1024]{2,1,0:T(8,128)(2,1)S(1)} %pad_maximum_fusion.2), channel_id=1, source_target_pairs={{0,16},{4,20},{8,24},{12,28},{16,0},{20,4},{24,8},{28,12},{1,17},{... | collective-permute-start | bytes 786440 | tf_op jit(solution)/shard_map/ppermute | solution.py:518
  29.6 15.4 %collective-permute-start.5 = (bf16[2,80,1024]{2,1,0:T(8,128)(2,1)S(1)}, bf16[2,80,1024]{2,1,0:T(8,128)(2,1)S(1)}, u32[]{:S(2)}, u32[]{:S(2)}) collective-permute-start(bf16[2,80,1024]{2,1,0:T(8,128)(2,1)S(1)} %pad_maximum_fusion.1), channel_id=1, source_target_pairs={{0,8},{4,12},{8,0},{12,4},{16,24},{20,28},{24,16},{28,20},{1,9},{5... | collective-permute-start | bytes 983048 | tf_op jit(solution)/shard_map/ppermute | solution.py:518
  45.1 16.2 %collective-permute-start.10 = (bf16[4,80,1024]{2,1,0:T(8,128)(2,1)S(1)}, bf16[4,80,1024]{2,1,0:T(8,128)(2,1)S(1)}, u32[]{:S(2)}, u32[]{:S(2)}) collective-permute-start(bf16[4,80,1024]{2,1,0:T(8,128)(2,1)S(1)} %constant_dynamic-update-slice_fusion.refs_5_), channel_id=1, source_target_pairs={{0,4},{4,0},{8,12},{12,8},{16,20},{20,16},{24,28},{28,24},{1,5},{5... | collective-permute-start | bytes 1966088 | tf_op jit(solution)/shard_map/ppermute | solution.py:518
  46.7 13.1 %collective-permute-start.11 = (bf16[4,64,1024]{2,1,0:T(8,128)(2,1)S(1)}, bf16[4,64,1024]{2,1,0:T(8,128)(2,1)S(1)}, u32[]{:S(2)}, u32[]{:S(2)}) collective-permute-start(bf16[4,64,1024]{2,1,0:T(8,128)(2,1)S(1)} %constant_dynamic-update-slice_fusion.3.refs_7_), channel_id=1, source_target_pairs={{0,8},{4,12},{8,0},{12,4},{16,24},{20,28},{24,16},{28,20},{1,9},{5... | collective-permute-start | bytes 1572872 | tf_op jit(solution)/shard_map/ppermute | solution.py:518
  67.4 40.2 %all-to-all-start = ((bf16[8,128,384]{2,1,0:T(8,128)(2,1)}), bf16[8,128,384]{2,1,0:T(8,128)(2,1)S(1)}, u32[]{:S(2)}, u32[]{:S(2)}) async-start(bf16[8,128,384]{2,1,0:T(8,128)(2,1)} %get-tuple-element.112), calls=%async_computation | async-start | bytes 1572864 | tf_op jit(solution)/shard_map/all_to_all | solution.py:1246
  72.3 221.2 %reduce-scatter.2.cloned.1.call-start = ((), (), s32[]{:S(2)}) async-start(), calls=%async_computation.7 | async-start | bytes 4718592 | tf_op jit(solution)/shard_map/reduce_scatter | solution.py:1360
  141.9 14.0 %collective-permute-start.13 = (bf16[256,1024]{1,0:T(8,128)(2,1)S(1)}, bf16[256,1024]{1,0:T(8,128)(2,1)S(1)}, u32[]{:S(2)}, u32[]{:S(2)}) collective-permute-start(bf16[256,1024]{1,0:T(8,128)(2,1)S(1)} %add_convert_fusion.3), channel_id=1, source_target_pairs={{0,2},{1,3},{2,0},{3,1},{4,6},{5,7},{6,4},{7,5},{8,10},{9,11},{10,... | collective-permute-start | bytes 1572872 | tf_op jit(solution)/shard_map/ppermute | solution.py:518
  156.4 14.6 %collective-permute-start.19 = (bf16[1,64,1024]{2,1,0:T(8,128)(2,1)S(1)}, bf16[1,64,1024]{2,1,0:T(8,128)(2,1)S(1)}, u32[]{:S(2)}, u32[]{:S(2)}) collective-permute-start(bf16[1,64,1024]{2,1,0:T(8,128)(2,1)S(1)} %get-tuple-element.230), channel_id=1, source_target_pairs={{0,24},{4,28},{8,16},{12,20},{16,8},{20,12},{24,0},{28,4},{1,25},{... | collective-permute-start | bytes 393224 | tf_op jit(solution)/shard_map/ppermute | solution.py:518
  157.6 13.5 %collective-permute-start.18 = (bf16[1,64,1024]{2,1,0:T(8,128)(2,1)S(1)}, bf16[1,64,1024]{2,1,0:T(8,128)(2,1)S(1)}, u32[]{:S(2)}, u32[]{:S(2)}) collective-permute-start(bf16[1,64,1024]{2,1,0:T(8,128)(2,1)S(1)} %get-tuple-element.231), channel_id=1, source_target_pairs={{0,16},{4,20},{8,24},{12,28},{16,0},{20,4},{24,8},{28,12},{1,17},{... | collective-permute-start | bytes 393224 | tf_op jit(solution)/shard_map/ppermute | solution.py:518
  157.6 13.5 %collective-permute-start.17 = (bf16[1,64,1024]{2,1,0:T(8,128)(2,1)S(1)}, bf16[1,64,1024]{2,1,0:T(8,128)(2,1)S(1)}, u32[]{:S(2)}, u32[]{:S(2)}) collective-permute-start(bf16[1,64,1024]{2,1,0:T(8,128)(2,1)S(1)} %get-tuple-element.232), channel_id=1, source_target_pairs={{0,8},{4,12},{8,0},{12,4},{16,24},{20,28},{24,16},{28,20},{1,9},{5... | collective-permute-start | bytes 393224 | tf_op jit(solution)/shard_map/ppermute | solution.py:518
  178.5 20.0 %collective-permute-start.20 = (bf16[4,64,1024]{2,1,0:T(8,128)(2,1)S(1)}, bf16[4,64,1024]{2,1,0:T(8,128)(2,1)S(1)}, u32[]{:S(2)}, u32[]{:S(2)}) collective-permute-start(bf16[4,64,1024]{2,1,0:T(8,128)(2,1)S(1)} %pad_maximum_fusion), channel_id=1, source_target_pairs={{0,4},{4,0},{8,12},{12,8},{16,20},{20,16},{24,28},{28,24},{1,5},{5... | collective-permute-start | bytes 1572872 | tf_op jit(solution)/shard_map/ppermute | solution.py:518
  180.6 18.0 %collective-permute-start.16 = (bf16[256,1024]{1,0:T(8,128)(2,1)S(1)}, bf16[256,1024]{1,0:T(8,128)(2,1)S(1)}, u32[]{:S(2)}, u32[]{:S(2)}) collective-permute-start(bf16[256,1024]{1,0:T(8,128)(2,1)S(1)} %add_convert_fusion.1), channel_id=1, source_target_pairs={{0,2},{1,3},{2,0},{3,1},{4,6},{5,7},{6,4},{7,5},{8,10},{9,11},{10,... | collective-permute-start | bytes 1572872 | tf_op jit(solution)/shard_map/ppermute | solution.py:518
  198.6 9.8 %collective-permute-start.22 = (bf16[8,64,1024]{2,1,0:T(8,128)(2,1)S(1)}, bf16[8,64,1024]{2,1,0:T(8,128)(2,1)}, u32[]{:S(2)}, u32[]{:S(2)}) collective-permute-start(bf16[8,64,1024]{2,1,0:T(8,128)(2,1)S(1)} %constant_dynamic-update-slice_fusion.6.refs_2_), channel_id=1, source_target_pairs={{0,1},{1,0},{2,3},{3,2},{4,5},{5,4},{6,7},{7,6},{8,9},{9,8},{10,11... | collective-permute-start | bytes 3145736 | tf_op jit(solution)/shard_map/ppermute | solution.py:518
  208.5 20.1 %all-to-all-start.2 = ((bf16[8,128,128]{2,1,0:T(8,128)(2,1)}), bf16[8,128,128]{2,1,0:T(8,128)(2,1)S(1)}, u32[]{:S(2)}, u32[]{:S(2)}) async-start(bf16[8,128,128]{2,1,0:T(8,128)(2,1)} %get-tuple-element.139), calls=%async_computation.2 | async-start | bytes 524288 | tf_op jit(solution)/shard_map/all_to_all | solution.py:1246
  217.6 18.6 %collective-permute-start.23 = (bf16[4,128,256]{2,1,0:T(8,128)(2,1)}, bf16[4,128,256]{2,1,0:T(8,128)(2,1)S(1)}, u32[]{:S(2)}, u32[]{:S(2)}) collective-permute-start(bf16[4,128,256]{2,1,0:T(8,128)(2,1)} %get-tuple-element.142), channel_id=1, source_target_pairs={{0,4},{4,0},{8,12},{12,8},{16,20},{20,16},{24,28},{28,24},{1,5},{5... | collective-permute-start | bytes 786440 | tf_op jit(solution)/shard_map/ppermute | solution.py:518
  219.3 21.5 %collective-permute-start.26 = (bf16[8,2,16,1024]{3,2,1,0:T(8,128)(2,1)S(1)}, bf16[8,2,16,1024]{3,2,1,0:T(8,128)(2,1)}, u32[]{:S(2)}, u32[]{:S(2)}) collective-permute-start(bf16[8,2,16,1024]{3,2,1,0:T(8,128)(2,1)S(1)} %dynamic-slice_bitcast_fusion), channel_id=1, source_target_pairs={{0,1},{1,0},{2,3},{3,2},{4,5},{5,4},{6,7},{7,6},{8,9},{9,8},{10,11... | collective-permute-start | bytes 1572872 | tf_op jit(solution)/shard_map/ppermute | solution.py:518
  236.2 26.2 %all-to-all-start.3 = ((bf16[8,128,384]{2,1,0:T(8,128)(2,1)}), bf16[8,128,384]{2,1,0:T(8,128)(2,1)S(1)}, u32[]{:S(2)}, u32[]{:S(2)}) async-start(bf16[8,128,384]{2,1,0:T(8,128)(2,1)} %bitcast.115), calls=%async_computation.3 | async-start | bytes 1572864 | tf_op jit(solution)/shard_map/all_to_all | solution.py:1246
  242.0 9.3 %collective-permute-start.27 = (bf16[8,16,1024]{2,1,0:T(8,128)(2,1)S(1)}, bf16[8,16,1024]{2,1,0:T(8,128)(2,1)}, u32[]{:S(2)}, u32[]{:S(2)}) collective-permute-start(bf16[8,16,1024]{2,1,0:T(8,128)(2,1)S(1)} %fusion.11), channel_id=1, source_target_pairs={{0,2},{1,3},{2,0},{3,1},{4,6},{5,7},{6,4},{7,5},{8,10},{9,11},{10,... | collective-permute-start | bytes 786440 | tf_op jit(solution)/shard_map/ppermute | solution.py:518
  247.8 14.7 %collective-permute-start.24 = (bf16[4,128,384]{2,1,0:T(8,128)(2,1)}, bf16[4,128,384]{2,1,0:T(8,128)(2,1)S(1)}, u32[]{:S(2)}, u32[]{:S(2)}) collective-permute-start(bf16[4,128,384]{2,1,0:T(8,128)(2,1)} %get-tuple-element.148), channel_id=1, source_target_pairs={{0,4},{4,0},{8,12},{12,8},{16,20},{20,16},{24,28},{28,24},{1,5},{5... | collective-permute-start | bytes 1179656 | tf_op jit(solution)/shard_map/ppermute | solution.py:518
  271.7 17.0 %collective-permute-start.28 = (bf16[2,128,768]{2,1,0:T(8,128)(2,1)}, bf16[2,128,768]{2,1,0:T(8,128)(2,1)S(1)}, u32[]{:S(2)}, u32[]{:S(2)}) collective-permute-start(bf16[2,128,768]{2,1,0:T(8,128)(2,1)} %get-tuple-element.158), channel_id=1, source_target_pairs={{0,8},{4,12},{8,0},{12,4},{16,24},{20,28},{24,16},{28,20},{1,9},{5... | collective-permute-start | bytes 1179656 | tf_op jit(solution)/shard_map/ppermute | solution.py:518
  277.9 10.8 %collective-permute-start.30 = (bf16[8,16,1024]{2,1,0:T(8,128)(2,1)S(1)}, bf16[8,16,1024]{2,1,0:T(8,128)(2,1)S(1)}, u32[]{:S(2)}, u32[]{:S(2)}) collective-permute-start(bf16[8,16,1024]{2,1,0:T(8,128)(2,1)S(1)} %fusion.12), channel_id=1, source_target_pairs={{0,2},{1,3},{2,0},{3,1},{4,6},{5,7},{6,4},{7,5},{8,10},{9,11},{10,... | collective-permute-start | bytes 786440 | tf_op jit(solution)/shard_map/ppermute | solution.py:518
  279.2 8.6 %collective-permute-start.31 = (bf16[1,128,256]{2,1,0:T(8,128)(2,1)}, bf16[1,128,256]{2,1,0:T(8,128)(2,1)}, u32[]{:S(2)}, u32[]{:S(2)}) collective-permute-start(bf16[1,128,256]{2,1,0:T(8,128)(2,1)} %dynamic-slice_convert_fusion.3), channel_id=1, source_target_pairs={{0,16},{4,20},{8,24},{12,28},{16,0},{20,4},{24,8},{28,12},{1,17},{... | collective-permute-start | bytes 196616 | tf_op jit(solution)/shard_map/ppermute | solution.py:518
  281.3 14.3 %all-to-all-start.4 = ((f32[32,8,128]{2,1,0:T(8,128)}), f32[32,8,128]{2,1,0:T(8,128)S(1)}, u32[]{:S(2)}, u32[]{:S(2)}) async-start(f32[32,8,128]{2,1,0:T(8,128)} %small_pack.1), calls=%async_computation.4 | async-start | bytes 262144 | tf_op jit(solution)/shard_map/all_to_all | solution.py:1408
  288.9 12.1 %collective-permute-start.32 = (bf16[1,128,768]{2,1,0:T(8,128)(2,1)S(1)}, bf16[1,128,768]{2,1,0:T(8,128)(2,1)S(1)}, u32[]{:S(2)}, u32[]{:S(2)}) collective-permute-start(bf16[1,128,768]{2,1,0:T(8,128)(2,1)S(1)} %dynamic-slice_convert_fusion.2), channel_id=1, source_target_pairs={{0,16},{4,20},{8,24},{12,28},{16,0},{20,4},{24,8},{28,12},{1,17},{... | collective-permute-start | bytes 589832 | tf_op jit(solution)/shard_map/ppermute | solution.py:518
  (37 other events, 279.2 us)
Sparse Core Ops, SparseCore 0:
  61.5 93.2 all-gather.1
  177.6 102.6 reduce-scatter.1

commit v3 on v2

--- a/solution.py
+++ b/solution.py
@@ -393,7 +393,7 @@
             queries = rows[low:high, lane : lane + HD]
             keys = rows[0:high, width + lane : width + lane + HD]
             values = rows[0:high, 2 * width + lane : 2 * width + lane + HD]
-            scores = jnp.where(allowed, mm(keys, queries, NT) * HD ** (-0.5), -1e30)
+            scores = jnp.where(allowed, mm(keys, queries * jnp.bfloat16(HD ** (-0.5)), NT), -1e30)
             top = jnp.max(scores, axis=0, keepdims=True)
             exponent = jnp.exp(scores - top)
             total = jnp.sum(exponent, axis=0, keepdims=True)
@@ -425,7 +425,7 @@
             keys = rows[0:high, width + lane : width + lane + HD]
             values = rows[0:high, 2 * width + lane : 2 * width + lane + HD]
             grad_out = grads[low:high, lane : lane + HD]
-            scores = jnp.where(allowed, mm(keys, queries, NT) * scale, -1e30)
+            scores = jnp.where(allowed, mm(keys, queries * jnp.bfloat16(scale), NT), -1e30)
             probs = jnp.exp(scores - log_ref[head : head + 1, low:high])
             grad_probs = mm(values, grad_out, NT)
             delta = jnp.sum(probs * grad_probs, axis=0, keepdims=True)

time: 312 us -> 312 us (level)
  no operation moved by 1% of the time
where the time goes in v3:
time: 312 us; the launch traced here: 311 us
  waiting for transfers between devices  124 us (40%)
  Pallas kernels  65.2 us (21%)
  starting transfers between devices  57.6 us (18%)
  blocking collectives  21.1 us (7%)
  between operations  14.7 us (5%)
  other arithmetic  13.1 us (4%)
  local copies, waits for them, and re-layouts  12.4 us (4%)
    ppermute x33, waiting for transfers between devices, swap(): return lax.ppermute(values, axis, [(i, i ^ bit) for i in range(count)])  80.9 us
    all_to_all x3, waiting for transfers between devices, exchange(): return lax.all_to_all(pieces, 'ctx', 0, 0, tiled=True)  42.9 us
    ppermute x33, starting transfers between devices, swap(): return lax.ppermute(values, axis, [(i, i ^ bit) for i in range(count)])  42.1 us
    all_to_all x1, blocking collectives, exchange(): return lax.all_to_all(pieces, 'ctx', 0, 0, tiled=True)  21.1 us
    all_to_all x3, starting transfers between devices, exchange(): return lax.all_to_all(pieces, 'ctx', 0, 0, tiled=True)  12.1 us
    pallas_call x1, Pallas kernels, feed_part(): pl.pallas_call(lambda *refs: feed_kernel(len(cot_parts), *refs), grid=(1,...  9.31 us
    unnamed x68, local copies, waits for them, and re-layouts  7.66 us
    pallas_call x1, Pallas kernels, attend_backward(): pl.pallas_call(lambda *refs: backward_kernel(block_rows, *refs), out_shap...  6.95 us
  transfers between devices with their start and end apart: 39, of which 18 were waited for; matrix products, arithmetic and copies ran while one was open for 7% of the time, Pallas kernels for 18%

profile of v3, /device:TPU:0, one launch (start us, length us, event | category | flops | bytes accessed | tf_op | source)
XLA Modules:
  0.0 310.9 jit_solution(8992676069414890204)
XLA Ops:
  13.5 2.8 collective-permute-start
  17.8 4.1 %collective-permute-done.1 = bf16[1,64,1024]{2,1,0:T(8,128)(2,1)S(1)} collective-permute-done((bf16[1,64,1024]{2,1,0:T(8,128)(2,1)}, bf16[1,64,1024]{2,1,0:T(8,128)(2,1)S(1)}, u32[]{:S(2)}, u32[]{:S(2)}) %collective-permute-start.1) | collective-permute-done | bytes 131104 | tf_op jit(solution)/shard_map/ppermute | solution.py:518
  21.9 2.8 collective-permute-done
  29.6 3.1 collective-permute-start.5
  34.6 8.0 %collective-permute-done.6 = bf16[2,64,1024]{2,1,0:T(8,128)(2,1)S(1)} collective-permute-done((bf16[2,64,1024]{2,1,0:T(8,128)(2,1)S(1)}, bf16[2,64,1024]{2,1,0:T(8,128)(2,1)S(1)}, u32[]{:S(2)}, u32[]{:S(2)}) %collective-permute-start.6) | collective-permute-done | bytes 262176 | tf_op jit(solution)/shard_map/ppermute | solution.py:518
  48.9 11.0 %collective-permute-done.11.refs_8_ = bf16[4,64,1024]{2,1,0:T(8,128)(2,1)S(1)} collective-permute-done((bf16[4,64,1024]{2,1,0:T(8,128)(2,1)S(1)}, bf16[4,64,1024]{2,1,0:T(8,128)(2,1)S(1)}, u32[]{:S(2)}, u32[]{:S(2)}) %collective-permute-start.11) | collective-permute-done | bytes 524320 | tf_op jit(solution)/shard_map/ppermute | solution.py:518
  62.2 5.2 %first_part.1 = (bf16[512,1024]{1,0:T(8,128)(2,1)}, bf16[512,1024]{1,0:T(8,128)(2,1)}, bf16[1024,768]{1,0:T(8,128)(2,1)}, bf16[256,1024]{1,0:T(8,128)(2,1)}, f32...) custom-call(s32[2]{0:T(128)} %pad_add_fusion.1.refs_0_.own_ref, bf16[8,16,1024]{2,1,0:T(8,128)(2,1)} %bitcast.106, ...), custom_call_target="tpu_custom_call" | custom-call | flops 805306368 | bytes 8388608 | tf_op jit(solution)/shard_map/first_part/pallas_call | solution.py:689
  67.4 4.9 %all-to-all-start = ((bf16[8,128,384]{2,1,0:T(8,128)(2,1)}), bf16[8,128,384]{2,1,0:T(8,128)(2,1)S(1)}, u32[]{:S(2)}, u32[]{:S(2)}) async-start(bf16[8,128,384]{2,1,0:T(8,128)(2,1)} %get-tuple-element.112), calls=%async_computation | async-start | bytes 1572864 | tf_op jit(solution)/shard_map/all_to_all | solution.py:1246
  73.8 33.7 %all-to-all-done = bf16[8,128,384]{2,1,0:T(8,128)(2,1)S(1)} async-done(((bf16[8,128,384]{2,1,0:T(8,128)(2,1)}), bf16[8,128,384]{2,1,0:T(8,128)(2,1)S(1)}, u32[]{:S(2)}, u32[]{:S(2)}) %all-to-all-start) | async-done | bytes 786464 | tf_op jit(solution)/shard_map/all_to_all | solution.py:1246
  108.4 6.5 %attend_forward.1 = (bf16[1024,128]{1,0:T(8,128)(2,1)}, f32[8,1024]{1,0:T(8,128)}) custom-call(s32[16]{0:T(128)} %select_reduce_fusion.refs_0_, bf16[1024,384]{1,0:T(8,128)(2,1)} %bitcast.113), custom_call_target="tpu_custom_call" | custom-call | flops 402653184 | bytes 1048576 | tf_op jit(solution)/shard_map/attend_forward/pallas_call | solution.py:474
  114.9 21.1 %all_to_all.25.attended_ref.right_ref = bf16[8,128,128]{2,1,0:T(8,128)(2,1)} all-to-all(bf16[8,128,128]{2,1,0:T(8,128)(2,1)} %bitcast.118), channel_id=1, replica_groups=mesh['ctx'=8,'tp'=4] {'ctx'}, dimensions={0} | all-to-all | bytes 524288 | tf_op jit(solution)/shard_map/all_to_all | solution.py:1246
  136.0 2.5 branch_part.1
  143.4 12.5 %collective-permute-done.13 = bf16[256,1024]{1,0:T(8,128)(2,1)S(1)} collective-permute-done((bf16[256,1024]{1,0:T(8,128)(2,1)S(1)}, bf16[256,1024]{1,0:T(8,128)(2,1)S(1)}, u32[]{:S(2)}, u32[]{:S(2)}) %collective-permute-start.13) | collective-permute-done | bytes 524320 | tf_op jit(solution)/shard_map/ppermute | solution.py:518
  157.5 3.4 %collective-permute-start.17 = (bf16[1,64,1024]{2,1,0:T(8,128)(2,1)S(1)}, bf16[1,64,1024]{2,1,0:T(8,128)(2,1)S(1)}, u32[]{:S(2)}, u32[]{:S(2)}) collective-permute-start(bf16[1,64,1024]{2,1,0:T(8,128)(2,1)S(1)} %get-tuple-element.232), channel_id=1, source_target_pairs={{0,8},{4,12},{8,0},{12,4},{16,24},{20,28},{24,16},{28,20},{1,9},{5... | collective-permute-start | bytes 393224 | tf_op jit(solution)/shard_map/ppermute | solution.py:518
  161.6 9.3 %feed_part.1 = (f32[512,1024]{1,0:T(8,128)}, bf16[512,1024]{1,0:T(8,128)(2,1)}, bf16[512,1024]{1,0:T(8,128)(2,1)}, bf16[512,1024]{1,0:T(8,128)(2,1)}, bf16[256,1...) custom-call(s32[2]{0:T(128)} %pad_add_fusion.1.refs_0_.own_ref, ...), custom_call_target="tpu_custom_call" | custom-call | flops 3221225472 | bytes 16777216 | tf_op jit(solution)/shard_map/feed_part/pallas_call | solution.py:1195
  171.0 6.4 %feed_grads.1 = bf16[1024,2048]{1,0:T(8,128)(2,1)} custom-call(bf16[512,1024]{1,0:T(8,128)(2,1)} %get-tuple-element.172.second_ref, bf16[512,1024]{1,0:T(8,128)(2,1)} %get-tuple-element.173.grad_pre_ref, bf16[512,1024]{1,0:T(8,128)(2,1)} %get-tuple-element.135.cot_ref, bf16[512,1024]{1,0:T(8,128)(2,1)} %get-tuple-element.151.activated_ref), custom_call_target="tpu_custom_call" | custom-call | flops 2147483648 | bytes 8388608 | tf_op jit(solution)/shard_map/feed_grads/pallas_call | solution.py:721
  182.1 16.4 %collective-permute-done.20 = bf16[4,64,1024]{2,1,0:T(8,128)(2,1)S(1)} collective-permute-done((bf16[4,64,1024]{2,1,0:T(8,128)(2,1)S(1)}, bf16[4,64,1024]{2,1,0:T(8,128)(2,1)S(1)}, u32[]{:S(2)}, u32[]{:S(2)}) %collective-permute-start.20) | collective-permute-done | bytes 524320 | tf_op jit(solution)/shard_map/ppermute | solution.py:518
  199.4 2.6 collective-permute-done.21.other_ref
  202.8 5.6 %hidden_grad_part.1 = (bf16[8,128,128]{2,1,0:T(8,128)(2,1)}, bf16[512,1024]{1,0:T(8,128)(2,1)}, f32[8,16,1024]{2,1,0:T(8,128)}, f32[8,1024]{1,0:T(8,128)}) custom-call(s32[2]{0:T(128)} %pad_add_fusion.1.refs_0_.own_ref, bf16[256,1024]{1,0:T(8,128)(2,1)} %copy-done.2, bf16[256,1024]{1,0:T(8,128)(2,1)} %copy-done.11, ...), custom_call_target="tpu_custom_call" | custom-call | tf_op jit(solution)/shard_map/hidden_grad_part/pallas_call | solution.py:931
  208.4 3.6 %all-to-all-start.2 = ((bf16[8,128,128]{2,1,0:T(8,128)(2,1)}), bf16[8,128,128]{2,1,0:T(8,128)(2,1)S(1)}, u32[]{:S(2)}, u32[]{:S(2)}) async-start(bf16[8,128,128]{2,1,0:T(8,128)(2,1)} %get-tuple-element.139), calls=%async_computation.2 | async-start | bytes 524288 | tf_op jit(solution)/shard_map/all_to_all | solution.py:1246
  212.1 2.9 fusion.2
  215.0 2.6 halved_grads.1
  219.3 9.2 %all-to-all-done.2 = bf16[8,128,128]{2,1,0:T(8,128)(2,1)S(1)} async-done(((bf16[8,128,128]{2,1,0:T(8,128)(2,1)}), bf16[8,128,128]{2,1,0:T(8,128)(2,1)S(1)}, u32[]{:S(2)}, u32[]{:S(2)}) %all-to-all-start.2) | async-done | bytes 262176 | tf_op jit(solution)/shard_map/all_to_all | solution.py:1246
  229.2 7.0 %attend_backward.1.refs_1_ = bf16[1024,384]{1,0:T(8,128)(2,1)} custom-call(s32[16]{0:T(128)} %select_reduce_fusion.refs_0_, bf16[1024,384]{1,0:T(8,128)(2,1)} %bitcast.114, bf16[1024,128]{1,0:T(8,128)(2,1)} %bitcast.117, f32[8,1024]{1,0:T(8,128)} %get-tuple-element.140.refs_3_), custom_call_target="tpu_custom_call" | custom-call | flops 939524096 | bytes 1835008 | tf_op jit(solution)/shard_map/attend_backward/pallas_call | solution.py:496
  236.2 3.6 %all-to-all-start.3 = ((bf16[8,128,384]{2,1,0:T(8,128)(2,1)}), bf16[8,128,384]{2,1,0:T(8,128)(2,1)S(1)}, u32[]{:S(2)}, u32[]{:S(2)}) async-start(bf16[8,128,384]{2,1,0:T(8,128)(2,1)} %bitcast.115), calls=%async_computation.3 | async-start | bytes 1572864 | tf_op jit(solution)/shard_map/all_to_all | solution.py:1246
  243.7 4.0 %mix_grads.1 = (bf16[4,128,384]{2,1,0:T(8,128)(2,1)}, bf16[4,128,384]{2,1,0:T(8,128)(2,1)}) custom-call(s32[2]{0:T(128)} %pad_add_fusion.1.refs_0_.own_ref, bf16[1024,384]{1,0:T(8,128)(2,1)} %attend_backward.1.refs_1_, bf16[8,64,1024]{2,1,0:T(8,128)(2,1)} %copy-done.24, bf16[8,64,1024]{2,1,0:T(8,128)(2,1)} %collective-permute-done.22.refs_3_), custom_call_target="tpu_custom_call" | custom-call | flops 805306368 | bytes 8388608 | tf_op jit(solution)/shard_map/mix_grads/pallas_call | solution.py:1014
  253.2 3.3 %collective-permute-done.25 = bf16[2,128,256]{2,1,0:T(8,128)(2,1)S(1)} collective-permute-done((bf16[2,128,256]{2,1,0:T(8,128)(2,1)S(1)}, bf16[2,128,256]{2,1,0:T(8,128)(2,1)S(1)}, u32[]{:S(2)}, u32[]{:S(2)}) %collective-permute-start.25) | collective-permute-done | bytes 131104 | tf_op jit(solution)/shard_map/ppermute | solution.py:518
  257.2 4.7 %collective-permute-done.24.came_ref = bf16[4,128,384]{2,1,0:T(8,128)(2,1)S(1)} collective-permute-done((bf16[4,128,384]{2,1,0:T(8,128)(2,1)}, bf16[4,128,384]{2,1,0:T(8,128)(2,1)S(1)}, u32[]{:S(2)}, u32[]{:S(2)}) %collective-permute-start.24) | collective-permute-done | bytes 393248 | tf_op jit(solution)/shard_map/ppermute | solution.py:518
  264.8 4.5 %first_grads.1 = (bf16[8,2,16,1024]{3,2,1,0:T(8,128)(2,1)}, bf16[8,2,16,1024]{3,2,1,0:T(8,128)(2,1)}, f32[8,1024]{1,0:T(8,128)}) custom-call(s32[2]{0:T(128)} %pad_add_fusion.1.refs_0_.own_ref, bf16[8,128,384]{2,1,0:T(8,128)(2,1)} %copy-done.1, bf16[1024,768]{1,0:T(8,128)(2,1)} %get-tuple-element.160.weight_ref, ...), custom_call_target="tpu_custom_call" | custom-call | tf_op jit(solution)/shard_map/first_grads/pallas_call | solution.py:1101
  271.2 5.2 %collective-permute-start.28 = (bf16[2,128,768]{2,1,0:T(8,128)(2,1)}, bf16[2,128,768]{2,1,0:T(8,128)(2,1)S(1)}, u32[]{:S(2)}, u32[]{:S(2)}) collective-permute-start(bf16[2,128,768]{2,1,0:T(8,128)(2,1)} %get-tuple-element.158), channel_id=1, source_target_pairs={{0,8},{4,12},{8,0},{12,4},{16,24},{20,28},{24,16},{28,20},{1,9},{5... | collective-permute-start | bytes 1179656 | tf_op jit(solution)/shard_map/ppermute | solution.py:518
  281.1 3.4 %all-to-all-start.4 = ((f32[32,8,128]{2,1,0:T(8,128)}), f32[32,8,128]{2,1,0:T(8,128)S(1)}, u32[]{:S(2)}, u32[]{:S(2)}) async-start(f32[32,8,128]{2,1,0:T(8,128)} %small_pack.1), calls=%async_computation.4 | async-start | bytes 262144 | tf_op jit(solution)/shard_map/all_to_all | solution.py:1408
  295.4 5.5 %collective-permute-done.32 = bf16[1,128,768]{2,1,0:T(8,128)(2,1)S(1)} collective-permute-done((bf16[1,128,768]{2,1,0:T(8,128)(2,1)S(1)}, bf16[1,128,768]{2,1,0:T(8,128)(2,1)S(1)}, u32[]{:S(2)}, u32[]{:S(2)}) %collective-permute-start.32) | collective-permute-done | bytes 196640 | tf_op jit(solution)/shard_map/ppermute | solution.py:518
  (179 shorter events, 74.9 us)
Async XLA Ops:
  7.2 153.7 %all-gather.2.cloned.1.call-start = ((), (), s32[]{:S(2)}) async-start(), calls=%async_computation.6 | async-start | bytes 4718592 | tf_op jit(solution)/shard_map/all_gather | solution.py:1328
  7.2 17.4 %collective-permute-start.4 = (bf16[8,16,1024]{2,1,0:T(8,128)(2,1)}, bf16[8,16,1024]{2,1,0:T(8,128)(2,1)S(1)}, u32[]{:S(2)}, u32[]{:S(2)}) collective-permute-start(bf16[8,16,1024]{2,1,0:T(8,128)(2,1)} %bitcast.103), channel_id=1, source_target_pairs={{0,3},{1,2},{2,1},{3,0},{4,7},{5,6},{6,5},{7,4},{8,11},{9,10},{10,... | collective-permute-start | bytes 786440 | tf_op jit(solution)/shard_map/ppermute | solution.py:518
  9.7 15.0 %collective-permute-start.3 = (bf16[8,16,1024]{2,1,0:T(8,128)(2,1)}, bf16[8,16,1024]{2,1,0:T(8,128)(2,1)S(1)}, u32[]{:S(2)}, u32[]{:S(2)}) collective-permute-start(bf16[8,16,1024]{2,1,0:T(8,128)(2,1)} %bitcast.104), channel_id=1, source_target_pairs={{0,2},{1,3},{2,0},{3,1},{4,6},{5,7},{6,4},{7,5},{8,10},{9,11},{10,... | collective-permute-start | bytes 786440 | tf_op jit(solution)/shard_map/ppermute | solution.py:518
  10.3 14.3 %collective-permute-start.2 = (bf16[8,16,1024]{2,1,0:T(8,128)(2,1)}, bf16[8,16,1024]{2,1,0:T(8,128)(2,1)S(1)}, u32[]{:S(2)}, u32[]{:S(2)}) collective-permute-start(bf16[8,16,1024]{2,1,0:T(8,128)(2,1)} %bitcast.105), channel_id=1, source_target_pairs={{0,1},{1,0},{2,3},{3,2},{4,5},{5,4},{6,7},{7,6},{8,9},{9,8},{10,11... | collective-permute-start | bytes 786440 | tf_op jit(solution)/shard_map/ppermute | solution.py:518
  13.5 11.2 %collective-permute-start = (bf16[1,80,1024]{2,1,0:T(8,128)(2,1)}, bf16[1,80,1024]{2,1,0:T(8,128)(2,1)S(1)}, u32[]{:S(2)}, u32[]{:S(2)}) collective-permute-start(bf16[1,80,1024]{2,1,0:T(8,128)(2,1)} %get-tuple-element.99), channel_id=1, source_target_pairs={{0,16},{4,20},{8,24},{12,28},{16,0},{20,4},{24,8},{28,12},{1,17},{... | collective-permute-start | bytes 491528 | tf_op jit(solution)/shard_map/ppermute | solution.py:518
  24.7 17.9 %collective-permute-start.9 = (bf16[8,16,1024]{2,1,0:T(8,128)(2,1)}, bf16[8,16,1024]{2,1,0:T(8,128)(2,1)S(1)}, u32[]{:S(2)}, u32[]{:S(2)}) collective-permute-start(bf16[8,16,1024]{2,1,0:T(8,128)(2,1)} %bitcast.138), channel_id=1, source_target_pairs={{0,3},{1,2},{2,1},{3,0},{4,7},{5,6},{6,5},{7,4},{8,11},{9,10},{10,... | collective-permute-start | bytes 786440 | tf_op jit(solution)/shard_map/ppermute | solution.py:518
  25.0 17.5 %collective-permute-start.8 = (bf16[8,16,1024]{2,1,0:T(8,128)(2,1)}, bf16[8,16,1024]{2,1,0:T(8,128)(2,1)S(1)}, u32[]{:S(2)}, u32[]{:S(2)}) collective-permute-start(bf16[8,16,1024]{2,1,0:T(8,128)(2,1)} %bitcast.139), channel_id=1, source_target_pairs={{0,2},{1,3},{2,0},{3,1},{4,6},{5,7},{6,4},{7,5},{8,10},{9,11},{10,... | collective-permute-start | bytes 786440 | tf_op jit(solution)/shard_map/ppermute | solution.py:518
  26.2 16.4 %collective-permute-start.7 = (bf16[8,16,1024]{2,1,0:T(8,128)(2,1)}, bf16[8,16,1024]{2,1,0:T(8,128)(2,1)S(1)}, u32[]{:S(2)}, u32[]{:S(2)}) collective-permute-start(bf16[8,16,1024]{2,1,0:T(8,128)(2,1)} %bitcast.140), channel_id=1, source_target_pairs={{0,1},{1,0},{2,3},{3,2},{4,5},{5,4},{6,7},{7,6},{8,9},{9,8},{10,11... | collective-permute-start | bytes 786440 | tf_op jit(solution)/shard_map/ppermute | solution.py:518
  27.6 15.0 %collective-permute-start.6 = (bf16[2,64,1024]{2,1,0:T(8,128)(2,1)S(1)}, bf16[2,64,1024]{2,1,0:T(8,128)(2,1)S(1)}, u32[]{:S(2)}, u32[]{:S(2)}) collective-permute-start(bf16[2,64,1024]{2,1,0:T(8,128)(2,1)S(1)} %pad_maximum_fusion.2), channel_id=1, source_target_pairs={{0,16},{4,20},{8,24},{12,28},{16,0},{20,4},{24,8},{28,12},{1,17},{... | collective-permute-start | bytes 786440 | tf_op jit(solution)/shard_map/ppermute | solution.py:518
  29.6 15.4 %collective-permute-start.5 = (bf16[2,80,1024]{2,1,0:T(8,128)(2,1)S(1)}, bf16[2,80,1024]{2,1,0:T(8,128)(2,1)S(1)}, u32[]{:S(2)}, u32[]{:S(2)}) collective-permute-start(bf16[2,80,1024]{2,1,0:T(8,128)(2,1)S(1)} %pad_maximum_fusion.1), channel_id=1, source_target_pairs={{0,8},{4,12},{8,0},{12,4},{16,24},{20,28},{24,16},{28,20},{1,9},{5... | collective-permute-start | bytes 983048 | tf_op jit(solution)/shard_map/ppermute | solution.py:518
  45.1 16.2 %collective-permute-start.10 = (bf16[4,80,1024]{2,1,0:T(8,128)(2,1)S(1)}, bf16[4,80,1024]{2,1,0:T(8,128)(2,1)S(1)}, u32[]{:S(2)}, u32[]{:S(2)}) collective-permute-start(bf16[4,80,1024]{2,1,0:T(8,128)(2,1)S(1)} %constant_dynamic-update-slice_fusion.refs_5_), channel_id=1, source_target_pairs={{0,4},{4,0},{8,12},{12,8},{16,20},{20,16},{24,28},{28,24},{1,5},{5... | collective-permute-start | bytes 1966088 | tf_op jit(solution)/shard_map/ppermute | solution.py:518
  46.7 13.1 %collective-permute-start.11 = (bf16[4,64,1024]{2,1,0:T(8,128)(2,1)S(1)}, bf16[4,64,1024]{2,1,0:T(8,128)(2,1)S(1)}, u32[]{:S(2)}, u32[]{:S(2)}) collective-permute-start(bf16[4,64,1024]{2,1,0:T(8,128)(2,1)S(1)} %constant_dynamic-update-slice_fusion.3.refs_7_), channel_id=1, source_target_pairs={{0,8},{4,12},{8,0},{12,4},{16,24},{20,28},{24,16},{28,20},{1,9},{5... | collective-permute-start | bytes 1572872 | tf_op jit(solution)/shard_map/ppermute | solution.py:518
  67.4 40.2 %all-to-all-start = ((bf16[8,128,384]{2,1,0:T(8,128)(2,1)}), bf16[8,128,384]{2,1,0:T(8,128)(2,1)S(1)}, u32[]{:S(2)}, u32[]{:S(2)}) async-start(bf16[8,128,384]{2,1,0:T(8,128)(2,1)} %get-tuple-element.112), calls=%async_computation | async-start | bytes 1572864 | tf_op jit(solution)/shard_map/all_to_all | solution.py:1246
  72.3 221.0 %reduce-scatter.2.cloned.1.call-start = ((), (), s32[]{:S(2)}) async-start(), calls=%async_computation.7 | async-start | bytes 4718592 | tf_op jit(solution)/shard_map/reduce_scatter | solution.py:1360
  141.9 14.0 %collective-permute-start.13 = (bf16[256,1024]{1,0:T(8,128)(2,1)S(1)}, bf16[256,1024]{1,0:T(8,128)(2,1)S(1)}, u32[]{:S(2)}, u32[]{:S(2)}) collective-permute-start(bf16[256,1024]{1,0:T(8,128)(2,1)S(1)} %add_convert_fusion.3), channel_id=1, source_target_pairs={{0,2},{1,3},{2,0},{3,1},{4,6},{5,7},{6,4},{7,5},{8,10},{9,11},{10,... | collective-permute-start | bytes 1572872 | tf_op jit(solution)/shard_map/ppermute | solution.py:518
  156.4 14.6 %collective-permute-start.19 = (bf16[1,64,1024]{2,1,0:T(8,128)(2,1)S(1)}, bf16[1,64,1024]{2,1,0:T(8,128)(2,1)S(1)}, u32[]{:S(2)}, u32[]{:S(2)}) collective-permute-start(bf16[1,64,1024]{2,1,0:T(8,128)(2,1)S(1)} %get-tuple-element.230), channel_id=1, source_target_pairs={{0,24},{4,28},{8,16},{12,20},{16,8},{20,12},{24,0},{28,4},{1,25},{... | collective-permute-start | bytes 393224 | tf_op jit(solution)/shard_map/ppermute | solution.py:518
  157.5 13.5 %collective-permute-start.18 = (bf16[1,64,1024]{2,1,0:T(8,128)(2,1)S(1)}, bf16[1,64,1024]{2,1,0:T(8,128)(2,1)S(1)}, u32[]{:S(2)}, u32[]{:S(2)}) collective-permute-start(bf16[1,64,1024]{2,1,0:T(8,128)(2,1)S(1)} %get-tuple-element.231), channel_id=1, source_target_pairs={{0,16},{4,20},{8,24},{12,28},{16,0},{20,4},{24,8},{28,12},{1,17},{... | collective-permute-start | bytes 393224 | tf_op jit(solution)/shard_map/ppermute | solution.py:518
  157.5 13.5 %collective-permute-start.17 = (bf16[1,64,1024]{2,1,0:T(8,128)(2,1)S(1)}, bf16[1,64,1024]{2,1,0:T(8,128)(2,1)S(1)}, u32[]{:S(2)}, u32[]{:S(2)}) collective-permute-start(bf16[1,64,1024]{2,1,0:T(8,128)(2,1)S(1)} %get-tuple-element.232), channel_id=1, source_target_pairs={{0,8},{4,12},{8,0},{12,4},{16,24},{20,28},{24,16},{28,20},{1,9},{5... | collective-permute-start | bytes 393224 | tf_op jit(solution)/shard_map/ppermute | solution.py:518
  178.5 20.0 %collective-permute-start.20 = (bf16[4,64,1024]{2,1,0:T(8,128)(2,1)S(1)}, bf16[4,64,1024]{2,1,0:T(8,128)(2,1)S(1)}, u32[]{:S(2)}, u32[]{:S(2)}) collective-permute-start(bf16[4,64,1024]{2,1,0:T(8,128)(2,1)S(1)} %pad_maximum_fusion), channel_id=1, source_target_pairs={{0,4},{4,0},{8,12},{12,8},{16,20},{20,16},{24,28},{28,24},{1,5},{5... | collective-permute-start | bytes 1572872 | tf_op jit(solution)/shard_map/ppermute | solution.py:518
  180.5 18.0 %collective-permute-start.16 = (bf16[256,1024]{1,0:T(8,128)(2,1)S(1)}, bf16[256,1024]{1,0:T(8,128)(2,1)S(1)}, u32[]{:S(2)}, u32[]{:S(2)}) collective-permute-start(bf16[256,1024]{1,0:T(8,128)(2,1)S(1)} %add_convert_fusion.1), channel_id=1, source_target_pairs={{0,2},{1,3},{2,0},{3,1},{4,6},{5,7},{6,4},{7,5},{8,10},{9,11},{10,... | collective-permute-start | bytes 1572872 | tf_op jit(solution)/shard_map/ppermute | solution.py:518
  198.5 9.8 %collective-permute-start.22 = (bf16[8,64,1024]{2,1,0:T(8,128)(2,1)S(1)}, bf16[8,64,1024]{2,1,0:T(8,128)(2,1)}, u32[]{:S(2)}, u32[]{:S(2)}) collective-permute-start(bf16[8,64,1024]{2,1,0:T(8,128)(2,1)S(1)} %constant_dynamic-update-slice_fusion.6.refs_2_), channel_id=1, source_target_pairs={{0,1},{1,0},{2,3},{3,2},{4,5},{5,4},{6,7},{7,6},{8,9},{9,8},{10,11... | collective-permute-start | bytes 3145736 | tf_op jit(solution)/shard_map/ppermute | solution.py:518
  208.4 20.1 %all-to-all-start.2 = ((bf16[8,128,128]{2,1,0:T(8,128)(2,1)}), bf16[8,128,128]{2,1,0:T(8,128)(2,1)S(1)}, u32[]{:S(2)}, u32[]{:S(2)}) async-start(bf16[8,128,128]{2,1,0:T(8,128)(2,1)} %get-tuple-element.139), calls=%async_computation.2 | async-start | bytes 524288 | tf_op jit(solution)/shard_map/all_to_all | solution.py:1246
  217.5 18.7 %collective-permute-start.23 = (bf16[4,128,256]{2,1,0:T(8,128)(2,1)}, bf16[4,128,256]{2,1,0:T(8,128)(2,1)S(1)}, u32[]{:S(2)}, u32[]{:S(2)}) collective-permute-start(bf16[4,128,256]{2,1,0:T(8,128)(2,1)} %get-tuple-element.142), channel_id=1, source_target_pairs={{0,4},{4,0},{8,12},{12,8},{16,20},{20,16},{24,28},{28,24},{1,5},{5... | collective-permute-start | bytes 786440 | tf_op jit(solution)/shard_map/ppermute | solution.py:518
  219.2 21.5 %collective-permute-start.26 = (bf16[8,2,16,1024]{3,2,1,0:T(8,128)(2,1)S(1)}, bf16[8,2,16,1024]{3,2,1,0:T(8,128)(2,1)}, u32[]{:S(2)}, u32[]{:S(2)}) collective-permute-start(bf16[8,2,16,1024]{3,2,1,0:T(8,128)(2,1)S(1)} %dynamic-slice_bitcast_fusion), channel_id=1, source_target_pairs={{0,1},{1,0},{2,3},{3,2},{4,5},{5,4},{6,7},{7,6},{8,9},{9,8},{10,11... | collective-permute-start | bytes 1572872 | tf_op jit(solution)/shard_map/ppermute | solution.py:518
  236.2 25.8 %all-to-all-start.3 = ((bf16[8,128,384]{2,1,0:T(8,128)(2,1)}), bf16[8,128,384]{2,1,0:T(8,128)(2,1)S(1)}, u32[]{:S(2)}, u32[]{:S(2)}) async-start(bf16[8,128,384]{2,1,0:T(8,128)(2,1)} %bitcast.115), calls=%async_computation.3 | async-start | bytes 1572864 | tf_op jit(solution)/shard_map/all_to_all | solution.py:1246
  242.0 9.3 %collective-permute-start.27 = (bf16[8,16,1024]{2,1,0:T(8,128)(2,1)S(1)}, bf16[8,16,1024]{2,1,0:T(8,128)(2,1)}, u32[]{:S(2)}, u32[]{:S(2)}) collective-permute-start(bf16[8,16,1024]{2,1,0:T(8,128)(2,1)S(1)} %fusion.11), channel_id=1, source_target_pairs={{0,2},{1,3},{2,0},{3,1},{4,6},{5,7},{6,4},{7,5},{8,10},{9,11},{10,... | collective-permute-start | bytes 786440 | tf_op jit(solution)/shard_map/ppermute | solution.py:518
  247.7 14.2 %collective-permute-start.24 = (bf16[4,128,384]{2,1,0:T(8,128)(2,1)}, bf16[4,128,384]{2,1,0:T(8,128)(2,1)S(1)}, u32[]{:S(2)}, u32[]{:S(2)}) collective-permute-start(bf16[4,128,384]{2,1,0:T(8,128)(2,1)} %get-tuple-element.148), channel_id=1, source_target_pairs={{0,4},{4,0},{8,12},{12,8},{16,20},{20,16},{24,28},{28,24},{1,5},{5... | collective-permute-start | bytes 1179656 | tf_op jit(solution)/shard_map/ppermute | solution.py:518
  271.2 17.5 %collective-permute-start.28 = (bf16[2,128,768]{2,1,0:T(8,128)(2,1)}, bf16[2,128,768]{2,1,0:T(8,128)(2,1)S(1)}, u32[]{:S(2)}, u32[]{:S(2)}) collective-permute-start(bf16[2,128,768]{2,1,0:T(8,128)(2,1)} %get-tuple-element.158), channel_id=1, source_target_pairs={{0,8},{4,12},{8,0},{12,4},{16,24},{20,28},{24,16},{28,20},{1,9},{5... | collective-permute-start | bytes 1179656 | tf_op jit(solution)/shard_map/ppermute | solution.py:518
  277.7 11.0 %collective-permute-start.30 = (bf16[8,16,1024]{2,1,0:T(8,128)(2,1)S(1)}, bf16[8,16,1024]{2,1,0:T(8,128)(2,1)S(1)}, u32[]{:S(2)}, u32[]{:S(2)}) collective-permute-start(bf16[8,16,1024]{2,1,0:T(8,128)(2,1)S(1)} %fusion.12), channel_id=1, source_target_pairs={{0,2},{1,3},{2,0},{3,1},{4,6},{5,7},{6,4},{7,5},{8,10},{9,11},{10,... | collective-permute-start | bytes 786440 | tf_op jit(solution)/shard_map/ppermute | solution.py:518
  279.0 8.6 %collective-permute-start.31 = (bf16[1,128,256]{2,1,0:T(8,128)(2,1)}, bf16[1,128,256]{2,1,0:T(8,128)(2,1)}, u32[]{:S(2)}, u32[]{:S(2)}) collective-permute-start(bf16[1,128,256]{2,1,0:T(8,128)(2,1)} %dynamic-slice_convert_fusion.3), channel_id=1, source_target_pairs={{0,16},{4,20},{8,24},{12,28},{16,0},{20,4},{24,8},{28,12},{1,17},{... | collective-permute-start | bytes 196616 | tf_op jit(solution)/shard_map/ppermute | solution.py:518
  281.1 14.3 %all-to-all-start.4 = ((f32[32,8,128]{2,1,0:T(8,128)}), f32[32,8,128]{2,1,0:T(8,128)S(1)}, u32[]{:S(2)}, u32[]{:S(2)}) async-start(f32[32,8,128]{2,1,0:T(8,128)} %small_pack.1), calls=%async_computation.4 | async-start | bytes 262144 | tf_op jit(solution)/shard_map/all_to_all | solution.py:1408
  288.8 12.1 %collective-permute-start.32 = (bf16[1,128,768]{2,1,0:T(8,128)(2,1)S(1)}, bf16[1,128,768]{2,1,0:T(8,128)(2,1)S(1)}, u32[]{:S(2)}, u32[]{:S(2)}) collective-permute-start(bf16[1,128,768]{2,1,0:T(8,128)(2,1)S(1)} %dynamic-slice_convert_fusion.2), channel_id=1, source_target_pairs={{0,16},{4,20},{8,24},{12,28},{16,0},{20,4},{24,8},{28,12},{1,17},{... | collective-permute-start | bytes 589832 | tf_op jit(solution)/shard_map/ppermute | solution.py:518
  (37 other events, 280.2 us)
Sparse Core Ops, SparseCore 0:
  61.5 93.2 all-gather.1
  177.5 102.7 reduce-scatter.1
